TPU v7x, 32 devices: a whole 2x2x4 slice. The times are simulated.
32 devices in a mesh: feat: 2 (over core), seq: 4 (over z), rows: 4 (over y, x).
Axes of the slice: x: 2, y: 2, z: 4, core: 2. Of those that a mesh axis runs over, the one named last changes fastest.
Arguments:
- tokens: float32 [8, 2048, 2048], P(('feat', 'rows'), 'seq'), may hold values from -6 to 6
- lengths: int32 [8, 8], replicated, may hold values from 1 to 2041, as said below
- gain_one: float32 [2048], replicated, may hold values from 0.5 to 1.5
- w_query: bfloat16 [2048, 256], replicated, may hold values from -0.125 to 0.125
- w_key: bfloat16 [2048, 256], replicated, may hold values from -0.125 to 0.125
- w_value: bfloat16 [2048, 2048], replicated, may hold values from -0.125 to 0.125
- w_out: bfloat16 [2048, 2048], replicated, may hold values from -1 to 1
- gain_two: float32 [2048], replicated, may hold values from 0.5 to 1.5
- w_gate: bfloat16 [2048, 5632], replicated, may hold values from -0.125 to 0.125
- w_up: bfloat16 [2048, 5632], replicated, may hold values from -0.125 to 0.125
- w_down: bfloat16 [5632, 2048], replicated, may hold values from -0.078125 to 0.078125
- cotangent: float32 [8, 2048, 2048], P(('feat', 'rows'), 'seq'), may hold values from -6 to 6
Outputs:
- layer_out: float32 [8, 2048, 2048], P(('feat', 'rows'), 'seq')
- grad_tokens: float32 [8, 2048, 2048], P(('feat', 'rows'), 'seq')
- grad_gain_one: float32 [2048], P(('feat', 'seq', 'rows'))
- grad_query_w: float32 [2048, 256], P(('feat', 'seq', 'rows'))
- grad_key_w: float32 [2048, 256], P(('feat', 'seq', 'rows'))
- grad_value_w: float32 [2048, 2048], P(('feat', 'seq', 'rows'))
- grad_out_w: float32 [2048, 2048], P(('feat', 'seq', 'rows'))
- grad_gain_two: float32 [2048], P(('feat', 'seq', 'rows'))
- grad_gate_w: float32 [2048, 5632], P(('feat', 'seq', 'rows'))
- grad_up_w: float32 [2048, 5632], P(('feat', 'seq', 'rows'))
- grad_down_w: float32 [5632, 2048], P(('feat', 'seq', 'rows'))
Inputs may be any that keep to these rules, and one draw needn't show every extreme that they name: Each row of lengths gives, in order, the lengths of 8 documents that together fill one packed row of 2048 tokens. Some rows may hold a document that begins before token 128 and ends after token 1920.
All inputs are finite; a program needn't handle non-finite values.
Results may differ from a plain program's by a relative error of at most 0.0096.
Values may be sent and summed in bfloat16 or wider, within the bound.
No kernel may reach another device: no remote copies, remote signals or barrier semaphores. Data moves between devices by JAX's collectives and lax.ppermute only.
A program may use at most 512 MiB of HBM per device.

v0:
```python
import jax
import jax.numpy as jnp
from jax import lax
from jax.sharding import PartitionSpec as P

HEADS = 16
FDIM = 16
VHEAD = 128


eps_norm = 1e-06
highest = lax.Precision.HIGHEST


def carried_in(value, axis, combine, identity):
    length, here = (lax.axis_size(axis), lax.axis_index(axis))
    everything = jax.tree.map(lambda part: lax.all_gather(part, axis), value)
    start = jax.tree.map(
        lambda part, zero: jnp.broadcast_to(jnp.asarray(zero, part.dtype), part.shape),
        value,
        identity,
    )

    def lap(k, before):
        reached = k < here
        new = combine(before, jax.tree.map(lambda part: part[k], everything))
        return jax.tree.map(lambda a, b: jnp.where(reached, a, b), new, before)

    return lax.fori_loop(0, length, lap, start)


def prefix(value, axis, join, neutral):
    count = lax.axis_size(axis)
    place = lax.axis_index(axis)
    ahead = count - 1 - place
    gathered = jax.tree.map(
        lambda a, kind: lax.all_gather(a.astype(kind), axis),
        value,
        jax.tree.map(lambda a: jnp.bfloat16 if a.dtype == jnp.float32 else a.dtype, value),
    )
    state = jax.tree.map(lambda a, e: jnp.zeros_like(a) + jnp.asarray(e, a.dtype), value, neutral)

    def one(lap, state):
        source = count - 1 - lap
        return join(
            state,
            jax.tree.map(
                lambda a, own: lax.dynamic_index_in_dim(a, source, 0, False).astype(own.dtype),
                gathered,
                value,
            ),
        )

    return lax.fori_loop(0, ahead, one, state)


def normalize(values, gain):
    return values * lax.rsqrt(jnp.mean(values * values, axis=-1, keepdims=True) + eps_norm) * gain


def contract_rows(former, latter):
    return lax.dot_general(
        former, latter, (((0,), (0,)), ((), ())), preferred_element_type=jnp.float32
    )


def times_transpose(former, latter):
    return lax.dot_general(
        former, latter, (((1,), (1,)), ((), ())), preferred_element_type=jnp.float32
    )


def rounded(values):
    return lax.optimization_barrier(values.astype(jnp.bfloat16)).astype(jnp.float32)


def gate_product(gate_act, up_act):
    return jax.nn.silu(gate_act) * up_act


def taylor_group(packed, first_group, groups):
    batch_rows, length = (packed.shape[0], packed.shape[1])
    values = packed.reshape(batch_rows, length, HEADS, FDIM)
    span_size = FDIM // groups
    block_vals = lax.dynamic_slice_in_dim(values, first_group * span_size, span_size, 3)
    constant = jnp.where(first_group == 0, 1.0, 0.0).astype(jnp.float32)
    constant_col = jnp.ones((batch_rows, length, HEADS, 1), jnp.float32) * constant
    linear = block_vals * FDIM ** (-0.25)
    square = block_vals[..., :, None] * values[..., None, :] * (2.0 * FDIM) ** (-0.5)
    square = square.reshape(batch_rows, length, HEADS, span_size * FDIM)
    return jnp.concatenate([constant_col, linear, square], axis=-1)


def doc_index(starts, places):
    return jnp.sum((starts[:, :, None] <= places[None, None, :]).astype(jnp.int32), axis=1)


def attend(query_feats, key_feats, values, state_in, sums_in, allowed, from_before):
    scores = (
        jnp.einsum("rthg,rshg->rhts", query_feats, key_feats, precision=highest) * allowed[:, None]
    )
    numerator = jnp.einsum("rhts,rshe->rthe", scores, values, precision=highest)
    denominator = jnp.transpose(jnp.sum(scores, axis=-1), (0, 2, 1))
    carried = jnp.einsum("rthg,rhge->rthe", query_feats, state_in, precision=highest)
    numerator = numerator + from_before[:, :, None, None] * carried
    earlier_den = jnp.einsum("rthg,rhg->rth", query_feats, sums_in, precision=highest)
    denominator = denominator + from_before[:, :, None] * earlier_den
    return (numerator, denominator)


def summarize(key_feats, values, at_end):
    kept_keys = key_feats * at_end[:, :, None, None]
    return (
        jnp.einsum("rshg,rshe->rhge", kept_keys, values, precision=highest),
        jnp.sum(kept_keys, axis=1),
    )


def carry_on(earlier, following):
    kept_share = 1.0 - following[2]
    return (
        following[0] + kept_share[:, None, None, None] * earlier[0],
        following[1] + kept_share[:, None, None] * earlier[1],
        jnp.maximum(earlier[2], following[2]),
    )


def shards(
    tokens,
    lengths,
    gain_one,
    w_query,
    w_key,
    w_value,
    w_out,
    gain_two,
    w_gate,
    w_up,
    w_down,
    cotangent,
):
    rows_dev, stretch, width = tokens.shape
    token_count = rows_dev * stretch
    flat = tokens.reshape(token_count, width)
    normed_one, norm_back_one = jax.vjp(normalize, flat, gain_one)
    low_one = normed_one.astype(jnp.bfloat16)
    queries = (
        jnp.dot(low_one, w_query, preferred_element_type=jnp.float32)
        .astype(jnp.bfloat16)
        .reshape(rows_dev, stretch, -1)
    )
    keys_low = (
        jnp.dot(low_one, w_key, preferred_element_type=jnp.float32)
        .astype(jnp.bfloat16)
        .reshape(rows_dev, stretch, -1)
    )
    values_low = (
        jnp.dot(low_one, w_value, preferred_element_type=jnp.float32)
        .astype(jnp.bfloat16)
        .reshape(rows_dev, stretch, width)
    )
    nfeat = lax.axis_size("feat")
    findex = lax.axis_index("feat")
    sindex = lax.axis_index("seq")
    rindex = lax.axis_index("rows")
    ndocs = lengths.shape[1]
    grouped = lengths.reshape(nfeat, -1, rows_dev, ndocs)
    grouped = lax.dynamic_index_in_dim(grouped, rindex, 1, keepdims=False)
    query_all, keys_all, values_all = (
        lax.all_gather(queries, "feat", axis=0, tiled=True),
        lax.all_gather(keys_low, "feat", axis=0, tiled=True),
        lax.all_gather(values_low, "feat", axis=0, tiled=True),
    )
    doc_lengths = grouped.reshape(nfeat * rows_dev, ndocs)
    first_group, groups = (findex, nfeat)
    attn_rows = query_all.shape[0]
    starts = jnp.cumsum(doc_lengths, axis=1) - doc_lengths
    offset = sindex * stretch
    places = offset + jnp.arange(stretch, dtype=jnp.int32)
    doc_ids = doc_index(starts, places)
    before = doc_index(starts, jnp.reshape(offset - 1, (1,)))
    final = doc_index(starts, jnp.reshape(offset + stretch - 1, (1,)))
    causal = jnp.arange(stretch)[None, :] <= jnp.arange(stretch)[:, None]
    allowed = ((doc_ids[:, :, None] == doc_ids[:, None, :]) & causal[None]).astype(jnp.float32)
    from_before = (doc_ids == before).astype(jnp.float32)
    at_end = (doc_ids == final).astype(jnp.float32)
    resets = (final[:, 0] != before[:, 0]).astype(jnp.float32)

    def feature_map(packed):
        return taylor_group(packed, first_group, groups)

    query_raw, query_feat_back = jax.vjp(feature_map, query_all.astype(jnp.float32))
    key_raw, key_feat_back = jax.vjp(feature_map, keys_all.astype(jnp.float32))
    query_feats = rounded(query_raw)
    key_feats = rounded(key_raw)
    values_wide = values_all.astype(jnp.float32).reshape(attn_rows, stretch, HEADS, VHEAD)

    def summarize_here(key_part, value_part):
        return summarize(key_part, value_part, at_end)

    (stretch_state, key_sums), summarize_back = jax.vjp(summarize_here, key_feats, values_wide)
    empty_state = (jnp.zeros_like(stretch_state), jnp.zeros_like(key_sums), jnp.zeros_like(resets))
    state_in, sums_in, _ = carried_in(
        (stretch_state, key_sums, resets), "seq", carry_on, empty_state
    )

    def attend_here(query_part, key_part, value_part, state_part, sums_part):
        return attend(query_part, key_part, value_part, state_part, sums_part, allowed, from_before)

    (numerator, denominator), attend_back = jax.vjp(
        attend_here, query_feats, key_feats, values_wide, state_in, sums_in
    )
    numerator_all, denominator_all = lax.psum((numerator, denominator), "feat")
    numerator_own = lax.dynamic_slice_in_dim(numerator_all, findex * rows_dev, rows_dev, 0)
    denominator_own = lax.dynamic_slice_in_dim(denominator_all, findex * rows_dev, rows_dev, 0)
    mixed = numerator_own / denominator_own[..., None]
    mixed_low = mixed.reshape(token_count, width).astype(jnp.bfloat16)
    middle = flat + jnp.dot(mixed_low, w_out, preferred_element_type=jnp.float32)
    normed_two, norm_back_two = jax.vjp(normalize, middle, gain_two)
    low_two = normed_two.astype(jnp.bfloat16)
    gate_act = jnp.dot(low_two, w_gate, preferred_element_type=jnp.float32)
    up_act = jnp.dot(low_two, w_up, preferred_element_type=jnp.float32)
    hidden_wide, gate_back = jax.vjp(gate_product, gate_act, up_act)
    hidden = hidden_wide.astype(jnp.bfloat16)
    layer_out = middle + jnp.dot(hidden, w_down, preferred_element_type=jnp.float32)
    seed_wide = cotangent.reshape(token_count, width)
    grad_branch = seed_wide.astype(jnp.bfloat16)
    grad_hidden = times_transpose(grad_branch, w_down)
    grad_gate_wide, grad_up_wide = gate_back(grad_hidden)
    grad_gate = grad_gate_wide.astype(jnp.bfloat16)
    grad_up = grad_up_wide.astype(jnp.bfloat16)
    grad_low_two = times_transpose(grad_gate, w_gate) + times_transpose(grad_up, w_up)
    grad_middle_norm, grad_gain_two = norm_back_two(grad_low_two)
    grad_middle = seed_wide + grad_middle_norm
    grad_mixed_low = grad_middle.astype(jnp.bfloat16)
    grad_mixed = times_transpose(grad_mixed_low, w_out).reshape(rows_dev, stretch, HEADS, VHEAD)
    grad_numerator = grad_mixed / denominator_own[..., None]
    grad_denominator = -jnp.sum(grad_mixed * mixed, axis=-1) / denominator_own
    grad_numer_all, grad_denom_all = (
        lax.all_gather(grad_numerator, "feat", axis=0, tiled=True),
        lax.all_gather(grad_denominator, "feat", axis=0, tiled=True),
    )
    grad_query_feats, grad_key_feats, grad_values, grad_state_in, grad_sums_in = attend_back(
        (grad_numer_all, grad_denom_all)
    )
    grad_state, grad_sums, _ = prefix(
        (grad_state_in, grad_sums_in, resets), "seq", carry_on, empty_state
    )
    grad_key_more, grad_values_more = summarize_back((grad_state, grad_sums))
    grad_key_feats = grad_key_feats + grad_key_more
    grad_values = (grad_values + grad_values_more).reshape(attn_rows, stretch, width)
    grad_query_part = query_feat_back(grad_query_feats)[0]
    grad_key_part = key_feat_back(grad_key_feats)[0]
    grad_query_own, grad_key_own, grad_value_own = (
        lax.psum_scatter(grad_query_part, "feat", scatter_dimension=0, tiled=True),
        lax.psum_scatter(grad_key_part, "feat", scatter_dimension=0, tiled=True),
        lax.psum_scatter(grad_values, "feat", scatter_dimension=0, tiled=True),
    )
    grad_queries = grad_query_own.reshape(token_count, -1).astype(jnp.bfloat16)
    grad_keys = grad_key_own.reshape(token_count, -1).astype(jnp.bfloat16)
    grad_values_low = grad_value_own.reshape(token_count, width).astype(jnp.bfloat16)
    grad_low_one = (
        times_transpose(grad_queries, w_query)
        + times_transpose(grad_keys, w_key)
        + times_transpose(grad_values_low, w_value)
    )
    grad_tokens_norm, grad_gain_one = norm_back_one(grad_low_one)
    grad_tokens = (grad_middle + grad_tokens_norm).reshape(rows_dev, stretch, width)
    shares = (
        lax.psum_scatter(grad_gain_one, ("feat", "seq", "rows"), scatter_dimension=0, tiled=True),
        lax.psum_scatter(
            contract_rows(low_one, grad_queries),
            ("feat", "seq", "rows"),
            scatter_dimension=0,
            tiled=True,
        ),
        lax.psum_scatter(
            contract_rows(low_one, grad_keys),
            ("feat", "seq", "rows"),
            scatter_dimension=0,
            tiled=True,
        ),
        lax.psum_scatter(
            contract_rows(low_one, grad_values_low),
            ("feat", "seq", "rows"),
            scatter_dimension=0,
            tiled=True,
        ),
        lax.psum_scatter(
            contract_rows(mixed_low, grad_mixed_low),
            ("feat", "seq", "rows"),
            scatter_dimension=0,
            tiled=True,
        ),
        lax.psum_scatter(grad_gain_two, ("feat", "seq", "rows"), scatter_dimension=0, tiled=True),
        lax.psum_scatter(
            contract_rows(low_two, grad_gate),
            ("feat", "seq", "rows"),
            scatter_dimension=0,
            tiled=True,
        ),
        lax.psum_scatter(
            contract_rows(low_two, grad_up),
            ("feat", "seq", "rows"),
            scatter_dimension=0,
            tiled=True,
        ),
        lax.psum_scatter(
            contract_rows(hidden, grad_branch),
            ("feat", "seq", "rows"),
            scatter_dimension=0,
            tiled=True,
        ),
    )
    return (
        layer_out.reshape(rows_dev, stretch, width),
        grad_tokens,
        shares[0],
        shares[1],
        shares[2],
        shares[3],
        shares[4],
        shares[5],
        shares[6],
        shares[7],
        shares[8],
    )


def solution(mesh):
    in_specs = (
        P(("feat", "rows"), "seq", None),
        P(),
        P(),
        P(),
        P(),
        P(),
        P(),
        P(),
        P(),
        P(),
        P(),
        P(("feat", "rows"), "seq", None),
    )
    out_specs = (
        P(("feat", "rows"), "seq", None),
        P(("feat", "rows"), "seq", None),
        P(("feat", "seq", "rows")),
        P(("feat", "seq", "rows"), None),
        P(("feat", "seq", "rows"), None),
        P(("feat", "seq", "rows"), None),
        P(("feat", "seq", "rows"), None),
        P(("feat", "seq", "rows")),
        P(("feat", "seq", "rows"), None),
        P(("feat", "seq", "rows"), None),
        P(("feat", "seq", "rows"), None),
    )
    return jax.shard_map(shards, mesh=mesh, in_specs=in_specs, out_specs=out_specs, check_vma=False)
```

profile of v0, /device:TPU:0, one launch (start us, length us, event | category | flops | bytes accessed | tf_op | source)
XLA Modules:
  0.0 4681.7 jit_solution(9552037892783775874)
XLA Ops:
  11.9 9.8 convolution_convert_fusion
  43.1 11.1 pad_maximum_fusion.1
  54.5 3.7 copy.128
  58.3 5.4 fusion.26
  67.1 13.8 all-reduce
  81.0 3.9 fusion.25
  84.9 14.7 all-gather.5
  100.1 17.9 multiply_reduce_fusion
  118.0 23.0 fusion.12
  141.0 89.4 %all-gather.18.cloned.1.call-done = f32[8,16,137,128]{3,1,2,0:T(8,128)} async-done(((f32[2,16,137,128]{3,1,2,0:T(8,128)}), f32[8,16,137,128]{3,1,2,0:T(8,128)}) %all-gather.18.cloned.1.call-update) | async-done | bytes 8978448 | tf_op jit(solution)/shard_map/all_gather | solution.py:17
  230.4 21.3 while.33
  236.3 3.9 fusion.154
  242.1 3.9 fusion.154
  247.8 3.9 fusion.154
  251.8 4.4 fusion.78
  256.9 12.1 add_bitcast_fusion.1
  269.1 37.6 all-reduce.8.cloned.1.call-done
  310.6 7.9 multiply_reduce_fusion.9
  321.0 19.8 fusion.93
  340.9 19.0 fusion.94
  359.9 29.1 multiply_convert_fusion
  389.0 19.6 fusion.95
  408.6 20.6 multiply_reduce_fusion.5
  432.6 9.1 fusion.55
  441.7 3.6 multiply_reduce_fusion.7
  445.4 5.5 copy.98
  451.3 11.9 all-reduce.1
  468.6 5.5 fusion.76
  474.2 13.1 all-gather.7
  487.3 6.1 multiply_bitcast_fusion
  493.4 10.0 copy.99
  503.4 9.4 convolution_convert_fusion.1
  514.2 25.2 fusion.28
  539.4 22.8 fusion.9
  562.3 13.7 add_bitcast_fusion
  576.0 4.4 split.16
  580.4 6.5 multiply_reduce_fusion.4
  586.9 4.0 multiply_reduce_fusion.3
  592.9 27.6 fusion.8
  622.2 15.2 while.32
  623.7 3.7 convert_add_fusion.4
  628.9 3.4 convert_add_fusion.4
  637.5 11.5 bitcast_add_fusion.1
  649.0 4.4 split.18
  653.4 5.5 multiply_reduce_fusion.2
  658.9 4.2 multiply_reduce_fusion.1
  664.4 46.1 fusion.10
  710.5 14.1 fusion.38
  734.8 14.2 fusion.53
  749.1 10.7 fusion.44
  761.4 20.9 fusion.96
  782.3 21.0 fusion.97
  803.4 24.4 fusion.89
  827.8 20.2 add_bitcast_fusion.2
  850.3 7.5 fusion.46
  857.9 4.0 multiply_reduce_fusion.6
  861.9 37.9 all-reduce.4
  900.9 7.6 fusion.35
  908.5 119.3 %reduce-scatter.19.cloned.1.call-done = f32[64,256]{1,0:T(8,128)} async-done(((f32[2048,256]{1,0:T(8,128)}), f32[64,256]{1,0:T(8,128)}) %reduce-scatter.19.cloned.1.call-update) | async-done | bytes 65552 | tf_op jit(solution)/shard_map/reduce_scatter | solution.py:277
  1027.9 357.1 %reduce-scatter.23.cloned.1.call-done = f32[64,2048]{1,0:T(8,128)} async-done(((f32[2048,2048]{1,0:T(8,128)}), f32[64,2048]{1,0:T(8,128)}) %reduce-scatter.23.cloned.1.call-update) | async-done | bytes 524304 | tf_op jit(solution)/shard_map/reduce_scatter | solution.py:289
  1385.0 362.9 %reduce-scatter.21.cloned.1.call-done = f32[64,2048]{1,0:T(8,128)} async-done(((f32[2048,2048]{1,0:T(8,128)}), f32[64,2048]{1,0:T(8,128)}) %reduce-scatter.21.cloned.1.call-update) | async-done | bytes 524304 | tf_op jit(solution)/shard_map/reduce_scatter | solution.py:283
  1747.8 973.0 %reduce-scatter.25.cloned.1.call-done = f32[64,5632]{1,0:T(8,128)} async-done(((f32[2048,5632]{1,0:T(8,128)}), f32[64,5632]{1,0:T(8,128)}) %reduce-scatter.25.cloned.1.call-update) | async-done | bytes 1441808 | tf_op jit(solution)/shard_map/reduce_scatter | solution.py:296
  2720.9 977.0 %reduce-scatter.27.cloned.1.call-done = f32[64,5632]{1,0:T(8,128)} async-done(((f32[2048,5632]{1,0:T(8,128)}), f32[64,5632]{1,0:T(8,128)}) %reduce-scatter.27.cloned.1.call-update) | async-done | bytes 1441808 | tf_op jit(solution)/shard_map/reduce_scatter | solution.py:302
  3697.9 977.0 %reduce-scatter.29.cloned.1.call-done = f32[176,2048]{1,0:T(8,128)} async-done(((f32[5632,2048]{1,0:T(8,128)}), f32[176,2048]{1,0:T(8,128)}) %reduce-scatter.29.cloned.1.call-update) | async-done | bytes 1441808 | tf_op jit(solution)/shard_map/reduce_scatter | solution.py:308
  (249 shorter events, 85.1 us)
Async XLA Ops:
  7.2 15.5 copy-start
  7.2 47.3 %all-gather.16.cloned.1.call-start = ((), (), s32[]{:S(2)}) async-start(), calls=%async_computation.21 | async-start | bytes 6291456 | tf_op jit(solution)/shard_map/all_gather | solution.py:172
  11.9 10.8 copy-start.28
  21.7 208.7 %all-gather.18.cloned.1.call-start = ((), (), s32[]{:S(2)}) async-start(), calls=%async_computation.22 | async-start | bytes 11223040 | tf_op jit(solution)/shard_map/all_gather | solution.py:17
  26.7 9.4 copy-start.15
  36.2 5.4 copy-start.17
  37.5 4.1 copy-start.21
  54.3 12.8 copy-start.51
  54.3 12.8 copy-start.53
  54.4 26.6 copy-start.39
  54.4 202.4 %copy-start.37 = (f32[2,512]{1,0:T(2,128)}, f32[2,512]{1,0:T(2,128)S(1)}, u32[]{:S(2)}) copy-start(f32[2,512]{1,0:T(2,128)S(1)} %get-tuple-element.355) | copy-start | bytes 12292
  54.5 3.8 copy-start.3
  58.2 5.4 copy-start.10
  65.7 240.9 %all-reduce.8.cloned.1.call-start = ((), (), s32[]{:S(2)}) async-start(), calls=%async_computation.24 | async-start | bytes 16908288 | tf_op jit(solution)/shard_map/psum | solution.py:213
  100.1 17.9 copy-start.1
  251.8 17.2 copy-start.32
  251.8 5.1 copy-start.8
  269.0 218.3 %all-gather.14.cloned.1.call-start = ((), (), s32[]{:S(2)}) async-start(), calls=%async_computation.10 | async-start | bytes 12582912 | tf_op jit(solution)/shard_map/all_gather | solution.py:240
  306.6 4.0 copy-start.6
  310.6 8.0 copy-start.14
  310.6 10.0 copy-start.47
  321.0 19.8 copy-start.26
  408.6 20.6 copy-start.12
  408.6 20.6 copy-start.24
  429.2 12.5 slice-start.2
  432.6 9.1 copy-start.13
  432.6 9.1 slice-start.3
  432.6 9.1 copy-start.36
  445.3 5.6 copy-start.52
  445.3 5.6 copy-start.54
  445.3 17.9 copy-start.18
  450.9 14.1 copy-start.16
  450.9 15.8 copy-start.43
  450.9 17.7 copy-start.38
  450.9 169.8 %all-gather.20.cloned.1.call-start = ((), (), s32[]{:S(2)}) async-start(), calls=%async_computation.23 | async-start | bytes 5611520 | tf_op jit(solution)/shard_map/all_gather | solution.py:37
  514.2 25.3 copy-start.2
  514.2 213.7 %reduce-scatter.11.cloned.1.call-start = ((), (), s32[]{:S(2)}) async-start(), calls=%async_computation.11 | async-start | bytes 1572864 | tf_op jit(solution)/shard_map/reduce_scatter | solution.py:255
  539.4 22.8 copy-start.9
  539.4 22.8 copy-start.33
  576.0 4.4 copy-start.31
  580.4 6.6 copy-start.23
  580.4 12.6 slice-start
  586.9 6.0 slice-start.1
  620.6 110.7 %reduce-scatter.13.cloned.1.call-start = ((), (), s32[]{:S(2)}) async-start(), calls=%async_computation.12 | async-start | bytes 1572864 | tf_op jit(solution)/shard_map/reduce_scatter | solution.py:256
  622.2 15.3 copy-start.40
  649.0 4.4 copy-start.30
  653.4 5.5 copy-start.22
  664.4 84.7 %reduce-scatter.15.cloned.1.call-start = ((), (), s32[]{:S(2)}) async-start(), calls=%async_computation.13 | async-start | bytes 12582912 | tf_op jit(solution)/shard_map/reduce_scatter | solution.py:257
  664.4 46.1 copy-start.4
  724.6 183.9 %reduce-scatter.17.cloned.1.call-start = ((), (), s32[]{:S(2)}) async-start(), calls=%async_computation.14 | async-start | bytes 2162688 | tf_op jit(solution)/shard_map/reduce_scatter | solution.py:271
  731.3 296.6 %reduce-scatter.19.cloned.1.call-start = ((), (), s32[]{:S(2)}) async-start(), calls=%async_computation.15 | async-start | bytes 2162688 | tf_op jit(solution)/shard_map/reduce_scatter | solution.py:277
  734.7 650.2 %reduce-scatter.23.cloned.1.call-start = ((), (), s32[]{:S(2)}) async-start(), calls=%async_computation.17 | async-start | bytes 17301504 | tf_op jit(solution)/shard_map/reduce_scatter | solution.py:289
  749.0 998.8 %reduce-scatter.21.cloned.1.call-start = ((), (), s32[]{:S(2)}) async-start(), calls=%async_computation.16 | async-start | bytes 17301504 | tf_op jit(solution)/shard_map/reduce_scatter | solution.py:283
  759.8 1961.1 %reduce-scatter.25.cloned.1.call-start = ((), (), s32[]{:S(2)}) async-start(), calls=%async_computation.18 | async-start | bytes 47579136 | tf_op jit(solution)/shard_map/reduce_scatter | solution.py:296
  782.3 2915.6 %reduce-scatter.27.cloned.1.call-start = ((), (), s32[]{:S(2)}) async-start(), calls=%async_computation.19 | async-start | bytes 47579136 | tf_op jit(solution)/shard_map/reduce_scatter | solution.py:302
  803.3 3871.5 %reduce-scatter.29.cloned.1.call-start = ((), (), s32[]{:S(2)}) async-start(), calls=%async_computation.20 | async-start | bytes 47579136 | tf_op jit(solution)/shard_map/reduce_scatter | solution.py:308
  827.8 20.3 copy-start.29
  827.8 20.2 copy-start.34
  850.3 7.5 copy-start.7
  850.3 7.5 copy-start.25
  850.3 7.5 copy-start.42
  850.3 7.5 copy-start.46
  857.8 4.0 copy-start.50
  857.8 43.0 copy-start.49
  (12 other events, 21.2 us)
Sparse Core Ops, SparseCore 0:
  21.8 16.3 all-gather.15
  65.8 164.5 all-gather.17
  269.1 37.4 all-reduce.7
  451.0 21.0 all-gather.13
  514.3 83.7 all-gather.19
  620.7 6.7 reduce-scatter.10
  664.5 6.4 reduce-scatter.12
  724.7 14.6 reduce-scatter.14
  742.3 143.5 reduce-scatter.16
  888.6 139.2 reduce-scatter.18
  1030.8 354.0 reduce-scatter.22
  1387.8 359.9 reduce-scatter.20
  1750.8 970.0 reduce-scatter.24
  2723.7 974.1 reduce-scatter.26
  3700.7 974.1 reduce-scatter.28
where the time goes:
time: 4700 us; the launch traced here: 4680 us
  waiting for transfers between devices  3890 us (83%)
  matrix products  507 us (11%)
  other arithmetic  101 us (2%)
  blocking collectives  97.7 us (2%)
  local copies, waits for them, and re-layouts  65 us (1%)
    reduce_scatter x1, waiting for transfers between devices, shards(): lax.psum_scatter(contract_rows(low_two, grad_up), ('feat', 'seq', 'rows')...  977 us
    reduce_scatter x1, waiting for transfers between devices, shards(): lax.psum_scatter(contract_rows(hidden, grad_branch), ('feat', 'seq', 'row...  977 us
    reduce_scatter x1, waiting for transfers between devices, shards(): lax.psum_scatter(contract_rows(low_two, grad_gate), ('feat', 'seq', 'rows...  973 us
    reduce_scatter x1, waiting for transfers between devices, shards(): lax.psum_scatter(contract_rows(low_one, grad_values_low), ('feat', 'seq',...  363 us
    reduce_scatter x1, waiting for transfers between devices, shards(): lax.psum_scatter(contract_rows(mixed_low, grad_mixed_low), ('feat', 'seq'...  357 us
    reduce_scatter x1, waiting for transfers between devices, shards(): lax.psum_scatter(contract_rows(low_one, grad_keys), ('feat', 'seq', 'rows...  119 us
    dot_general x7, matrix products, contract_rows(): lax.dot_general(former, latter, (((0,), (0,)), ((), ())), preferred_eleme...  97.9 us
    dot_general x3, matrix products, attend(): numerator = jnp.einsum('rhts,rshe->rthe', scores, values, precision=highest)  94.3 us
  transfers between devices with their start and end apart: 15, of which 8 were waited for; matrix products, arithmetic and copies ran while one was open for 9% of the time, Pallas kernels for 0%

commit v1 on v0

v1 whole, which is shorter than its diff:
```python
import functools

import jax
import jax.numpy as jnp
import numpy as np
from jax import lax
from jax.experimental import pallas as pl
from jax.experimental.pallas import tpu as pltpu
from jax.sharding import PartitionSpec as P

HEADS = 16
FDIM = 16
VHEAD = 128
EPS = 1e-06

bf16 = jnp.bfloat16
f32 = jnp.float32

PAIRS = [(a, b) for a in range(FDIM + 1) for b in range(a, FDIM + 1)]
NPAIR = len(PAIRS)
PADF = 256
STATE_ROWS = 160
CONST = 1 << 20

NN = (((1,), (0,)), ((), ()))
NT = (((1,), (1,)), ((), ()))
TN = (((0,), (0,)), ((), ()))


def mm(a, b, dims=NN):
    return lax.dot_general(a, b, dims, preferred_element_type=f32)


def feature_tables():
    index = np.full((8, PADF), -CONST, np.int32)
    level = np.zeros((8, PADF), np.float32)
    for f, (a, b) in enumerate(PAIRS):
        index[0, f] = a if a < FDIM else CONST
        index[1, f] = b if b < FDIM else CONST
        level[0, f] = float(a == FDIM)
        level[1, f] = float(b == FDIM)
        if a == FDIM:
            level[2, f] = 1.0
        elif b == FDIM:
            level[2, f] = FDIM**-0.5
        elif a == b:
            level[2, f] = 1.0 / (2 * FDIM)
        else:
            level[2, f] = 1.0 / FDIM
    return jnp.asarray(index), jnp.asarray(level)


def cost(flops, moved, trans=0):
    return pl.CostEstimate(flops=int(flops), bytes_accessed=int(moved), transcendentals=int(trans))


def params(mib):
    return pltpu.CompilerParams(vmem_limit_bytes=mib << 20)


def selectors(head, index):
    lanes = lax.broadcasted_iota(jnp.int32, (HEADS * FDIM, PADF), 0) - FDIM * head
    pick_a = jnp.where(lanes == index[0:1, :], 1.0, 0.0).astype(bf16)
    pick_b = jnp.where(lanes == index[1:2, :], 1.0, 0.0).astype(bf16)
    return pick_a, pick_b


def factors(packed, pick_a, pick_b, level):
    return mm(packed, pick_a) + level[0:1, :], mm(packed, pick_b) + level[1:2, :]


def own_lanes(head, packed):
    lane = lax.broadcasted_iota(jnp.int32, packed.shape, 1)
    return jnp.where(lane // FDIM == head, packed, jnp.zeros_like(packed))


def pack_state(state, sums):
    block = state[:STATE_ROWS]
    high = sums.astype(bf16).astype(f32)
    low = sums - high
    row = lax.broadcasted_iota(jnp.int32, block.shape, 0)
    for k, part in enumerate((high[:, :128], high[:, 128:], low[:, :128], low[:, 128:])):
        block = jnp.where(row == NPAIR + k, part, block)
    return block.astype(bf16)


def unpack_state(block):
    row = lax.broadcasted_iota(jnp.int32, block.shape, 0)

    def line(k):
        return jnp.sum(jnp.where(row == NPAIR + k, block, 0.0), axis=0, keepdims=True)

    sums = jnp.concatenate([line(0) + line(2), line(1) + line(3)], axis=1)
    state = jnp.where(row < NPAIR, block, 0.0).astype(bf16)
    pad = jnp.zeros((PADF - STATE_ROWS, VHEAD), bf16)
    return jnp.concatenate([state, pad], axis=0), sums


def column(ref, head):
    lane = lax.broadcasted_iota(jnp.int32, ref.shape, 1)
    return jnp.sum(jnp.where(lane == head, ref[...], 0.0), axis=1, keepdims=True)


def key_state_kernel(index, level, k_ref, v_ref, end_ref, out_ref):
    head = pl.program_id(0)
    pick_a, pick_b = selectors(head, index)
    one, two = factors(k_ref[...], pick_a, pick_b, level)
    feats = (one * two * end_ref[:, 0:1]).astype(bf16)
    state = mm(feats, v_ref[...], TN)
    sums = jnp.sum(feats.astype(f32), axis=0, keepdims=True)
    out_ref[0] = pack_state(state, sums)


def intra_kernel(q_ref, k_ref, v_ref, mask_ref, num_ref, den_ref):
    head = pl.program_id(0)
    scores = mm(own_lanes(head, q_ref[...]), k_ref[...], NT)
    lin = scores * 0.25 + 1.0
    weights = ((lin * lin * 0.5 + 0.5) * mask_ref[...]).astype(bf16)
    values = v_ref[...]
    both = mm(weights, jnp.concatenate([values, jnp.ones_like(values)], axis=1))
    num_ref[...] = both[:, :VHEAD]
    lane = lax.broadcasted_iota(jnp.int32, den_ref.shape, 1)

    @pl.when(head == 0)
    def _():
        den_ref[...] = jnp.zeros_like(den_ref)

    den_ref[...] = jnp.where(lane == head, both[:, VHEAD:], den_ref[...])


def combine_kernel(index, level, q_ref, num_ref, den_ref, state_ref, from_ref, mixed_ref, total_ref):
    head = pl.program_id(0)
    pick_a, pick_b = selectors(head, index)
    one, two = factors(q_ref[...], pick_a, pick_b, level)
    feats = (one * two * level[2:3, :]).astype(bf16)
    state, sums = unpack_state(state_ref[0])
    reach = from_ref[:, 0:1]
    carried = mm(feats, state)
    carried_den = jnp.sum(feats.astype(f32) * sums, axis=1, keepdims=True)
    den = column(den_ref, head) + reach * carried_den
    mixed_ref[...] = ((num_ref[...] + reach * carried) / den).astype(bf16)
    lane = lax.broadcasted_iota(jnp.int32, total_ref.shape, 1)

    @pl.when(head == 0)
    def _():
        total_ref[...] = jnp.zeros_like(total_ref)

    total_ref[...] = jnp.where(lane == head, den, total_ref[...])


def query_state_kernel(
    index, level, q_ref, grad_ref, mixed_ref, den_ref, from_ref, out_ref, gnum_ref, gden_ref
):
    head = pl.program_id(0)
    pick_a, pick_b = selectors(head, index)
    one, two = factors(q_ref[...], pick_a, pick_b, level)
    feats = (one * two * level[2:3, :]).astype(bf16)
    gnum = (grad_ref[...] / column(den_ref, head)).astype(bf16)
    wide = gnum.astype(f32)
    gden = -jnp.sum(wide * mixed_ref[...].astype(f32), axis=1, keepdims=True)
    reach = from_ref[:, 0:1]
    state = mm(feats, (wide * reach).astype(bf16), TN)
    sums = jnp.sum(feats.astype(f32) * (gden * reach), axis=0, keepdims=True)
    out_ref[0] = pack_state(state, sums)
    gnum_ref[...] = gnum
    lane = lax.broadcasted_iota(jnp.int32, gden_ref.shape, 1)

    @pl.when(head == 0)
    def _():
        gden_ref[...] = jnp.zeros_like(gden_ref)

    gden_ref[...] = jnp.where(lane == head, gden, gden_ref[...])


def back_kernel(
    index,
    level,
    q_ref,
    k_ref,
    v_ref,
    mask_ref,
    gnum_ref,
    gden_ref,
    state_ref,
    from_ref,
    gq_ref,
    gk_ref,
    gv_ref,
    gq_sum,
):
    head = pl.program_id(0)
    queries, keys, values = q_ref[...], k_ref[...], v_ref[...]
    gnum = gnum_ref[...]
    gden = column(gden_ref, head)
    q_own, k_own = own_lanes(head, queries), own_lanes(head, keys)
    scores = mm(q_own, keys, NT)
    lin = scores * 0.25 + 1.0
    mask = mask_ref[...]
    weights = ((lin * lin * 0.5 + 0.5) * mask).astype(bf16)
    slopes = ((mm(gnum, values, NT) + gden) * (mask * lin * 0.25)).astype(bf16)
    gv_ref[...] = mm(weights, gnum, TN)
    grad_q = mm(slopes, k_own)
    grad_k = mm(slopes, q_own, TN)

    pick_a, pick_b = selectors(head, index)
    one, two = factors(queries, pick_a, pick_b, level)
    state, sums = unpack_state(state_ref[0])
    gfeat = (mm(gnum, state, NT) + gden * sums) * from_ref[:, 0:1] * level[2:3, :]
    grad_q += mm((gfeat * two).astype(bf16), pick_a, NT)
    grad_q += mm((gfeat * one).astype(bf16), pick_b, NT)

    @pl.when(head == 0)
    def _():
        gq_sum[...] = jnp.zeros_like(gq_sum)
        gk_ref[...] = jnp.zeros_like(gk_ref)

    gq_sum[...] += grad_q
    gk_ref[...] += grad_k

    @pl.when(head == HEADS - 1)
    def _():
        gq_ref[...] = gq_sum[...].astype(bf16)


def back_state_kernel(
    index, level, k_ref, v_ref, gstate_ref, end_ref, gk_in, gv_in, gk_ref, gv_ref, gk_sum
):
    head = pl.program_id(0)
    values = v_ref[...]
    pick_a, pick_b = selectors(head, index)
    one, two = factors(k_ref[...], pick_a, pick_b, level)
    state, sums = unpack_state(gstate_ref[0])
    reach = end_ref[:, 0:1]
    feats = (one * two * reach).astype(bf16)
    gv_ref[...] = (gv_in[...] + mm(feats, state)).astype(bf16)
    gfeat = (mm(values, state, NT) + sums) * reach
    grad_k = mm((gfeat * two).astype(bf16), pick_a, NT)
    grad_k += mm((gfeat * one).astype(bf16), pick_b, NT)

    @pl.when(head == 0)
    def _():
        gk_sum[...] = gk_in[...]

    gk_sum[...] += grad_k

    @pl.when(head == HEADS - 1)
    def _():
        gk_ref[...] = gk_sum[...].astype(bf16)


def whole(shape):
    return pl.BlockSpec(shape, lambda h: (0,) * len(shape))


def per_head(length):
    return pl.BlockSpec((length, VHEAD), lambda h: (0, h))


STATE_SPEC = pl.BlockSpec((1, STATE_ROWS, VHEAD), lambda h: (h, 0, 0))


def head_call(kernel, tables, operands, in_specs, out_shape, out_specs, scratch, flops, moved):
    if tables is not None:

        def body(index_ref, level_ref, *refs):
            kernel(index_ref[...], level_ref[...], *refs)

        operands = (*tables, *operands)
        in_specs = [whole((8, PADF)), whole((8, PADF)), *in_specs]
    else:
        body = kernel
    return pl.pallas_call(
        body,
        grid=(HEADS,),
        in_specs=in_specs,
        out_specs=out_specs,
        out_shape=out_shape,
        scratch_shapes=scratch,
        compiler_params=params(40),
        cost_estimate=cost(flops, moved),
    )(*operands)


def sds(shape, dtype):
    return jax.ShapeDtypeStruct(shape, dtype)


def ff_act_kernel(half, which_ref, x0, x1, g0, g1, wg, wu, wd, hid, gg, gu):
    step = pl.program_id(0)
    first = step < half
    tokens = jnp.where(first, x0[...], x1[...])
    branch = jnp.where(first, g0[...], g1[...])
    gate = mm(tokens, wg[...])
    up = mm(tokens, wu[...])
    grad = mm(branch, wd[...], NT)
    sig = 1.0 / (1.0 + jnp.exp(-gate))
    silu = gate * sig
    hid[...] = (silu * up).astype(bf16)
    gg[...] = (grad * up * (sig * (1.0 + gate * (1.0 - sig)))).astype(bf16)
    gu[...] = (grad * silu).astype(bf16)


def ff_out_kernel(half, which_ref, hid, gg, gu, wg, wu, wd, low0, low1, lay0, lay1):
    step = pl.program_id(0)
    low = (mm(gg[...], wg[...], NT) + mm(gu[...], wu[...], NT)).astype(bf16)
    lay = mm(hid[...], wd[...]).astype(bf16)

    @pl.when(step < half)
    def _():
        low0[...] = low
        lay0[...] = lay

    @pl.when(step >= half)
    def _():
        low1[...] = low
        lay1[...] = lay


def ff_specs(width, slice_ff):
    once = pl.Buffered(1)
    return [
        pl.BlockSpec((width, slice_ff), lambda i, w: (0, w[0]), pipeline_mode=once),
        pl.BlockSpec((width, slice_ff), lambda i, w: (0, w[0]), pipeline_mode=once),
        pl.BlockSpec((slice_ff, width), lambda i, w: (w[0], 0), pipeline_mode=once),
    ]


def ff_act(which, x0, x1, g0, g1, wg, wu, wd, slice_ff):
    count, width = x0.shape
    tile = min(256, count)
    half = count // tile
    low = pl.BlockSpec((tile, width), lambda i, w: (jnp.minimum(i, half - 1), 0))
    high = pl.BlockSpec((tile, width), lambda i, w: (jnp.maximum(i - half, 0), 0))
    out = pl.BlockSpec((tile, slice_ff), lambda i, w: (i, 0))
    total = 2 * count
    return pl.pallas_call(
        functools.partial(ff_act_kernel, half),
        grid_spec=pltpu.PrefetchScalarGridSpec(
            num_scalar_prefetch=1,
            grid=(2 * half,),
            in_specs=[low, high, low, high, *ff_specs(width, slice_ff)],
            out_specs=[out, out, out],
        ),
        out_shape=[sds((total, slice_ff), bf16)] * 3,
        compiler_params=params(56),
        cost_estimate=cost(
            6 * total * width * slice_ff,
            6 * width * slice_ff + 4 * total * width + 6 * total * slice_ff,
            2 * total * slice_ff,
        ),
    )(which, x0, x1, g0, g1, wg, wu, wd)


def ff_out(which, hid, gg, gu, wg, wu, wd, slice_ff):
    total, width = hid.shape[0], wg.shape[0]
    count = total // 2
    tile = min(256, count)
    half = count // tile
    row = pl.BlockSpec((tile, slice_ff), lambda i, w: (i, 0))
    low = pl.BlockSpec((tile, width), lambda i, w: (jnp.minimum(i, half - 1), 0))
    high = pl.BlockSpec((tile, width), lambda i, w: (jnp.maximum(i - half, 0), 0))
    return pl.pallas_call(
        functools.partial(ff_out_kernel, half),
        grid_spec=pltpu.PrefetchScalarGridSpec(
            num_scalar_prefetch=1,
            grid=(2 * half,),
            in_specs=[row, row, row, *ff_specs(width, slice_ff)],
            out_specs=[low, high, low, high],
        ),
        out_shape=[sds((count, width), bf16)] * 4,
        compiler_params=params(56),
        cost_estimate=cost(
            6 * total * width * slice_ff,
            6 * width * slice_ff + 4 * total * width + 6 * total * slice_ff,
        ),
    )(which, hid, gg, gu, wg, wu, wd)


def wide_grad_kernel(groups, ybit_ref, l0, l1, l2, l3, near, far, send, keep):
    count = l0.shape[0]
    total = mm(l0[...], near[:count, :], TN)
    total += mm(l1[...], near[count:, :], TN)
    total += mm(l2[...], far[:count, :], TN)
    total += mm(l3[...], far[count:, :], TN)
    rows = total.shape[0] // groups
    high = ybit_ref[0] == 1
    for g in range(groups):
        a = total[g * rows : g * rows + rows // 2]
        b = total[g * rows + rows // 2 : (g + 1) * rows]
        send[g] = jnp.where(high, a, b).astype(bf16)
        keep[g] = jnp.where(high, b, a).astype(bf16)


def wide_grad(ybit, lows, near, far, group_rows):
    count, width = lows[0].shape
    cols = near.shape[1]
    tile = min(256, width)
    groups = tile // group_rows
    lane = pl.BlockSpec((count, tile), lambda i, w: (0, i))
    held = pl.BlockSpec((2 * count, cols), lambda i, w: (0, 0), pipeline_mode=pl.Buffered(1))
    out = pl.BlockSpec((groups, group_rows // 2, cols), lambda i, w: (i, 0, 0))
    shape = sds((width // group_rows, group_rows // 2, cols), bf16)
    return pl.pallas_call(
        functools.partial(wide_grad_kernel, groups),
        grid_spec=pltpu.PrefetchScalarGridSpec(
            num_scalar_prefetch=1,
            grid=(width // tile,),
            in_specs=[lane, lane, lane, lane, held, held],
            out_specs=[out, out],
        ),
        out_shape=[shape, shape],
        compiler_params=params(48),
        cost_estimate=cost(
            8 * count * width * cols, 8 * count * (width + cols) + 2 * width * cols
        ),
    )(ybit, *lows, near, far)


def down_grad_kernel(near, far, g0, g1, g2, g3, out):
    count = g0.shape[0]
    total = mm(near[:count, :], g0[...], TN)
    total += mm(near[count:, :], g1[...], TN)
    total += mm(far[:count, :], g2[...], TN)
    total += mm(far[count:, :], g3[...], TN)
    out[...] = total.astype(bf16)


def down_grad(near, far, grads):
    count, width = grads[0].shape
    rows = near.shape[1]
    tile = min(256, width)
    lane = pl.BlockSpec((count, tile), lambda i: (0, i))
    held = pl.BlockSpec((2 * count, rows), lambda i: (0, 0), pipeline_mode=pl.Buffered(1))
    return pl.pallas_call(
        down_grad_kernel,
        grid=(width // tile,),
        in_specs=[held, held, lane, lane, lane, lane],
        out_specs=pl.BlockSpec((rows, tile), lambda i: (0, i)),
        out_shape=sds((rows, width), bf16),
        compiler_params=params(48),
        cost_estimate=cost(
            8 * count * width * rows, 8 * count * (width + rows) + 2 * width * rows
        ),
    )(near, far, *grads)


def total_of(terms):
    total = terms[0].astype(f32)
    for term in terms[1:]:
        total = total + term.astype(f32)
    return total


def take(terms, dim, place):
    return [lax.dynamic_index_in_dim(t, place, dim, keepdims=False) for t in terms]


def pair_sum(terms, dim, bit, swap, kind=bf16):
    sent = total_of(take(terms, dim, 1 - bit)).astype(kind)
    return [*take(terms, dim, bit), swap(sent)]


def ring_sum(pick, seq, length, kind=bf16):
    ring = [(s, (s + 1) % length) for s in range(length)]
    held = None
    for k in range(length - 1):
        block = lax.rem(seq - 1 - k + 2 * length, length)
        terms = pick(block) + ([held] if held is not None else [])
        held = lax.ppermute(total_of(terms).astype(kind), "seq", ring)
    return pick(seq) + [held]


def shards(
    tokens,
    lengths,
    gain_one,
    w_query,
    w_key,
    w_value,
    w_out,
    gain_two,
    w_gate,
    w_up,
    w_down,
    cotangent,
):
    rows_dev, stretch, width = tokens.shape
    nfeat, nseq, nrows = (lax.axis_size(a) for a in ("feat", "seq", "rows"))
    assert rows_dev == 1 and nfeat == 2 and nrows == 4 and nseq % 2 == 0
    ff = w_gate.shape[1]
    fi, si, ri = (lax.axis_index(a) for a in ("feat", "seq", "rows"))
    xb, yb = ri % 2, ri // 2
    slice_ff = ff // 4
    which = jnp.reshape(2 * fi + xb, (1,)).astype(jnp.int32)
    ybit = jnp.reshape(yb, (1,)).astype(jnp.int32)

    def over_feat(a):
        return lax.ppermute(a, "feat", [(0, 1), (1, 0)])

    def over_x(a):
        return lax.ppermute(a, "rows", [(r, r ^ 1) for r in range(nrows)])

    def over_y(a):
        return lax.ppermute(a, "rows", [(r, r ^ 2) for r in range(nrows)])

    def spread(own):
        near = over_feat(own)
        far = over_x(own)
        return near, far, over_feat(far)

    flat = tokens.reshape(stretch, width)
    seed = cotangent.reshape(stretch, width)
    grad_branch = lax.optimization_barrier(seed.astype(bf16))
    branch1, branch2, branch3 = spread(grad_branch)

    ndocs = lengths.shape[1]
    doc_lengths = lax.dynamic_index_in_dim(lengths, fi * nrows + ri, 0, keepdims=False)
    starts = jnp.cumsum(doc_lengths) - doc_lengths
    offset = si * stretch

    def doc_of(places):
        return jnp.sum((starts[None, :] <= places[:, None]).astype(jnp.int32), axis=1)

    places = offset + jnp.arange(stretch, dtype=jnp.int32)
    docs = doc_of(places)
    hops = jnp.arange(1, nseq, dtype=jnp.int32)
    before = doc_of(jnp.reshape(offset - 1, (1,)))
    final = doc_of(jnp.reshape(offset + stretch - 1, (1,)))
    causal = jnp.arange(stretch)[None, :] <= jnp.arange(stretch)[:, None]
    mask = ((docs[:, None] == docs[None, :]) & causal).astype(f32)
    from_before = jnp.broadcast_to((docs == before).astype(f32)[:, None], (stretch, 128))
    at_end = jnp.broadcast_to((docs == final).astype(f32)[:, None], (stretch, 128))
    earlier = (doc_of(offset - 1 - (hops - 1) * stretch) == before).astype(f32)
    later = (doc_of(offset + hops * stretch - 1) == final).astype(f32)

    tables = feature_tables()
    length_spec = whole((stretch, 128))
    pack_spec = whole((stretch, HEADS * FDIM))
    mask_spec = whole((stretch, stretch))
    head_spec = per_head(stretch)
    state_shape = sds((HEADS, STATE_ROWS, VHEAD), bf16)
    unit = 2 * HEADS * stretch * 256

    def carried(state, shift, kept):
        pairs = [(s, s + shift) for s in range(nseq) if 0 <= s + shift < nseq]
        total = jnp.zeros(state.shape, f32)
        for k in range(nseq - 1):
            state = lax.ppermute(state, "seq", pairs)
            total = total + kept[k] * state.astype(f32)
        return total

    root_one = lax.rsqrt(jnp.mean(flat * flat, axis=-1, keepdims=True) + EPS)
    low_one = (flat * root_one * gain_one).astype(bf16)
    keys = mm(low_one, w_key).astype(bf16)
    values = mm(low_one, w_value).astype(bf16)
    queries = mm(low_one, w_query).astype(bf16)

    key_state = head_call(
        key_state_kernel,
        tables,
        (keys, values, at_end),
        [pack_spec, head_spec, length_spec],
        state_shape,
        STATE_SPEC,
        [],
        unit * 3 * 256,
        4 << 20,
    )
    state_in = carried(key_state, 1, earlier)
    numer, denom_here = head_call(
        intra_kernel,
        None,
        (queries, keys, values, mask),
        [pack_spec, pack_spec, head_spec, mask_spec],
        [sds((stretch, width), f32), sds((stretch, 128), f32)],
        [head_spec, length_spec],
        [],
        unit * 4 * 256,
        9 << 20,
    )
    mixed_low, denom = head_call(
        combine_kernel,
        tables,
        (queries, numer, denom_here, state_in, from_before),
        [pack_spec, head_spec, length_spec, STATE_SPEC, length_spec],
        [sds((stretch, width), bf16), sds((stretch, 128), f32)],
        [head_spec, length_spec],
        [],
        unit * 3 * 256,
        9 << 20,
    )
    middle = flat + mm(mixed_low, w_out)
    root_two = lax.rsqrt(jnp.mean(middle * middle, axis=-1, keepdims=True) + EPS)
    low_two = lax.optimization_barrier((middle * root_two * gain_two).astype(bf16))
    low1, low2, low3 = spread(low_two)

    weights = (w_gate, w_up, w_down)
    hid_n, gg_n, gu_n = ff_act(
        which, low_two, low1, grad_branch, branch1, *weights, slice_ff
    )
    glow0, glow1, lay0, lay1 = ff_out(which, hid_n, gg_n, gu_n, *weights, slice_ff)
    hid_f, gg_f, gu_f = ff_act(which, low2, low3, branch2, branch3, *weights, slice_ff)
    glow2, glow3, lay2, lay3 = ff_out(which, hid_f, gg_f, gu_f, *weights, slice_ff)

    def gathered(own, near, far, far_near):
        other = (far.astype(f32) + over_feat(far_near).astype(f32)).astype(bf16)
        return total_of([own, over_feat(near), over_x(other)])

    grad_low_two = gathered(glow0, glow1, glow2, glow3)
    lay_sum = gathered(lay0, lay1, lay2, lay3)
    layer_out = middle + lay_sum

    lows = (low_two, low1, low2, low3)
    group_rows = width // (2 * nseq)

    def wide_share(near, far):
        sent, kept = wide_grad(ybit, lows, near, far, group_rows)
        terms = [kept, over_y(sent)]
        split = [t.reshape(2, nseq, 2, group_rows // 4, slice_ff) for t in terms]
        mine = total_of(ring_sum(lambda b: take(split, 1, b), si, nseq)).astype(bf16)
        own = lax.dynamic_index_in_dim(mine, xb, 1, keepdims=False)
        other = over_x(lax.dynamic_index_in_dim(mine, 1 - xb, 1, keepdims=False))
        cols = jnp.where(
            xb == 0,
            jnp.concatenate([own, other], axis=-1),
            jnp.concatenate([other, own], axis=-1),
        )
        own = lax.dynamic_index_in_dim(cols, fi, 0, keepdims=False)
        other = over_feat(lax.dynamic_index_in_dim(cols, 1 - fi, 0, keepdims=False))
        return jnp.where(
            fi == 0,
            jnp.concatenate([own, other], axis=-1),
            jnp.concatenate([other, own], axis=-1),
        ).astype(f32)

    def down_share():
        grad = down_grad(hid_n, hid_f, (grad_branch, branch1, branch2, branch3))
        rows = slice_ff // (2 * nseq)
        split = grad.reshape(nseq // 2, 2, 2, rows, width)

        def pick(b):
            zero = jnp.int32(0)
            part = lax.dynamic_slice(
                split,
                (b % (nseq // 2), zero, b // (nseq // 2), zero, zero),
                (1, 2, 1, rows, width),
            )
            return [part.reshape(2, rows, width)]

        terms = ring_sum(pick, si, nseq)
        terms = pair_sum(terms, 0, yb, over_y)
        mine = total_of(terms).astype(bf16)
        swaps = []
        for s in range(nseq):
            for r in range(nrows):
                x = s // (nseq // 2)
                if x != r % 2:
                    to = (r % 2) * (nseq // 2) + s % (nseq // 2)
                    swaps.append((s * nrows + r, to * nrows + (r ^ 1)))
        moved = lax.ppermute(mine, ("seq", "rows"), swaps)
        stays = (si // (nseq // 2)) == xb
        return jnp.where(stays, mine, moved).astype(f32)

    grad_gate_w = wide_share(gg_n, gg_f)
    grad_up_w = wide_share(gu_n, gu_f)
    grad_down_w = down_share()

    unit_two = middle * root_two
    grad_gain_two = jnp.sum(grad_low_two * unit_two, axis=0)
    scaled = grad_low_two * gain_two
    grad_middle = seed + root_two * (
        scaled - unit_two * jnp.mean(scaled * unit_two, axis=-1, keepdims=True)
    )
    grad_mixed_low = grad_middle.astype(bf16)
    grad_mixed = mm(grad_mixed_low, w_out, NT)

    query_state, gnum, gden = head_call(
        query_state_kernel,
        tables,
        (queries, grad_mixed, mixed_low, denom, from_before),
        [pack_spec, head_spec, head_spec, length_spec, length_spec],
        [state_shape, sds((stretch, width), bf16), sds((stretch, 128), f32)],
        [STATE_SPEC, head_spec, length_spec],
        [],
        unit * 3 * 256,
        10 << 20,
    )
    state_back = carried(query_state, -1, later)
    grad_queries, grad_keys_part, grad_values_part = head_call(
        back_kernel,
        tables,
        (queries, keys, values, mask, gnum, gden, state_in, from_before),
        [
            pack_spec,
            pack_spec,
            head_spec,
            mask_spec,
            head_spec,
            length_spec,
            STATE_SPEC,
            length_spec,
        ],
        [
            sds((stretch, HEADS * FDIM), bf16),
            sds((stretch, HEADS * FDIM), f32),
            sds((stretch, width), f32),
        ],
        [pack_spec, pack_spec, head_spec],
        [pltpu.VMEM((stretch, HEADS * FDIM), f32)],
        unit * 15 * 256,
        10 << 20,
    )
    grad_keys, grad_values_low = head_call(
        back_state_kernel,
        tables,
        (keys, values, state_back, at_end, grad_keys_part, grad_values_part),
        [pack_spec, head_spec, STATE_SPEC, length_spec, pack_spec, head_spec],
        [sds((stretch, HEADS * FDIM), bf16), sds((stretch, width), bf16)],
        [pack_spec, head_spec],
        [pltpu.VMEM((stretch, HEADS * FDIM), f32)],
        unit * 6 * 256,
        10 << 20,
    )
    grad_low_one = (
        mm(grad_queries, w_query, NT)
        + mm(grad_keys, w_key, NT)
        + mm(grad_values_low, w_value, NT)
    )
    unit_one = flat * root_one
    grad_gain_one = jnp.sum(grad_low_one * unit_one, axis=0)
    scaled = grad_low_one * gain_one
    grad_tokens = grad_middle + root_one * (
        scaled - unit_one * jnp.mean(scaled * unit_one, axis=-1, keepdims=True)
    )

    part = width // (8 * nseq)

    def share(grad, order, kind=bf16):
        terms = [grad.reshape(2, nseq, 2, 2, part, grad.shape[-1])]
        dims = {"feat": 0, "seq": 1, "y": 2, "x": 3}
        for name in order:
            dim = dims.pop(name)
            dims = {k: v - (v > dim) for k, v in dims.items()}
            if name == "seq":
                now = terms
                terms = ring_sum(lambda b: take(now, dim, b), si, nseq, kind)
            else:
                bit, swap = {
                    "feat": (fi, over_feat),
                    "x": (xb, over_x),
                    "y": (yb, over_y),
                }[name]
                terms = pair_sum(terms, dim, bit, swap, kind)
        return total_of(terms)

    grad_out_w = share(mm(mixed_low, grad_mixed_low, TN).astype(bf16), ("feat", "x", "y", "seq"))
    grad_value_w = share(
        mm(low_one, grad_values_low, TN).astype(bf16), ("feat", "x", "y", "seq")
    )
    grad_qk = mm(low_one, jnp.concatenate([grad_queries, grad_keys], axis=-1), TN).astype(bf16)
    grad_qk_w = share(grad_qk, ("feat", "x", "seq", "y"))
    both = jnp.concatenate(
        [grad_gain_one.reshape(-1, 1, part), grad_gain_two.reshape(-1, 1, part)], axis=-1
    )
    blocks = [both.reshape(2, nseq, 2, 2, 2 * part)]
    blocks = pair_sum(blocks, 0, fi, over_feat, f32)
    blocks = pair_sum(blocks, 1, yb, over_y, f32)
    blocks = pair_sum(blocks, 1, xb, over_x, f32)
    now = blocks
    gains = total_of(ring_sum(lambda b: take(now, 0, b), si, nseq, f32))

    qk = w_query.shape[1]
    return (
        layer_out.reshape(rows_dev, stretch, width),
        grad_tokens.reshape(rows_dev, stretch, width),
        gains[:part],
        grad_qk_w[:, :qk],
        grad_qk_w[:, qk:],
        grad_value_w,
        grad_out_w,
        gains[part:],
        grad_gate_w,
        grad_up_w,
        grad_down_w,
    )


def solution(mesh):
    split = P(("feat", "rows"), "seq", None)
    vector = P(("feat", "seq", "rows"))
    matrix = P(("feat", "seq", "rows"), None)
    in_specs = (split, *(P() for _ in range(10)), split)
    out_specs = (
        split,
        split,
        vector,
        matrix,
        matrix,
        matrix,
        matrix,
        vector,
        matrix,
        matrix,
        matrix,
    )
    return jax.shard_map(shards, mesh=mesh, in_specs=in_specs, out_specs=out_specs, check_vma=False)
```

time: 4700 us -> 842 us (0.18)
  waiting for transfers between devices: 3890 us -> 351 us
  matrix products: 507 us -> 49.3 us
  Pallas kernels: 0 us -> 271 us
  blocking collectives: 97.7 us -> 0 us
  starting transfers between devices: 0.62 us -> 55 us
    reduce_scatter x10 -> x0, waiting for transfers between devices: 3770 us -> none  [the longest x1 977 us: shards(): lax.psum_scatter(contract_rows(low_two, grad_up), ('feat', 'seq', 'rows')...]
    dot_general x35 -> x11, matrix products: 507 us -> 49.3 us  [mm(): return lax.dot_general(a, b, dims, preferred_element_type=f32)]
    ppermute x0 -> x59, waiting for transfers between devices: none -> 351 us  [the longest x10 146 us: over_x(): return lax.ppermute(a, 'rows', [(r, r ^ 1) for r in range(nrows)])]
    pallas_call x0 -> x13, Pallas kernels: none -> 271 us  [the longest x6 95.2 us: head_call(): pl.pallas_call(body, grid=(HEADS,), in_specs=in_specs, out_specs=out_spec...]
    all_gather x4 -> x0, waiting for transfers between devices: 89.4 us -> none  [the longest x1 89.4 us: carried_in(): everything = jax.tree.map(lambda part: lax.all_gather(part, axis), value)]
    unnamed x3 -> x0, blocking collectives: 63.5 us -> none
    ppermute x0 -> x59, starting transfers between devices: none -> 55 us  [the longest x6 18.7 us: carried(): state = lax.ppermute(state, 'seq', pairs)]
    convert_element_type x7 -> x38, other arithmetic: 7.61 us -> 59.5 us  [the longest x17 24.6 us: ring_sum(): held = lax.ppermute(total_of(terms).astype(kind), 'seq', ring)]
  transfers between devices with their start and end apart: 15 -> 59, of which waited for: 8 -> 27; matrix products, arithmetic and copies ran while one was open for 9% -> 16% of each run, Pallas kernels for 0% -> 26%
where the time goes in v1:
time: 842 us; the launch traced here: 836 us
  waiting for transfers between devices  351 us (42%)
  Pallas kernels  271 us (32%)
  other arithmetic  87.3 us (10%)
  starting transfers between devices  55 us (7%)
  matrix products  49.3 us (6%)
  local copies, waits for them, and re-layouts  21.2 us (3%)
    ppermute x10, waiting for transfers between devices, over_x(): return lax.ppermute(a, 'rows', [(r, r ^ 1) for r in range(nrows)])  146 us
    pallas_call x6, Pallas kernels, head_call(): pl.pallas_call(body, grid=(HEADS,), in_specs=in_specs, out_specs=out_spec...  95.2 us
    ppermute x21, waiting for transfers between devices, ring_sum(): held = lax.ppermute(total_of(terms).astype(kind), 'seq', ring)  74.2 us
    ppermute x6, waiting for transfers between devices, carried(): state = lax.ppermute(state, 'seq', pairs)  66.3 us
    ppermute x7, waiting for transfers between devices, over_y(): return lax.ppermute(a, 'rows', [(r, r ^ 2) for r in range(nrows)])  63.8 us
    pallas_call x2, Pallas kernels, ff_out(): pl.pallas_call(functools.partial(ff_out_kernel, half), grid_spec=pltpu.Pr...  60.6 us
    pallas_call x2, Pallas kernels, ff_act(): pl.pallas_call(functools.partial(ff_act_kernel, half), grid_spec=pltpu.Pr...  58.5 us
    dot_general x11, matrix products, mm(): return lax.dot_general(a, b, dims, preferred_element_type=f32)  49.3 us
  transfers between devices with their start and end apart: 59, of which 27 were waited for; matrix products, arithmetic and copies ran while one was open for 16% of the time, Pallas kernels for 26%

profile of v1, /device:TPU:0, one launch (start us, length us, event | category | flops | bytes accessed | tf_op | source)
XLA Modules:
  0.0 836.0 jit_solution(2020117832853615801)
XLA Ops:
  1.6 2.7 fusion.2
  6.2 8.8 %convolution_convert_fusion.3.v_ref.refs_1_.refs_2_ = bf16[512,2048]{1,0:T(8,128)(2,1)S(1)} fusion(bf16[512,2048]{1,0:T(8,128)(2,1)S(1)} %multiply_convert_fusion.1, bf16[2048,2048]{1,0:T(8,128)(2,1)} %param.19), kind=kOutput, calls=%fused_computation.28 | convolution fusion | flops 4296015872 | bytes 12582912 | tf_op jit(solution)/shard_map/dot_general | solution.py:31
  18.8 9.3 %shard_map.222 = bf16[16,160,128]{2,1,0:T(8,128)(2,1)S(1)} custom-call(s32[8,256]{1,0:T(8,128)S(1)} %copy-done.11, f32[8,256]{1,0:T(8,128)S(1)} %copy-done.13, bf16[512,256]{1,0:T(8,128)(2,1)S(1)} %convolution_convert_fusion.4.k_ref.refs_0_.refs_1_, bf16[512,2048]{1,0:T(8,128)(2,1)S(1)} %convolution_convert_fusion.3.v_ref.refs_1_.refs_2_, ...), custom_call_target="tpu_custom_call" | custom-call | flops 3221225472 | bytes 4194304 | tf_op jit(solution)/shard_map/pallas_call | solution.py:272
  28.1 5.1 collective-permute-start
  35.2 12.0 %collective-permute-done = bf16[16,160,128]{2,1,0:T(8,128)(2,1)S(1)} collective-permute-done((bf16[16,160,128]{2,1,0:T(8,128)(2,1)S(1)}, bf16[16,160,128]{2,1,0:T(8,128)(2,1)S(1)}, u32[]{:S(2)}, u32[]{:S(2)}) %collective-permute-start) | collective-permute-done | bytes 655392 | tf_op jit(solution)/shard_map/ppermute | solution.py:548
  47.2 4.4 collective-permute-start.1
  53.9 10.9 %collective-permute-done.1 = bf16[16,160,128]{2,1,0:T(8,128)(2,1)S(1)} collective-permute-done((bf16[16,160,128]{2,1,0:T(8,128)(2,1)S(1)}, bf16[16,160,128]{2,1,0:T(8,128)(2,1)S(1)}, u32[]{:S(2)}, u32[]{:S(2)}) %collective-permute-start.1) | collective-permute-done | bytes 655392 | tf_op jit(solution)/shard_map/ppermute | solution.py:548
  64.8 4.9 collective-permute-start.2
  70.5 10.7 %shard_map.221 = (f32[512,2048]{1,0:T(8,128)S(1)}, f32[512,128]{1,0:T(8,128)S(1)}) custom-call(bf16[512,256]{1,0:T(8,128)(2,1)S(1)} %convolution_convert_fusion.5.q_ref.refs_0_, bf16[512,256]{1,0:T(8,128)(2,1)S(1)} %convolution_convert_fusion.4.k_ref.refs_0_.refs_1_, bf16[512,2048]{1,0:T(8,128)(2,1)S(1)} %convolution_convert_fusion.3.v_ref.refs_1_.refs_2_, ...), custom_call_target="tpu_custom_call" | custom-call | flops 4294967296 | bytes 9437184 | tf_op jit(solution)/shard_map/pallas_call | solution.py:272
  81.5 2.6 multiply_add_fusion.1.refs_3_.refs_6_
  84.3 15.9 %shard_map.223 = (bf16[512,2048]{1,0:T(8,128)(2,1)S(1)}, f32[512,128]{1,0:T(8,128)S(1)}) custom-call(s32[8,256]{1,0:T(8,128)S(1)} %copy-done.11, f32[8,256]{1,0:T(8,128)S(1)} %copy-done.13, bf16[512,256]{1,0:T(8,128)(2,1)S(1)} %convolution_convert_fusion.5.q_ref.refs_0_, f32[512,2048]{1,0:T(8,128)S(1)} %get-tuple-element.41.refs_1_, ...), custom_call_target="tpu_custom_call" | custom-call | flops 3221225472 | bytes 9437184 | tf_op jit(solution)/shard_map/pallas_call | solution.py:272
  100.3 4.6 multiply_reduce_fusion.4
  109.5 43.6 %collective-permute-done.6.x0.l2 = bf16[512,2048]{1,0:T(8,128)(2,1)} collective-permute-done((bf16[512,2048]{1,0:T(8,128)(2,1)}, bf16[512,2048]{1,0:T(8,128)(2,1)}, u32[]{:S(2)}, u32[]{:S(2)}) %collective-permute-start.6) | collective-permute-done | bytes 2097184 | tf_op jit(solution)/shard_map/ppermute | solution.py:501
  153.7 29.1 %shard_map.224 = (bf16[1024,1408]{1,0:T(8,128)(2,1)}, bf16[1024,1408]{1,0:T(8,128)(2,1)}, bf16[1024,1408]{1,0:T(8,128)(2,1)}) custom-call(s32[1]{0:T(128)} %bitcast.5.which_ref, bf16[512,2048]{1,0:T(8,128)(2,1)} %multiply_convert_fusion.x0.l0, bf16[512,2048]{1,0:T(8,128)(2,1)} %collective-permute-done.3.x1.l1, bf16[512,2048]{1,0:T(8,128)(2,1)} %copy-done.1, ...), custom_call_target="tpu_custom_call" | custom-call | flops 17716740096 | bytes 34340864 | tf_op jit(solution)/shard_map/pallas_call | solution.py:336
  182.8 29.4 %shard_map.226 = (bf16[1024,1408]{1,0:T(8,128)(2,1)}, bf16[1024,1408]{1,0:T(8,128)(2,1)}, bf16[1024,1408]{1,0:T(8,128)(2,1)}) custom-call(s32[1]{0:T(128)} %bitcast.5.which_ref, bf16[512,2048]{1,0:T(8,128)(2,1)} %collective-permute-done.6.x0.l2, bf16[512,2048]{1,0:T(8,128)(2,1)} %collective-permute-done.7.x1.l3, ...), custom_call_target="tpu_custom_call" | custom-call | flops 17716740096 | bytes 34340864 | tf_op jit(solution)/shard_map/pallas_call | solution.py:336
  212.3 18.0 %shard_map.233 = bf16[1408,2048]{1,0:T(8,128)(2,1)} custom-call(bf16[1024,1408]{1,0:T(8,128)(2,1)} %get-tuple-element.44.hid.near, bf16[1024,1408]{1,0:T(8,128)(2,1)} %get-tuple-element.49.hid.far, bf16[512,2048]{1,0:T(8,128)(2,1)S(1)} %copy-done.2, bf16[512,2048]{1,0:T(8,128)(2,1)} %collective-permute-done.4.g1, ...), custom_call_target="tpu_custom_call" | custom-call | flops 11811160064 | bytes 19922944 | tf_op jit(solution)/shard_map/pallas_call | solution.py:434
  230.3 2.6 dynamic-slice_bitcast_fusion.2
  235.1 19.3 %shard_map.232 = (bf16[8,128,1408]{2,1,0:T(8,128)(2,1)}, bf16[8,128,1408]{2,1,0:T(8,128)(2,1)}) custom-call(s32[1]{0:T(128)} %bitcast.101.ybit_ref, bf16[512,2048]{1,0:T(8,128)(2,1)} %multiply_convert_fusion.x0.l0, bf16[512,2048]{1,0:T(8,128)(2,1)} %collective-permute-done.3.x1.l1, bf16[512,2048]{1,0:T(8,128)(2,1)} %collective-permute-done.6.x0.l2, ...), custom_call_target="tpu_custom_call" | custom-call | flops 11811160064 | bytes 19922944 | tf_op jit(solution)/shard_map/pallas_call | solution.py:403
  255.9 30.3 %shard_map.227 = (bf16[512,2048]{1,0:T(8,128)(2,1)}, bf16[512,2048]{1,0:T(8,128)(2,1)}, bf16[512,2048]{1,0:T(8,128)(2,1)}, bf16[512,2048]{1,0:T(8,128)(2,1)}) custom-call(s32[1]{0:T(128)} %bitcast.5.which_ref, bf16[1024,1408]{1,0:T(8,128)(2,1)} %get-tuple-element.49.hid.far, bf16[1024,1408]{1,0:T(8,128)(2,1)} %get-tuple-element.50.gg.far, ...), custom_call_target="tpu_custom_call" | custom-call | flops 17716740096 | bytes 34340864 | tf_op jit(solution)/shard_map/pallas_call | solution.py:362
  286.1 18.9 %shard_map.231 = (bf16[8,128,1408]{2,1,0:T(8,128)(2,1)}, bf16[8,128,1408]{2,1,0:T(8,128)(2,1)}) custom-call(s32[1]{0:T(128)} %bitcast.101.ybit_ref, bf16[512,2048]{1,0:T(8,128)(2,1)} %multiply_convert_fusion.x0.l0, bf16[512,2048]{1,0:T(8,128)(2,1)} %collective-permute-done.3.x1.l1, bf16[512,2048]{1,0:T(8,128)(2,1)} %collective-permute-done.6.x0.l2, ...), custom_call_target="tpu_custom_call" | custom-call | flops 11811160064 | bytes 19922944 | tf_op jit(solution)/shard_map/pallas_call | solution.py:403
  306.0 30.4 %shard_map.225 = (bf16[512,2048]{1,0:T(8,128)(2,1)}, bf16[512,2048]{1,0:T(8,128)(2,1)}, bf16[512,2048]{1,0:T(8,128)(2,1)}, bf16[512,2048]{1,0:T(8,128)(2,1)}) custom-call(s32[1]{0:T(128)} %bitcast.5.which_ref, bf16[1024,1408]{1,0:T(8,128)(2,1)} %get-tuple-element.44.hid.near, bf16[1024,1408]{1,0:T(8,128)(2,1)} %get-tuple-element.45.gg.near, ...), custom_call_target="tpu_custom_call" | custom-call | flops 17716740096 | bytes 34340864 | tf_op jit(solution)/shard_map/pallas_call | solution.py:362
  340.5 2.5 add_convert_fusion
  347.1 2.7 add_convert_fusion.1
  349.8 31.3 %collective-permute-done.42 = bf16[8,128,1408]{2,1,0:T(8,128)(2,1)} collective-permute-done((bf16[8,128,1408]{2,1,0:T(8,128)(2,1)}, bf16[8,128,1408]{2,1,0:T(8,128)(2,1)}, u32[]{:S(2)}, u32[]{:S(2)}) %collective-permute-start.42) | collective-permute-done | bytes 2883616 | tf_op jit(solution)/shard_map/ppermute | solution.py:504
  384.0 5.9 collective-permute-done.49
  391.6 2.4 fusion.10
  394.0 15.3 %collective-permute-done.43 = bf16[2,2,64,1408]{3,2,1,0:T(8,128)(2,1)S(1)} collective-permute-done((bf16[2,2,64,1408]{3,2,1,0:T(8,128)(2,1)S(1)}, bf16[2,2,64,1408]{3,2,1,0:T(8,128)(2,1)S(1)}, u32[]{:S(2)}, u32[]{:S(2)}) %collective-permute-start.43) | collective-permute-done | bytes 720928 | tf_op jit(solution)/shard_map/ppermute | solution.py:469
  413.9 21.9 %collective-permute-done.11 = bf16[512,2048]{1,0:T(8,128)(2,1)} collective-permute-done((bf16[512,2048]{1,0:T(8,128)(2,1)S(1)}, bf16[512,2048]{1,0:T(8,128)(2,1)}, u32[]{:S(2)}, u32[]{:S(2)}) %collective-permute-start.11) | collective-permute-done | bytes 2097184 | tf_op jit(solution)/shard_map/ppermute | solution.py:501
  435.8 6.7 bitcast_add_fusion
  442.4 6.8 convolution_convert_fusion
  449.3 6.9 fusion.18.refs_1_
  456.3 4.8 dynamic-slice_bitcast_fusion
  461.2 11.7 %shard_map.228 = (bf16[16,160,128]{2,1,0:T(8,128)(2,1)S(1)}, bf16[512,2048]{1,0:T(8,128)(2,1)S(1)}, f32[512,128]{1,0:T(8,128)S(1)}) custom-call(s32[8,256]{1,0:T(8,128)S(1)} %copy-done.12, f32[8,256]{1,0:T(8,128)S(1)} %copy-done.14, bf16[512,256]{1,0:T(8,128)(2,1)S(1)} %copy-done.18, f32[512,2048]{1,0:T(8,128)S(1)} %fusion.18.refs_1_, ...), custom_call_target="tpu_custom_call" | custom-call | flops 3221225472 | bytes 10485760 | tf_op jit(solution)/shard_map/pallas_call | solution.py:272
  474.3 31.5 %shard_map.229 = (bf16[512,256]{1,0:T(8,128)(2,1)S(1)}, f32[512,256]{1,0:T(8,128)S(1)}, f32[512,2048]{1,0:T(8,128)S(1)}) custom-call(s32[8,256]{1,0:T(8,128)S(1)} %copy-done.12, f32[8,256]{1,0:T(8,128)S(1)} %copy-done.14, bf16[512,256]{1,0:T(8,128)(2,1)S(1)} %copy-done.18, bf16[512,256]{1,0:T(8,128)(2,1)S(1)} %copy-done.16, ...), custom_call_target="tpu_custom_call" | custom-call | flops 16106127360 | bytes 10485760 | tf_op jit(solution)/shard_map/pallas_call | solution.py:272
  514.9 2.7 collective-permute-start.51
  522.0 8.3 collective-permute-done.57
  532.7 3.5 collective-permute-done.51
  537.6 2.6 collective-permute-start.52
  540.2 11.3 %collective-permute-done.45 = bf16[2,2,64,1408]{3,2,1,0:T(8,128)(2,1)S(1)} collective-permute-done((bf16[2,2,64,1408]{3,2,1,0:T(8,128)(2,1)S(1)}, bf16[2,2,64,1408]{3,2,1,0:T(8,128)(2,1)S(1)}, u32[]{:S(2)}, u32[]{:S(2)}) %collective-permute-start.45) | collective-permute-done | bytes 720928 | tf_op jit(solution)/shard_map/ppermute | solution.py:469
  554.5 7.5 collective-permute-done.46
  562.3 2.5 collective-permute-done.16
  569.0 40.7 %collective-permute-done.17 = bf16[16,160,128]{2,1,0:T(8,128)(2,1)S(1)} collective-permute-done((bf16[16,160,128]{2,1,0:T(8,128)(2,1)S(1)}, bf16[16,160,128]{2,1,0:T(8,128)(2,1)S(1)}, u32[]{:S(2)}, u32[]{:S(2)}) %collective-permute-start.17) | collective-permute-done | bytes 655392 | tf_op jit(solution)/shard_map/ppermute | solution.py:548
  609.7 3.3 multiply_add_fusion.refs_2_
  613.1 15.9 %shard_map.230 = (bf16[512,256]{1,0:T(8,128)(2,1)S(1)}, bf16[512,2048]{1,0:T(8,128)(2,1)S(1)}) custom-call(s32[8,256]{1,0:T(8,128)S(1)} %copy-done.12, f32[8,256]{1,0:T(8,128)S(1)} %copy-done.14, bf16[512,256]{1,0:T(8,128)(2,1)S(1)} %copy-done.16, bf16[512,2048]{1,0:T(8,128)(2,1)S(1)} %copy-done.23, f32[16,160,128]{2,1,0:T(8,128)S(1)} %multiply_add_fusion.refs_2_, ...), custom_call_target="tpu_custom_call" | custom-call | flops 6442450944 | bytes 10485760 | tf_op jit(solution)/shard_map/pallas_call | solution.py:272
  629.0 6.4 convolution_convert_fusion.1
  635.5 2.8 dynamic-slice_bitcast_fusion.1
  644.5 7.1 fusion.98
  651.7 3.7 multiply_reduce_fusion.1
  657.5 3.1 collective-permute-done.19
  660.7 3.2 fusion
  668.8 3.2 fusion.1
  673.9 3.1 add_bitcast_fusion
  677.1 46.7 %collective-permute-done.25 = bf16[4,2,64,512]{3,2,1,0:T(8,128)(2,1)} collective-permute-done((bf16[4,2,64,512]{3,2,1,0:T(8,128)(2,1)}, bf16[4,2,64,512]{3,2,1,0:T(8,128)(2,1)}, u32[]{:S(2)}, u32[]{:S(2)}) %collective-permute-start.25) | collective-permute-done | bytes 524320 | tf_op jit(solution)/shard_map/ppermute | solution.py:501
  725.7 6.0 collective-permute-done.26
  735.5 4.4 collective-permute-done.27
  741.0 25.9 %collective-permute-done.31 = bf16[4,2,64,2048]{3,2,1,0:T(8,128)(2,1)} collective-permute-done((bf16[4,2,64,2048]{3,2,1,0:T(8,128)(2,1)S(1)}, bf16[4,2,64,2048]{3,2,1,0:T(8,128)(2,1)}, u32[]{:S(2)}, u32[]{:S(2)}) %collective-permute-start.31) | collective-permute-done | bytes 2097184 | tf_op jit(solution)/shard_map/ppermute | solution.py:501
  766.9 2.4 fusion.6
  773.1 21.1 %collective-permute-done.29 = bf16[64,512]{1,0:T(8,128)(2,1)S(1)} collective-permute-done((bf16[64,512]{1,0:T(8,128)(2,1)S(1)}, bf16[64,512]{1,0:T(8,128)(2,1)S(1)}, u32[]{:S(2)}, u32[]{:S(2)}) %collective-permute-start.29) | collective-permute-done | bytes 65568 | tf_op jit(solution)/shard_map/ppermute | solution.py:504
  798.9 7.6 collective-permute-done.39
  807.8 4.3 collective-permute-done.33
  813.5 4.2 collective-permute-done.40
  819.0 5.3 collective-permute-done.34
  825.6 3.3 collective-permute-done.41
  831.0 2.8 collective-permute-done.35
  (281 shorter events, 104.8 us)
Async XLA Ops:
  6.2 46.9 %copy-start.42 = (bf16[512,2048]{1,0:T(8,128)(2,1)}, bf16[512,2048]{1,0:T(8,128)(2,1)S(1)}, u32[]{:S(2)}) copy-start(bf16[512,2048]{1,0:T(8,128)(2,1)S(1)} %multiply_convert_fusion.1) | copy-start | bytes 6291460
  15.1 55.4 %copy-start.21 = (bf16[512,2048]{1,0:T(8,128)(2,1)}, bf16[512,2048]{1,0:T(8,128)(2,1)S(1)}, u32[]{:S(2)}) copy-start(bf16[512,2048]{1,0:T(8,128)(2,1)S(1)} %convolution_convert_fusion.3.v_ref.refs_1_.refs_2_) | copy-start | bytes 6291460
  15.8 54.7 %copy-start.15 = (bf16[512,256]{1,0:T(8,128)(2,1)}, bf16[512,256]{1,0:T(8,128)(2,1)S(1)}, u32[]{:S(2)}) copy-start(bf16[512,256]{1,0:T(8,128)(2,1)S(1)} %convolution_convert_fusion.4.k_ref.refs_0_.refs_1_) | copy-start | bytes 786436
  28.1 19.0 %collective-permute-start = (bf16[16,160,128]{2,1,0:T(8,128)(2,1)S(1)}, bf16[16,160,128]{2,1,0:T(8,128)(2,1)S(1)}, u32[]{:S(2)}, u32[]{:S(2)}) collective-permute-start(bf16[16,160,128]{2,1,0:T(8,128)(2,1)S(1)} %shard_map.222), channel_id=1, source_target_pairs={{0,4},{4,8},{8,12},{1,5},{5,9},{9,13},{2,6},{6,10},{10,14},{3,7},{... | collective-permute-start | bytes 1966088 | tf_op jit(solution)/shard_map/ppermute | solution.py:548
  33.6 75.4 %copy-start.1 = (bf16[512,2048]{1,0:T(8,128)(2,1)}, bf16[512,2048]{1,0:T(8,128)(2,1)S(1)}, u32[]{:S(2)}) copy-start(bf16[512,2048]{1,0:T(8,128)(2,1)S(1)} %bitcast_convert_fusion.g0) | copy-start | bytes 6291460
  33.6 75.9 %collective-permute-start.8 = (bf16[512,2048]{1,0:T(8,128)(2,1)S(1)}, bf16[512,2048]{1,0:T(8,128)(2,1)}, u32[]{:S(2)}, u32[]{:S(2)}) collective-permute-start(bf16[512,2048]{1,0:T(8,128)(2,1)S(1)} %bitcast_convert_fusion.g0), channel_id=1, source_target_pairs={{0,1},{1,0},{2,3},{3,2},{4,5},{5,4},{6,7},{7,6},{8,9},{9,8},{10,11... | collective-permute-start | bytes 6291464 | tf_op jit(solution)/shard_map/ppermute | solution.py:501
  47.2 17.6 %collective-permute-start.1 = (bf16[16,160,128]{2,1,0:T(8,128)(2,1)S(1)}, bf16[16,160,128]{2,1,0:T(8,128)(2,1)S(1)}, u32[]{:S(2)}, u32[]{:S(2)}) collective-permute-start(bf16[16,160,128]{2,1,0:T(8,128)(2,1)S(1)} %collective-permute-done), channel_id=1, source_target_pairs={{0,4},{4,8},{8,12},{1,5},{5,9},{9,13},{2,6},{6,10},{10,14},{3,7},{... | collective-permute-start | bytes 1966088 | tf_op jit(solution)/shard_map/ppermute | solution.py:548
  64.8 16.8 %collective-permute-start.2 = (bf16[16,160,128]{2,1,0:T(8,128)(2,1)S(1)}, bf16[16,160,128]{2,1,0:T(8,128)(2,1)S(1)}, u32[]{:S(2)}, u32[]{:S(2)}) collective-permute-start(bf16[16,160,128]{2,1,0:T(8,128)(2,1)S(1)} %collective-permute-done.1), channel_id=1, source_target_pairs={{0,4},{4,8},{8,12},{1,5},{5,9},{9,13},{2,6},{6,10},{10,14},{3,7},{... | collective-permute-start | bytes 1966088 | tf_op jit(solution)/shard_map/ppermute | solution.py:548
  107.5 45.6 %collective-permute-start.6 = (bf16[512,2048]{1,0:T(8,128)(2,1)}, bf16[512,2048]{1,0:T(8,128)(2,1)}, u32[]{:S(2)}, u32[]{:S(2)}) collective-permute-start(bf16[512,2048]{1,0:T(8,128)(2,1)} %multiply_convert_fusion.x0.l0), channel_id=1, source_target_pairs={{0,1},{1,0},{2,3},{3,2},{4,5},{5,4},{6,7},{7,6},{8,9},{9,8},{10,11... | collective-permute-start | bytes 6291464 | tf_op jit(solution)/shard_map/ppermute | solution.py:501
  109.0 44.7 %collective-permute-start.4 = (bf16[512,2048]{1,0:T(8,128)(2,1)S(1)}, bf16[512,2048]{1,0:T(8,128)(2,1)}, u32[]{:S(2)}, u32[]{:S(2)}) collective-permute-start(bf16[512,2048]{1,0:T(8,128)(2,1)S(1)} %bitcast_convert_fusion.g0), channel_id=1, source_target_pairs={{0,16},{16,0},{1,17},{17,1},{2,18},{18,2},{3,19},{19,3},{4,20},{20... | collective-permute-start | bytes 6291464 | tf_op jit(solution)/shard_map/ppermute | solution.py:498
  109.0 44.7 %collective-permute-start.3 = (bf16[512,2048]{1,0:T(8,128)(2,1)}, bf16[512,2048]{1,0:T(8,128)(2,1)}, u32[]{:S(2)}, u32[]{:S(2)}) collective-permute-start(bf16[512,2048]{1,0:T(8,128)(2,1)} %multiply_convert_fusion.x0.l0), channel_id=1, source_target_pairs={{0,16},{16,0},{1,17},{17,1},{2,18},{18,2},{3,19},{19,3},{4,20},{20... | collective-permute-start | bytes 6291464 | tf_op jit(solution)/shard_map/ppermute | solution.py:498
  109.5 73.3 %collective-permute-start.9 = (bf16[512,2048]{1,0:T(8,128)(2,1)}, bf16[512,2048]{1,0:T(8,128)(2,1)}, u32[]{:S(2)}, u32[]{:S(2)}) collective-permute-start(bf16[512,2048]{1,0:T(8,128)(2,1)} %collective-permute-done.8.g0.g2), channel_id=1, source_target_pairs={{0,16},{16,0},{1,17},{17,1},{2,18},{18,2},{3,19},{19,3},{4,20},{20... | collective-permute-start | bytes 6291464 | tf_op jit(solution)/shard_map/ppermute | solution.py:498
  153.1 29.7 %collective-permute-start.7 = (bf16[512,2048]{1,0:T(8,128)(2,1)}, bf16[512,2048]{1,0:T(8,128)(2,1)}, u32[]{:S(2)}, u32[]{:S(2)}) collective-permute-start(bf16[512,2048]{1,0:T(8,128)(2,1)} %collective-permute-done.6.x0.l2), channel_id=1, source_target_pairs={{0,16},{16,0},{1,17},{17,1},{2,18},{18,2},{3,19},{19,3},{4,20},{20... | collective-permute-start | bytes 6291464 | tf_op jit(solution)/shard_map/ppermute | solution.py:498
  232.9 103.5 %collective-permute-start.54 = (bf16[2,176,2048]{2,1,0:T(8,128)(2,1)}, bf16[2,176,2048]{2,1,0:T(8,128)(2,1)}, u32[]{:S(2)}, u32[]{:S(2)}) collective-permute-start(bf16[2,176,2048]{2,1,0:T(8,128)(2,1)} %dynamic-slice_bitcast_fusion.2), channel_id=1, source_target_pairs={{0,4},{4,8},{8,12},{12,0},{1,5},{5,9},{9,13},{13,1},{2,6},{6,10},{... | collective-permute-start | bytes 4325384 | tf_op jit(solution)/shard_map/ppermute | solution.py:469
  254.3 88.7 %collective-permute-start.48 = (bf16[8,128,1408]{2,1,0:T(8,128)(2,1)}, bf16[8,128,1408]{2,1,0:T(8,128)(2,1)}, u32[]{:S(2)}, u32[]{:S(2)}) collective-permute-start(bf16[8,128,1408]{2,1,0:T(8,128)(2,1)} %get-tuple-element.70), channel_id=1, source_target_pairs={{0,2},{1,3},{2,0},{3,1},{4,6},{5,7},{6,4},{7,5},{8,10},{9,11},{10,... | collective-permute-start | bytes 8650760 | tf_op jit(solution)/shard_map/ppermute | solution.py:504
  305.0 76.1 %collective-permute-start.42 = (bf16[8,128,1408]{2,1,0:T(8,128)(2,1)}, bf16[8,128,1408]{2,1,0:T(8,128)(2,1)}, u32[]{:S(2)}, u32[]{:S(2)}) collective-permute-start(bf16[8,128,1408]{2,1,0:T(8,128)(2,1)} %get-tuple-element.68), channel_id=1, source_target_pairs={{0,2},{1,3},{2,0},{3,1},{4,6},{5,7},{6,4},{7,5},{8,10},{9,11},{10,... | collective-permute-start | bytes 8650760 | tf_op jit(solution)/shard_map/ppermute | solution.py:504
  305.5 40.1 %collective-permute-start.10 = (bf16[512,2048]{1,0:T(8,128)(2,1)}, bf16[512,2048]{1,0:T(8,128)(2,1)}, u32[]{:S(2)}, u32[]{:S(2)}) collective-permute-start(bf16[512,2048]{1,0:T(8,128)(2,1)} %get-tuple-element.53), channel_id=1, source_target_pairs={{0,16},{16,0},{1,17},{17,1},{2,18},{18,2},{3,19},{19,3},{4,20},{20... | collective-permute-start | bytes 6291464 | tf_op jit(solution)/shard_map/ppermute | solution.py:498
  305.5 33.1 %collective-permute-start.13 = (bf16[512,2048]{1,0:T(8,128)(2,1)}, bf16[512,2048]{1,0:T(8,128)(2,1)}, u32[]{:S(2)}, u32[]{:S(2)}) collective-permute-start(bf16[512,2048]{1,0:T(8,128)(2,1)} %get-tuple-element.57), channel_id=1, source_target_pairs={{0,16},{16,0},{1,17},{17,1},{2,18},{18,2},{3,19},{19,3},{4,20},{20... | collective-permute-start | bytes 6291464 | tf_op jit(solution)/shard_map/ppermute | solution.py:498
  336.4 75.2 %collective-permute-start.12 = (bf16[512,2048]{1,0:T(8,128)(2,1)}, bf16[512,2048]{1,0:T(8,128)(2,1)S(1)}, u32[]{:S(2)}, u32[]{:S(2)}) collective-permute-start(bf16[512,2048]{1,0:T(8,128)(2,1)} %get-tuple-element.55), channel_id=1, source_target_pairs={{0,16},{16,0},{1,17},{17,1},{2,18},{18,2},{3,19},{19,3},{4,20},{20... | collective-permute-start | bytes 6291464 | tf_op jit(solution)/shard_map/ppermute | solution.py:498
  338.6 43.8 %collective-permute-start.55 = (bf16[2,176,2048]{2,1,0:T(8,128)(2,1)S(1)}, bf16[2,176,2048]{2,1,0:T(8,128)(2,1)S(1)}, u32[]{:S(2)}, u32[]{:S(2)}) collective-permute-start(bf16[2,176,2048]{2,1,0:T(8,128)(2,1)S(1)} %fusion.3), channel_id=1, source_target_pairs={{0,4},{4,8},{8,12},{12,0},{1,5},{5,9},{9,13},{13,1},{2,6},{6,10},{... | collective-permute-start | bytes 4325384 | tf_op jit(solution)/shard_map/ppermute | solution.py:469
  343.0 68.5 %collective-permute-start.14 = (bf16[512,2048]{1,0:T(8,128)(2,1)S(1)}, bf16[512,2048]{1,0:T(8,128)(2,1)S(1)}, u32[]{:S(2)}, u32[]{:S(2)}) collective-permute-start(bf16[512,2048]{1,0:T(8,128)(2,1)S(1)} %add_convert_fusion), channel_id=1, source_target_pairs={{0,1},{1,0},{2,3},{3,2},{4,5},{5,4},{6,7},{7,6},{8,9},{9,8},{10,11... | collective-permute-start | bytes 6291464 | tf_op jit(solution)/shard_map/ppermute | solution.py:501
  345.6 44.4 %collective-permute-start.49 = (bf16[2,2,64,1408]{3,2,1,0:T(8,128)(2,1)S(1)}, bf16[2,2,64,1408]{3,2,1,0:T(8,128)(2,1)S(1)}, u32[]{:S(2)}, u32[]{:S(2)}) collective-permute-start(bf16[2,2,64,1408]{3,2,1,0:T(8,128)(2,1)S(1)} %fusion.23), channel_id=1, source_target_pairs={{0,4},{4,8},{8,12},{12,0},{1,5},{5,9},{9,13},{13,1},{2,6},{6,10},{... | collective-permute-start | bytes 2162696 | tf_op jit(solution)/shard_map/ppermute | solution.py:469
  381.1 32.8 %collective-permute-start.5 = (bf16[512,2048]{1,0:T(8,128)(2,1)}, bf16[512,2048]{1,0:T(8,128)(2,1)S(1)}, u32[]{:S(2)}, u32[]{:S(2)}) collective-permute-start(bf16[512,2048]{1,0:T(8,128)(2,1)} %get-tuple-element.48), channel_id=1, source_target_pairs={{0,16},{16,0},{1,17},{17,1},{2,18},{18,2},{3,19},{19,3},{4,20},{20... | collective-permute-start | bytes 6291464 | tf_op jit(solution)/shard_map/ppermute | solution.py:498
  382.4 53.3 %collective-permute-start.11 = (bf16[512,2048]{1,0:T(8,128)(2,1)S(1)}, bf16[512,2048]{1,0:T(8,128)(2,1)}, u32[]{:S(2)}, u32[]{:S(2)}) collective-permute-start(bf16[512,2048]{1,0:T(8,128)(2,1)S(1)} %add_convert_fusion.1), channel_id=1, source_target_pairs={{0,1},{1,0},{2,3},{3,2},{4,5},{5,4},{6,7},{7,6},{8,9},{9,8},{10,11... | collective-permute-start | bytes 6291464 | tf_op jit(solution)/shard_map/ppermute | solution.py:501
  389.9 19.4 %collective-permute-start.43 = (bf16[2,2,64,1408]{3,2,1,0:T(8,128)(2,1)S(1)}, bf16[2,2,64,1408]{3,2,1,0:T(8,128)(2,1)S(1)}, u32[]{:S(2)}, u32[]{:S(2)}) collective-permute-start(bf16[2,2,64,1408]{3,2,1,0:T(8,128)(2,1)S(1)} %fusion.22), channel_id=1, source_target_pairs={{0,4},{4,8},{8,12},{12,0},{1,5},{5,9},{9,13},{13,1},{2,6},{6,10},{... | collective-permute-start | bytes 2162696 | tf_op jit(solution)/shard_map/ppermute | solution.py:469
  409.3 100.7 %collective-permute-start.56 = (bf16[2,176,2048]{2,1,0:T(8,128)(2,1)}, bf16[2,176,2048]{2,1,0:T(8,128)(2,1)}, u32[]{:S(2)}, u32[]{:S(2)}) collective-permute-start(bf16[2,176,2048]{2,1,0:T(8,128)(2,1)} %fusion.4), channel_id=1, source_target_pairs={{0,4},{4,8},{8,12},{12,0},{1,5},{5,9},{9,13},{13,1},{2,6},{6,10},{... | collective-permute-start | bytes 4325384 | tf_op jit(solution)/shard_map/ppermute | solution.py:469
  411.6 101.7 %collective-permute-start.50 = (bf16[2,2,64,1408]{3,2,1,0:T(8,128)(2,1)}, bf16[2,2,64,1408]{3,2,1,0:T(8,128)(2,1)}, u32[]{:S(2)}, u32[]{:S(2)}) collective-permute-start(bf16[2,2,64,1408]{3,2,1,0:T(8,128)(2,1)} %fusion.10), channel_id=1, source_target_pairs={{0,4},{4,8},{8,12},{12,0},{1,5},{5,9},{9,13},{13,1},{2,6},{6,10},{... | collective-permute-start | bytes 2162696 | tf_op jit(solution)/shard_map/ppermute | solution.py:469
  411.6 106.0 %collective-permute-start.44 = (bf16[2,2,64,1408]{3,2,1,0:T(8,128)(2,1)}, bf16[2,2,64,1408]{3,2,1,0:T(8,128)(2,1)}, u32[]{:S(2)}, u32[]{:S(2)}) collective-permute-start(bf16[2,2,64,1408]{3,2,1,0:T(8,128)(2,1)} %fusion.13), channel_id=1, source_target_pairs={{0,4},{4,8},{8,12},{12,0},{1,5},{5,9},{9,13},{13,1},{2,6},{6,10},{... | collective-permute-start | bytes 2162696 | tf_op jit(solution)/shard_map/ppermute | solution.py:469
  461.1 199.5 %collective-permute-start.36 = (bf16[4,2,2,64,2048]{4,3,2,1,0:T(8,128)(2,1)}, bf16[4,2,2,64,2048]{4,3,2,1,0:T(8,128)(2,1)}, u32[]{:S(2)}, u32[]{:S(2)}) collective-permute-start(bf16[4,2,2,64,2048]{4,3,2,1,0:T(8,128)(2,1)} %dynamic-slice_bitcast_fusion), channel_id=1, source_target_pairs={{0,16},{16,0},{1,17},{17,1},{2,18},{18,2},{3,19},{19,3},{4,20},{20... | collective-permute-start | bytes 12582920 | tf_op jit(solution)/shard_map/ppermute | solution.py:498
  472.9 47.8 %collective-permute-start.15 = (bf16[16,160,128]{2,1,0:T(8,128)(2,1)S(1)}, bf16[16,160,128]{2,1,0:T(8,128)(2,1)}, u32[]{:S(2)}, u32[]{:S(2)}) collective-permute-start(bf16[16,160,128]{2,1,0:T(8,128)(2,1)S(1)} %get-tuple-element.62), channel_id=1, source_target_pairs={{4,0},{8,4},{12,8},{5,1},{9,5},{13,9},{6,2},{10,6},{14,10},{7,3},{... | collective-permute-start | bytes 1966088 | tf_op jit(solution)/shard_map/ppermute | solution.py:548
  511.7 18.6 %collective-permute-start.57 = (bf16[176,2048]{1,0:T(8,128)(2,1)S(1)}, bf16[176,2048]{1,0:T(8,128)(2,1)S(1)}, u32[]{:S(2)}, u32[]{:S(2)}) collective-permute-start(bf16[176,2048]{1,0:T(8,128)(2,1)S(1)} %fusion.7), channel_id=1, source_target_pairs={{0,2},{1,3},{2,0},{3,1},{4,6},{5,7},{6,4},{7,5},{8,10},{9,11},{10,... | collective-permute-start | bytes 2162696 | tf_op jit(solution)/shard_map/ppermute | solution.py:504
  514.9 21.3 %collective-permute-start.51 = (bf16[2,2,64,1408]{3,2,1,0:T(8,128)(2,1)S(1)}, bf16[2,2,64,1408]{3,2,1,0:T(8,128)(2,1)S(1)}, u32[]{:S(2)}, u32[]{:S(2)}) collective-permute-start(bf16[2,2,64,1408]{3,2,1,0:T(8,128)(2,1)S(1)} %fusion.11), channel_id=1, source_target_pairs={{0,4},{4,8},{8,12},{12,0},{1,5},{5,9},{9,13},{13,1},{2,6},{6,10},{... | collective-permute-start | bytes 2162696 | tf_op jit(solution)/shard_map/ppermute | solution.py:469
  519.2 32.4 %collective-permute-start.45 = (bf16[2,2,64,1408]{3,2,1,0:T(8,128)(2,1)S(1)}, bf16[2,2,64,1408]{3,2,1,0:T(8,128)(2,1)S(1)}, u32[]{:S(2)}, u32[]{:S(2)}) collective-permute-start(bf16[2,2,64,1408]{3,2,1,0:T(8,128)(2,1)S(1)} %fusion.14), channel_id=1, source_target_pairs={{0,4},{4,8},{8,12},{12,0},{1,5},{5,9},{9,13},{13,1},{2,6},{6,10},{... | collective-permute-start | bytes 2162696 | tf_op jit(solution)/shard_map/ppermute | solution.py:469
  520.7 44.1 %collective-permute-start.16 = (bf16[16,160,128]{2,1,0:T(8,128)(2,1)}, bf16[16,160,128]{2,1,0:T(8,128)(2,1)S(1)}, u32[]{:S(2)}, u32[]{:S(2)}) collective-permute-start(bf16[16,160,128]{2,1,0:T(8,128)(2,1)} %collective-permute-done.15), channel_id=1, source_target_pairs={{4,0},{8,4},{12,8},{5,1},{9,5},{13,9},{6,2},{10,6},{14,10},{7,3},{... | collective-permute-start | bytes 1966088 | tf_op jit(solution)/shard_map/ppermute | solution.py:548
  532.0 108.1 %collective-permute-start.58 = (bf16[176,2048]{1,0:T(8,128)(2,1)S(1)}, bf16[176,2048]{1,0:T(8,128)(2,1)S(1)}, u32[]{:S(2)}, u32[]{:S(2)}) collective-permute-start(bf16[176,2048]{1,0:T(8,128)(2,1)S(1)} %fusion.9), channel_id=1, source_target_pairs={{1,8},{3,10},{5,12},{7,14},{8,1},{10,3},{12,5},{14,7},{17,24},{19,... | collective-permute-start | bytes 2162696 | tf_op jit(solution)/shard_map/ppermute | solution.py:660
  537.6 16.6 %collective-permute-start.52 = (bf16[2,64,1408]{2,1,0:T(8,128)(2,1)S(1)}, bf16[2,64,1408]{2,1,0:T(8,128)(2,1)S(1)}, u32[]{:S(2)}, u32[]{:S(2)}) collective-permute-start(bf16[2,64,1408]{2,1,0:T(8,128)(2,1)S(1)} %get-tuple-element.84), channel_id=1, source_target_pairs={{0,1},{1,0},{2,3},{3,2},{4,5},{5,4},{6,7},{7,6},{8,9},{9,8},{10,11... | collective-permute-start | bytes 1081352 | tf_op jit(solution)/shard_map/ppermute | solution.py:501
  553.0 9.1 %collective-permute-start.46 = (bf16[2,64,1408]{2,1,0:T(8,128)(2,1)S(1)}, bf16[2,64,1408]{2,1,0:T(8,128)(2,1)S(1)}, u32[]{:S(2)}, u32[]{:S(2)}) collective-permute-start(bf16[2,64,1408]{2,1,0:T(8,128)(2,1)S(1)} %get-tuple-element.88), channel_id=1, source_target_pairs={{0,1},{1,0},{2,3},{3,2},{4,5},{5,4},{6,7},{7,6},{8,9},{9,8},{10,11... | collective-permute-start | bytes 1081352 | tf_op jit(solution)/shard_map/ppermute | solution.py:501
  554.4 12.1 %collective-permute-start.53 = (bf16[64,2816]{1,0:T(8,128)(2,1)S(1)}, bf16[64,2816]{1,0:T(8,128)(2,1)S(1)}, u32[]{:S(2)}, u32[]{:S(2)}) collective-permute-start(bf16[64,2816]{1,0:T(8,128)(2,1)S(1)} %get-tuple-element.82), channel_id=1, source_target_pairs={{0,16},{16,0},{1,17},{17,1},{2,18},{18,2},{3,19},{19,3},{4,20},{20... | collective-permute-start | bytes 1081352 | tf_op jit(solution)/shard_map/ppermute | solution.py:498
  562.3 5.5 collective-permute-start.47
  564.8 44.9 %collective-permute-start.17 = (bf16[16,160,128]{2,1,0:T(8,128)(2,1)S(1)}, bf16[16,160,128]{2,1,0:T(8,128)(2,1)S(1)}, u32[]{:S(2)}, u32[]{:S(2)}) collective-permute-start(bf16[16,160,128]{2,1,0:T(8,128)(2,1)S(1)} %collective-permute-done.16), channel_id=1, source_target_pairs={{4,0},{8,4},{12,8},{5,1},{9,5},{13,9},{6,2},{10,6},{14,10},{7,3},{... | collective-permute-start | bytes 1966088 | tf_op jit(solution)/shard_map/ppermute | solution.py:548
  566.5 46.5 %copy-start.25 = (f32[512,2048]{1,0:T(8,128)S(1)}, f32[512,2048]{1,0:T(8,128)}, u32[]{:S(2)}) copy-start(f32[512,2048]{1,0:T(8,128)} %copy-done.24) | copy-start | bytes 12582916
  640.0 28.8 %collective-permute-start.30 = (bf16[4,2,2,64,2048]{4,3,2,1,0:T(8,128)(2,1)}, bf16[4,2,2,64,2048]{4,3,2,1,0:T(8,128)(2,1)}, u32[]{:S(2)}, u32[]{:S(2)}) collective-permute-start(bf16[4,2,2,64,2048]{4,3,2,1,0:T(8,128)(2,1)} %dynamic-slice_bitcast_fusion.1), channel_id=1, source_target_pairs={{0,16},{16,0},{1,17},{17,1},{2,18},{18,2},{3,19},{19,3},{4,20},{20... | collective-permute-start | bytes 12582920 | tf_op jit(solution)/shard_map/ppermute | solution.py:498
  644.5 22.3 %collective-permute-start.24 = (bf16[4,2,2,64,512]{4,3,2,1,0:T(8,128)(2,1)}, bf16[4,2,2,64,512]{4,3,2,1,0:T(8,128)(2,1)}, u32[]{:S(2)}, u32[]{:S(2)}) collective-permute-start(bf16[4,2,2,64,512]{4,3,2,1,0:T(8,128)(2,1)} %dynamic-slice_bitcast_fusion.3), channel_id=1, source_target_pairs={{0,16},{16,0},{1,17},{17,1},{2,18},{18,2},{3,19},{19,3},{4,20},{20... | collective-permute-start | bytes 3145736 | tf_op jit(solution)/shard_map/ppermute | solution.py:498
  655.5 1.3 collective-permute-start.18
  656.9 3.6 collective-permute-start.19
  660.6 5.3 collective-permute-start.20
  663.9 68.9 %collective-permute-start.37 = (bf16[4,2,64,2048]{3,2,1,0:T(8,128)(2,1)S(1)}, bf16[4,2,64,2048]{3,2,1,0:T(8,128)(2,1)S(1)}, u32[]{:S(2)}, u32[]{:S(2)}) collective-permute-start(bf16[4,2,64,2048]{3,2,1,0:T(8,128)(2,1)S(1)} %fusion), channel_id=1, source_target_pairs={{0,1},{1,0},{2,3},{3,2},{4,5},{5,4},{6,7},{7,6},{8,9},{9,8},{10,11... | collective-permute-start | bytes 6291464 | tf_op jit(solution)/shard_map/ppermute | solution.py:501
  666.0 11.0 %collective-permute-start.21 = (f32[128]{0:T(128)S(1)}, f32[128]{0:T(128)S(1)}, u32[]{:S(2)}, u32[]{:S(2)}) collective-permute-start(f32[128]{0:T(128)S(1)} %fusion.91), channel_id=1, source_target_pairs={{0,4},{4,8},{8,12},{12,0},{1,5},{5,9},{9,13},{13,1},{2,6},{6,10},{... | collective-permute-start | bytes 1544 | tf_op jit(solution)/shard_map/ppermute | solution.py:469
  668.8 55.1 %collective-permute-start.25 = (bf16[4,2,64,512]{3,2,1,0:T(8,128)(2,1)}, bf16[4,2,64,512]{3,2,1,0:T(8,128)(2,1)}, u32[]{:S(2)}, u32[]{:S(2)}) collective-permute-start(bf16[4,2,64,512]{3,2,1,0:T(8,128)(2,1)} %fusion.16), channel_id=1, source_target_pairs={{0,1},{1,0},{2,3},{3,2},{4,5},{5,4},{6,7},{7,6},{8,9},{9,8},{10,11... | collective-permute-start | bytes 1572872 | tf_op jit(solution)/shard_map/ppermute | solution.py:501
  672.0 95.0 %collective-permute-start.31 = (bf16[4,2,64,2048]{3,2,1,0:T(8,128)(2,1)S(1)}, bf16[4,2,64,2048]{3,2,1,0:T(8,128)(2,1)}, u32[]{:S(2)}, u32[]{:S(2)}) collective-permute-start(bf16[4,2,64,2048]{3,2,1,0:T(8,128)(2,1)S(1)} %fusion.1), channel_id=1, source_target_pairs={{0,1},{1,0},{2,3},{3,2},{4,5},{5,4},{6,7},{7,6},{8,9},{9,8},{10,11... | collective-permute-start | bytes 6291464 | tf_op jit(solution)/shard_map/ppermute | solution.py:501
  677.1 48.5 %collective-permute-start.22 = (f32[128]{0:T(128)S(1)}, f32[128]{0:T(128)S(1)}, u32[]{:S(2)}, u32[]{:S(2)}) collective-permute-start(f32[128]{0:T(128)S(1)} %fusion.83), channel_id=1, source_target_pairs={{0,4},{4,8},{8,12},{12,0},{1,5},{5,9},{9,13},{13,1},{2,6},{6,10},{... | collective-permute-start | bytes 1544 | tf_op jit(solution)/shard_map/ppermute | solution.py:469
  724.8 6.8 collective-permute-start.26
  725.6 44.3 %collective-permute-start.23 = (f32[128]{0:T(128)S(1)}, f32[128]{0:T(128)S(1)}, u32[]{:S(2)}, u32[]{:S(2)}) collective-permute-start(f32[128]{0:T(128)S(1)} %fusion.74), channel_id=1, source_target_pairs={{0,4},{4,8},{8,12},{12,0},{1,5},{5,9},{9,13},{13,1},{2,6},{6,10},{... | collective-permute-start | bytes 1544 | tf_op jit(solution)/shard_map/ppermute | solution.py:469
  732.7 7.2 collective-permute-start.27
  734.9 60.2 %collective-permute-start.38 = (bf16[4,64,2048]{2,1,0:T(8,128)(2,1)S(1)}, bf16[4,64,2048]{2,1,0:T(8,128)(2,1)S(1)}, u32[]{:S(2)}, u32[]{:S(2)}) collective-permute-start(bf16[4,64,2048]{2,1,0:T(8,128)(2,1)S(1)} %fusion.5), channel_id=1, source_target_pairs={{0,2},{1,3},{2,0},{3,1},{4,6},{5,7},{6,4},{7,5},{8,10},{9,11},{10,... | collective-permute-start | bytes 3145736 | tf_op jit(solution)/shard_map/ppermute | solution.py:504
  740.9 29.1 %collective-permute-start.28 = (bf16[2,64,512]{2,1,0:T(8,128)(2,1)S(1)}, bf16[2,64,512]{2,1,0:T(8,128)(2,1)S(1)}, u32[]{:S(2)}, u32[]{:S(2)}) collective-permute-start(bf16[2,64,512]{2,1,0:T(8,128)(2,1)S(1)} %fusion.45), channel_id=1, source_target_pairs={{0,4},{4,8},{8,12},{12,0},{1,5},{5,9},{9,13},{13,1},{2,6},{6,10},{... | collective-permute-start | bytes 393224 | tf_op jit(solution)/shard_map/ppermute | solution.py:469
  769.3 28.3 %collective-permute-start.32 = (bf16[4,64,2048]{2,1,0:T(8,128)(2,1)S(1)}, bf16[4,64,2048]{2,1,0:T(8,128)(2,1)S(1)}, u32[]{:S(2)}, u32[]{:S(2)}) collective-permute-start(bf16[4,64,2048]{2,1,0:T(8,128)(2,1)S(1)} %fusion.6), channel_id=1, source_target_pairs={{0,2},{1,3},{2,0},{3,1},{4,6},{5,7},{6,4},{7,5},{8,10},{9,11},{10,... | collective-permute-start | bytes 3145736 | tf_op jit(solution)/shard_map/ppermute | solution.py:504
  770.9 23.2 %collective-permute-start.29 = (bf16[64,512]{1,0:T(8,128)(2,1)S(1)}, bf16[64,512]{1,0:T(8,128)(2,1)S(1)}, u32[]{:S(2)}, u32[]{:S(2)}) collective-permute-start(bf16[64,512]{1,0:T(8,128)(2,1)S(1)} %fusion.46), channel_id=1, source_target_pairs={{0,2},{1,3},{2,0},{3,1},{4,6},{5,7},{6,4},{7,5},{8,10},{9,11},{10,... | collective-permute-start | bytes 196616 | tf_op jit(solution)/shard_map/ppermute | solution.py:504
  796.2 10.3 %collective-permute-start.39 = (bf16[64,2048]{1,0:T(8,128)(2,1)S(1)}, bf16[64,2048]{1,0:T(8,128)(2,1)S(1)}, u32[]{:S(2)}, u32[]{:S(2)}) collective-permute-start(bf16[64,2048]{1,0:T(8,128)(2,1)S(1)} %fusion.29), channel_id=1, source_target_pairs={{0,4},{4,8},{8,12},{12,0},{1,5},{5,9},{9,13},{13,1},{2,6},{6,10},{... | collective-permute-start | bytes 786440 | tf_op jit(solution)/shard_map/ppermute | solution.py:469
  798.8 13.3 %collective-permute-start.33 = (bf16[64,2048]{1,0:T(8,128)(2,1)S(1)}, bf16[64,2048]{1,0:T(8,128)(2,1)S(1)}, u32[]{:S(2)}, u32[]{:S(2)}) collective-permute-start(bf16[64,2048]{1,0:T(8,128)(2,1)S(1)} %fusion.35), channel_id=1, source_target_pairs={{0,4},{4,8},{8,12},{12,0},{1,5},{5,9},{9,13},{13,1},{2,6},{6,10},{... | collective-permute-start | bytes 786440 | tf_op jit(solution)/shard_map/ppermute | solution.py:469
  807.7 9.9 %collective-permute-start.40 = (bf16[64,2048]{1,0:T(8,128)(2,1)S(1)}, bf16[64,2048]{1,0:T(8,128)(2,1)S(1)}, u32[]{:S(2)}, u32[]{:S(2)}) collective-permute-start(bf16[64,2048]{1,0:T(8,128)(2,1)S(1)} %fusion.31), channel_id=1, source_target_pairs={{0,4},{4,8},{8,12},{12,0},{1,5},{5,9},{9,13},{13,1},{2,6},{6,10},{... | collective-permute-start | bytes 786440 | tf_op jit(solution)/shard_map/ppermute | solution.py:469
  813.4 10.9 %collective-permute-start.34 = (bf16[64,2048]{1,0:T(8,128)(2,1)S(1)}, bf16[64,2048]{1,0:T(8,128)(2,1)S(1)}, u32[]{:S(2)}, u32[]{:S(2)}) collective-permute-start(bf16[64,2048]{1,0:T(8,128)(2,1)S(1)} %fusion.37), channel_id=1, source_target_pairs={{0,4},{4,8},{8,12},{12,0},{1,5},{5,9},{9,13},{13,1},{2,6},{6,10},{... | collective-permute-start | bytes 786440 | tf_op jit(solution)/shard_map/ppermute | solution.py:469
  818.9 10.1 %collective-permute-start.41 = (bf16[64,2048]{1,0:T(8,128)(2,1)S(1)}, bf16[64,2048]{1,0:T(8,128)(2,1)S(1)}, u32[]{:S(2)}, u32[]{:S(2)}) collective-permute-start(bf16[64,2048]{1,0:T(8,128)(2,1)S(1)} %fusion.33), channel_id=1, source_target_pairs={{0,4},{4,8},{8,12},{12,0},{1,5},{5,9},{9,13},{13,1},{2,6},{6,10},{... | collective-permute-start | bytes 786440 | tf_op jit(solution)/shard_map/ppermute | solution.py:469
  825.6 8.2 collective-permute-start.35
  (52 other events, 692.2 us)

commit v2 on v1

v2 whole, which is shorter than its diff:
```python
import functools

import jax
import jax.numpy as jnp
import ml_dtypes
import numpy as np
from jax import lax
from jax.experimental import pallas as pl
from jax.experimental.pallas import tpu as pltpu
from jax.sharding import PartitionSpec as P

HEADS = 16
FDIM = 16
VHEAD = 128
EPS = 1e-06

bf16 = jnp.bfloat16
f32 = jnp.float32

PAIRS = [(a, b) for a in range(FDIM + 1) for b in range(a, FDIM + 1)]
NPAIR = len(PAIRS)
PADF = 256
STATE_ROWS = 160
VMEM_MIB = 30
bf16 = jnp.bfloat16
f32 = jnp.float32

PAIRS = [(a, b) for a in range(FDIM + 1) for b in range(a, FDIM + 1)]
NPAIR = len(PAIRS)
PADF = 256
STATE_ROWS = 160
VMEM_MIB = 30
SCALE = 20

NN = (((1,), (0,)), ((), ()))
NT = (((1,), (1,)), ((), ()))
TN = (((0,), (0,)), ((), ()))


def mm(a, b, dims=NN):
    return lax.dot_general(a, b, dims, preferred_element_type=f32)


def feature_tables():
    level = np.zeros((8, PADF), np.float32)
    for f, (a, b) in enumerate(PAIRS):
        level[0, f] = float(a == FDIM)
        level[1, f] = float(b == FDIM)
        if a == FDIM:
            level[2, f] = 1.0
        elif b == FDIM:
            level[2, f] = FDIM**-0.5
        elif a == b:
            level[2, f] = 1.0 / (2 * FDIM)
        else:
            level[2, f] = 1.0 / FDIM
    pick = np.zeros((2, HEADS, HEADS * FDIM, PADF), np.float32)
    for head in range(HEADS):
        for f, pair in enumerate(PAIRS):
            for k, entry in enumerate(pair):
                if entry < FDIM:
                    pick[k, head, head * FDIM + entry, f] = 1.0
    pick = pick.astype(ml_dtypes.bfloat16)
    return jnp.asarray(pick[0]), jnp.asarray(pick[1]), jnp.asarray(level)


FREE = pl.CostEstimate(flops=0, bytes_accessed=0, transcendentals=0)


def params(mib):
    return pltpu.CompilerParams(vmem_limit_bytes=mib << 20)


def factors(packed, pick_a, pick_b, level):
    return mm(packed, pick_a[0]) + level[0:1, :], mm(packed, pick_b[0]) + level[1:2, :]


def wide(value, times):
    return jnp.concatenate([value] * times, axis=1)


def parts(value):
    high = value.astype(bf16)
    return high, (value - high.astype(f32)).astype(bf16)


def own_lanes(head, packed):
    lane = lax.broadcasted_iota(jnp.int32, packed.shape, 1)
    return jnp.where(lane // FDIM == head, packed, jnp.zeros_like(packed))


def pack_state(state, sums):
    block = state[:STATE_ROWS]
    high = sums.astype(bf16).astype(f32)
    low = sums - high
    row = lax.broadcasted_iota(jnp.int32, block.shape, 0)
    for k, part in enumerate((high[:, :128], high[:, 128:], low[:, :128], low[:, 128:])):
        block = jnp.where(row == NPAIR + k, part, block)
    return block.astype(bf16)


def unpack_state(block):
    row = lax.broadcasted_iota(jnp.int32, block.shape, 0)

    def line(k):
        return jnp.sum(jnp.where(row == NPAIR + k, block, 0.0), axis=0, keepdims=True)

    sums = jnp.concatenate([line(0) + line(2), line(1) + line(3)], axis=1)
    state = jnp.where(row < NPAIR, block, 0.0).astype(bf16)
    pad = jnp.zeros((PADF - STATE_ROWS, VHEAD), bf16)
    return jnp.concatenate([state, pad], axis=0), sums


def sum_against(feats, sums):
    return sum(mm(feats, p, NT) for p in parts(jnp.broadcast_to(sums, (128, PADF))))


def column(ref, head):
    row = lax.broadcasted_iota(jnp.int32, (128, 128), 0)
    pick = jnp.where(row == head, 1.0, 0.0).astype(bf16)
    return sum(mm(p, pick) for p in parts(ref[...]))


def row_sum(value):
    ones = jnp.ones((128, 128), bf16)
    return sum(mm(p, ones) for p in parts(value))


def set_column(ref, head, value):
    lane = lax.broadcasted_iota(jnp.int32, ref.shape, 1)

    @pl.when(head == 0)
    def _():
        ref[...] = jnp.zeros_like(ref)

    ref[...] = jnp.where(lane == head, value, ref[...])


def key_state_kernel(head, pick_a, pick_b, level, k_ref, v_ref, end_ref, out_ref):
    one, two = factors(k_ref[...], pick_a, pick_b, level)
    feats = (one * two * wide(end_ref[...], 2)).astype(bf16)
    state = mm(feats, v_ref[...], TN)
    sums = jnp.sum(feats.astype(f32), axis=0, keepdims=True)
    out_ref[0] = pack_state(state, sums)


def intra_kernel(head, pick_a, pick_b, level, q_ref, k_ref, v_ref, mask_ref, num_ref, den_ref, feat_ref):
    queries = q_ref[...]
    scores = mm(own_lanes(head, queries), k_ref[...], NT)
    lin = scores * 0.25 + 1.0
    weights = ((lin * lin * 0.5 + 0.5) * mask_ref[...]).astype(bf16)
    values = v_ref[...]
    both = mm(weights, jnp.concatenate([values, jnp.ones_like(values)], axis=1))
    num_ref[...] = both[:, :VHEAD]
    set_column(den_ref, head, both[:, VHEAD:])
    one, two = factors(queries, pick_a, pick_b, level)
    feat_ref[0] = (one * two * level[2:3, :]).astype(bf16)


def kept_state(kept_ref, state_refs):
    block = jnp.zeros(state_refs[0].shape[1:], f32)
    for k, ref in enumerate(state_refs):
        block = block + kept_ref[k] * ref[0].astype(f32)
    return block


def combine_kernel(head, kept_ref, feat_ref, num_ref, den_ref, from_ref, *refs):
    *state_refs, mixed_ref, total_ref, block_ref = refs
    feats = feat_ref[0]
    block = kept_state(kept_ref, state_refs)
    block_ref[0] = block
    state, sums = unpack_state(block)
    reach = from_ref[...]
    den = column(den_ref, head) + reach * sum_against(feats, sums)
    mixed_ref[...] = ((num_ref[...] + reach * mm(feats, state)) * (1.0 / den)).astype(bf16)
    set_column(total_ref, head, den)


def query_state_kernel(
    head, feat_ref, grad_ref, mixed_ref, den_ref, from_ref, out_ref, gnum_ref, gden_ref
):
    feats = feat_ref[0]
    gnum = (grad_ref[...] * (1.0 / column(den_ref, head))).astype(bf16)
    far = gnum.astype(f32)
    gden = -row_sum(far * mixed_ref[...].astype(f32))
    reach = from_ref[...]
    state = mm(feats, (far * reach).astype(bf16), TN)
    sums = jnp.sum(feats.astype(f32) * wide(gden * reach, 2), axis=0, keepdims=True)
    out_ref[0] = pack_state(state, sums)
    gnum_ref[...] = gnum
    set_column(gden_ref, head, gden)


def back_kernel(
    first,
    head,
    pick_a,
    pick_b,
    level,
    q_ref,
    k_ref,
    v_ref,
    mask_ref,
    gnum_ref,
    gden_ref,
    state_ref,
    from_ref,
    gq_in,
    gk_in,
    gv_in,
    gq_ref,
    gk_ref,
    gv_ref,
):
    queries, keys, values = q_ref[...], k_ref[...], v_ref[...]
    gnum = gnum_ref[...]
    gden = column(gden_ref, head)
    q_own, k_own = own_lanes(head, queries), own_lanes(head, keys)
    scores = mm(q_own, keys, NT)
    lin = scores * 0.25 + 1.0
    mask = mask_ref[...]
    weights = ((lin * lin * 0.5 + 0.5) * mask).astype(bf16)
    spread = wide(gden, keys.shape[0] // 128)
    slopes = ((mm(gnum, values, NT) + spread) * (mask * lin * 0.25)).astype(bf16)
    gv_ref[...] = mm(weights, gnum, TN)
    grad_q = mm(slopes, k_own)
    grad_k = mm(slopes, q_own, TN)

    one, two = factors(queries, pick_a, pick_b, level)
    state, sums = unpack_state(state_ref[0])
    reach = from_ref[...]
    gfeat = (mm(gnum, state, NT) + wide(gden, 2) * sums) * wide(reach, 2) * level[2:3, :]
    grad_q += mm((gfeat * two).astype(bf16), pick_a[0], NT)
    grad_q += mm((gfeat * one).astype(bf16), pick_b[0], NT)

    @pl.when(head == first)
    def _():
        if first == 0:
            gq_ref[...] = jnp.zeros_like(gq_ref)
            gk_ref[...] = jnp.zeros_like(gk_ref)
        else:
            gq_ref[...] = gq_in[...]
            gk_ref[...] = gk_in[...]

    gq_ref[...] += grad_q
    gk_ref[...] += grad_k


def back_state_kernel(
    head, kept_ref, pick_a, pick_b, level, k_ref, v_ref, end_ref, gk_in, gv_in, *refs
):
    *state_refs, gk_ref, gv_ref, gk_sum = refs
    values = v_ref[...]
    one, two = factors(k_ref[...], pick_a, pick_b, level)
    state, sums = unpack_state(kept_state(kept_ref, state_refs))
    reach = wide(end_ref[...], 2)
    feats = (one * two * reach).astype(bf16)
    gv_ref[...] = (gv_in[...] + mm(feats, state)).astype(bf16)
    gfeat = (mm(values, state, NT) + sums) * reach
    grad_k = mm((gfeat * two).astype(bf16), pick_a[0], NT)
    grad_k += mm((gfeat * one).astype(bf16), pick_b[0], NT)

    @pl.when(head == 0)
    def _():
        gk_sum[...] = gk_in[...]

    gk_sum[...] += grad_k

    @pl.when(head == HEADS - 1)
    def _():
        gk_ref[...] = gk_sum[...].astype(bf16)


def head_call(kernel, ins, outs, heads=(0, HEADS), scratch=(), aliases=None):
    first, last = heads

    def spec(kind, shape):
        if kind == "all":
            return pl.BlockSpec(shape, lambda h: (0,) * len(shape))
        if kind == "head":
            return pl.BlockSpec((shape[0], VHEAD), lambda h: (0, h + first))
        if kind == "state":
            return pl.BlockSpec((1, *shape[1:]), lambda h: (h + first, 0, 0))
        if kind == "smem":
            return pl.BlockSpec(memory_space=pltpu.SMEM)
        return pl.BlockSpec(memory_space=pl.ANY)

    def body(*refs):
        kernel(pl.program_id(0) + first, *refs)

    return pl.pallas_call(
        body,
        grid=(last - first,),
        in_specs=[spec(kind, a.shape) for kind, a in ins],
        out_specs=[spec(kind, shape) for kind, shape, _ in outs],
        out_shape=[sds(shape, dtype) for _, shape, dtype in outs],
        scratch_shapes=list(scratch),
        input_output_aliases=aliases or {},
        compiler_params=params(20),
        cost_estimate=FREE,
    )(*(a for _, a in ins))


def sds(shape, dtype):
    return jax.ShapeDtypeStruct(shape, dtype)


def hidden_grad_kernel(half, which_ref, g0, g1, wd, out):
    branch = jnp.where(pl.program_id(0) < half, g0[...], g1[...])
    out[...] = mm(branch, wd[...], NT).astype(bf16)


def act_kernel(half, which_ref, x0, x1, grad_ref, wg, wu, hid, gg, gu):
    tokens = jnp.where(pl.program_id(0) < half, x0[...], x1[...])
    gate = mm(tokens, wg[...])
    up = mm(tokens, wu[...])
    grad = grad_ref[...].astype(f32)
    sig = 1.0 / (1.0 + jnp.exp(-gate))
    silu = gate * sig
    hid[...] = (silu * up).astype(bf16)
    gg[...] = (grad * up * (sig * (1.0 + gate * (1.0 - sig)))).astype(bf16)
    gu[...] = (grad * silu).astype(bf16)


def put(half, value, low, pieces):
    step = pl.program_id(0)

    @pl.when(step < half)
    def _():
        low[...] = value

    for k, piece in enumerate(pieces):
        here = step == half + k if len(pieces) > 1 else step >= half

        @pl.when(here)
        def _(piece=piece):
            piece[...] = value


def low_grad_kernel(half, which_ref, gg, gu, wg, wu, low, *pieces):
    value = (mm(gg[...], wg[...], NT) + mm(gu[...], wu[...], NT)).astype(bf16)
    put(half, value, low, pieces)


def layer_kernel(half, which_ref, hid, wd, low, *pieces):
    put(half, mm(hid[...], wd[...]).astype(bf16), low, pieces)


def token_call(kernel, which, count, ins, outs, width, slice_ff):
    tile = min(256, count)
    half = count // tile
    once = pl.Buffered(1)
    low = pl.BlockSpec((tile, width), lambda i, w: (jnp.minimum(i, half - 1), 0))
    high = pl.BlockSpec((tile, width), lambda i, w: (jnp.maximum(i - half, 0), 0))
    row = pl.BlockSpec((tile, slice_ff), lambda i, w: (i, 0))
    specs, operands = [], []
    for kind, *arrays in ins:
        operands += arrays
        specs += {
            "pair": [low, high],
            "row": [row],
            "wide": [pl.BlockSpec((width, slice_ff), lambda i, w: (0, w[0]), pipeline_mode=once)],
            "tall": [pl.BlockSpec((slice_ff, width), lambda i, w: (w[0], 0), pipeline_mode=once)],
        }[kind]
    out_specs, out_shapes = [], []
    for kind in outs:
        if kind == "row":
            out_specs.append(row)
            out_shapes.append(sds((2 * count, slice_ff), bf16))
        elif kind == "two":
            out_specs += [low, high]
            out_shapes += [sds((count, width), bf16)] * 2
        else:
            piece = pl.BlockSpec((tile, width), lambda i, w: (0, 0))
            out_specs += [low] + [piece] * half
            out_shapes += [sds((count, width), bf16)] + [sds((tile, width), bf16)] * half
    return pl.pallas_call(
        functools.partial(kernel, half),
        grid_spec=pltpu.PrefetchScalarGridSpec(
            num_scalar_prefetch=1,
            grid=(2 * half,),
            in_specs=specs,
            out_specs=out_specs,
        ),
        out_shape=out_shapes,
        compiler_params=params(VMEM_MIB),
        cost_estimate=FREE,
    )(which, *operands)


def split_rows(total, high, send, keep):
    groups = send.shape[0]
    rows = total.shape[0] // groups
    for g in range(groups):
        a = total[g * rows : g * rows + rows // 2]
        b = total[g * rows + rows // 2 : (g + 1) * rows]
        send[g] = jnp.where(high, a, b).astype(bf16)
        keep[g] = jnp.where(high, b, a).astype(bf16)


def wide_grad_kernel(ybit_ref, l0, l1, l2, l3, near, far, send, keep):
    count = l0.shape[0]
    total = mm(l0[...], near[:count, :], TN)
    total += mm(l1[...], near[count:, :], TN)
    total += mm(l2[...], far[:count, :], TN)
    total += mm(l3[...], far[count:, :], TN)
    split_rows(total, ybit_ref[0] == 1, send, keep)


def wide_grad(ybit, lows, near, far, group_rows):
    count, width = lows[0].shape
    cols = near.shape[1]
    tile = min(256, width)
    groups = tile // group_rows
    lane = pl.BlockSpec((count, tile), lambda i, w: (0, i))
    held = pl.BlockSpec((2 * count, cols), lambda i, w: (0, 0), pipeline_mode=pl.Buffered(1))
    out = pl.BlockSpec((groups, group_rows // 2, cols), lambda i, w: (i, 0, 0))
    shape = sds((width // group_rows, group_rows // 2, cols), bf16)
    return pl.pallas_call(
        wide_grad_kernel,
        grid_spec=pltpu.PrefetchScalarGridSpec(
            num_scalar_prefetch=1,
            grid=(width // tile,),
            in_specs=[lane, lane, lane, lane, held, held],
            out_specs=[out, out],
        ),
        out_shape=[shape, shape],
        compiler_params=params(VMEM_MIB),
        cost_estimate=FREE,
    )(ybit, *lows, near, far)


def down_grad_kernel(ybit_ref, near, far, g0, g1, g2, g3, send, keep):
    count = g0.shape[0]
    total = mm(near[:count, :], g0[...], TN)
    total += mm(near[count:, :], g1[...], TN)
    total += mm(far[:count, :], g2[...], TN)
    total += mm(far[count:, :], g3[...], TN)
    split_rows(total, ybit_ref[0] == 1, send, keep)


def down_grad(ybit, near, far, grads, group_rows):
    count, width = grads[0].shape
    rows = near.shape[1]
    tile = min(256, width)
    lane = pl.BlockSpec((count, tile), lambda i, w: (0, i))
    held = pl.BlockSpec((2 * count, rows), lambda i, w: (0, 0), pipeline_mode=pl.Buffered(1))
    out = pl.BlockSpec((rows // group_rows, group_rows // 2, tile), lambda i, w: (0, 0, i))
    shape = sds((rows // group_rows, group_rows // 2, width), bf16)
    return pl.pallas_call(
        down_grad_kernel,
        grid_spec=pltpu.PrefetchScalarGridSpec(
            num_scalar_prefetch=1,
            grid=(width // tile,),
            in_specs=[held, held, lane, lane, lane, lane],
            out_specs=[out, out],
        ),
        out_shape=[shape, shape],
        compiler_params=params(VMEM_MIB),
        cost_estimate=FREE,
    )(ybit, near, far, *grads)


def norm_back_kernel(low, near, far, middle, seed, gain, w, grad_ref, low_ref, mixed_ref, gain_ref, *copies):
    grad = low[...].astype(f32) + near[...].astype(f32) + far[...].astype(f32)
    value = middle[...]
    root = lax.rsqrt(jnp.mean(value * value, axis=-1, keepdims=True) + EPS)
    unit = value * root

    @pl.when(pl.program_id(0) == 0)
    def _():
        gain_ref[...] = jnp.zeros_like(gain_ref)

    gain_ref[...] += jnp.broadcast_to(jnp.sum(grad * unit, axis=0, keepdims=True), gain_ref.shape)
    scaled = grad * gain[...]
    total = seed[...] + root * (scaled - unit * jnp.mean(scaled * unit, axis=-1, keepdims=True))
    grad_ref[...] = total
    narrow = total.astype(bf16)
    low_ref[...] = narrow
    for k, copy in enumerate(copies):

        @pl.when(pl.program_id(0) // 2 == k)
        def _(copy=copy):
            copy[...] = narrow

    mixed_ref[...] = mm(narrow, w[...], NT)


def norm_back(low, near, far, middle, seed, gain, w):
    count, width = middle.shape
    tile = min(128, count // 2)
    halves = count // (2 * tile)
    row = pl.BlockSpec((tile, width), lambda i: (i, 0))

    def held(shape):
        return pl.BlockSpec(shape, lambda i: (0, 0), pipeline_mode=pl.Buffered(1))

    return pl.pallas_call(
        norm_back_kernel,
        grid=(count // tile,),
        in_specs=[row] * 5 + [held((1, width)), held(w.shape)],
        out_specs=[row] * 3
        + [pl.BlockSpec((8, width), lambda i: (0, 0))]
        + [
            pl.BlockSpec((tile, width), lambda i, k=k: (jnp.clip(i - 2 * k, 0, 1), 0))
            for k in range(halves)
        ],
        out_shape=[
            sds((count, width), f32),
            sds((count, width), bf16),
            sds((count, width), f32),
            sds((8, width), f32),
            *[sds((2 * tile, width), bf16)] * halves,
        ],
        compiler_params=params(VMEM_MIB),
        cost_estimate=FREE,
    )(low, near, far, middle, seed, gain.reshape(1, width), w)


def core_grad_kernel(along_x, bits_ref, r0, r1, c0, *refs):
    *others, send, keep = refs
    total = mm(r0[...], c0[...], TN)
    first = 0
    for c1 in others:
        count = c1.shape[0]
        total += mm(r1[first : first + count, :], c1[...], TN)
        first += count
    groups, _, rows, _ = send.shape
    high = bits_ref[1 if along_x else 2] == 1
    for g in range(groups):

        def block(y, x):
            first = (4 * g + 2 * y + x) * rows
            return total[first : first + rows]

        for k in range(2):
            a, b = (block(k, 0), block(k, 1)) if along_x else (block(0, k), block(1, k))
            send[g, k] = jnp.where(high, a, b).astype(bf16)
            keep[g, k] = jnp.where(high, b, a).astype(bf16)


def core_grad(bits, r0, r1, c0, others, place, parts, nseq, along_x):
    count, width = r0.shape
    cols = c0.shape[1] // parts
    tile = min(256, width // 2)
    steps = width // 2 // tile
    rows = width // (8 * nseq)
    groups = tile // (4 * rows)
    lane = pl.BlockSpec((count, tile), lambda i, w: (0, w[0] * steps + i))

    def held(a):
        return pl.BlockSpec(
            (a.shape[0], cols), lambda i, w: (0, place), pipeline_mode=pl.Buffered(1)
        )

    out = pl.BlockSpec((groups, 2, rows, cols), lambda i, w: (i, 0, 0, 0))
    return pl.pallas_call(
        functools.partial(core_grad_kernel, along_x),
        grid_spec=pltpu.PrefetchScalarGridSpec(
            num_scalar_prefetch=1,
            grid=(steps,),
            in_specs=[lane, lane, held(c0), *(held(c) for c in others)],
            out_specs=[out, out],
        ),
        out_shape=[sds((nseq, 2, rows, cols), bf16)] * 2,
        compiler_params=params(VMEM_MIB),
        cost_estimate=FREE,
    )(bits, r0, r1, c0, *others)


def total_of(terms):
    total = terms[0].astype(f32)
    for term in terms[1:]:
        total = total + term.astype(f32)
    return total


def take(terms, dim, place):
    return [lax.dynamic_index_in_dim(t, place, dim, keepdims=False) for t in terms]


class Line:
    def __init__(self, mark):
        self.mark = mark

    def fence(self, *values):
        *values, self.mark = lax.optimization_barrier((*values, self.mark))
        return values[0] if len(values) == 1 else tuple(values)


class Task:
    def __init__(self, line, chain):
        self.line, self.chain, self.done = line, chain, False
        self.result = None
        self.waiting = next(chain)

    def step(self, count=1):
        for _ in range(count):
            if self.done:
                return
            try:
                self.waiting = self.chain.send(self.line.fence(self.waiting))
            except StopIteration as end:
                self.done, self.result = True, end.value

    def drain(self):
        while not self.done:
            self.step()
        return self.result


def shards(
    tokens,
    lengths,
    gain_one,
    w_query,
    w_key,
    w_value,
    w_out,
    gain_two,
    w_gate,
    w_up,
    w_down,
    cotangent,
):
    rows_dev, stretch, width = tokens.shape
    nfeat, nseq, nrows = (lax.axis_size(a) for a in ("feat", "seq", "rows"))
    assert rows_dev == 1 and nfeat == 2 and nrows == 4 and nseq % 2 == 0
    ff = w_gate.shape[1]
    fi, si, ri = (lax.axis_index(a) for a in ("feat", "seq", "rows"))
    xb, yb = ri % 2, ri // 2
    slice_ff = ff // 4
    which = jnp.reshape(2 * fi + xb, (1,)).astype(jnp.int32)
    ybit = jnp.reshape(yb, (1,)).astype(jnp.int32)
    bits = jnp.stack([fi, xb, yb]).astype(jnp.int32)

    line = Line((lengths[0, :1] < 0).astype(f32))
    fence = line.fence

    def over_feat(a):
        return lax.ppermute(a, "feat", [(0, 1), (1, 0)])

    def over_x(a):
        return lax.ppermute(a, "rows", [(r, r ^ 1) for r in range(nrows)])

    def over_y(a):
        return lax.ppermute(a, "rows", [(r, r ^ 2) for r in range(nrows)])

    def over_seq(a, shift=1):
        return lax.ppermute(a, "seq", [(s, (s + shift) % nseq) for s in range(nseq)])

    def hops(state):
        states = []
        for _ in range(nseq - 1):
            state = yield over_seq(state)
            states.append(state)
        return states

    def hops_back(own):
        states, state = [], own
        for last in range(nseq - 1, 0, -1):
            state = yield lax.ppermute(state, "seq", [(last, last - 1)])
            states.append(state)
            state = low_sum([own, passes * state.astype(f32)])
        return states

    def low_sum(terms):
        return total_of(terms).astype(bf16)

    def pair_step(terms, dim, bit, swap):
        arrived = yield swap(low_sum(take(terms, dim, 1 - bit)))
        return [*take(terms, dim, bit), arrived]

    def ring_step(pick):
        held = []
        for k in range(nseq - 1):
            block = lax.rem(si - 1 - k + 2 * nseq, nseq)
            arrived = yield over_seq(low_sum(pick(block) + held))
            held = [arrived]
        return pick(si) + held

    flat = tokens.reshape(stretch, width)
    seed = cotangent.reshape(stretch, width)
    branch0 = fence(seed.astype(bf16))
    branch1, branch2 = over_feat(branch0), over_x(branch0)

    ndocs = lengths.shape[1]
    doc_lengths = lax.dynamic_index_in_dim(lengths, fi * nrows + ri, 0, keepdims=False)
    starts = jnp.cumsum(doc_lengths) - doc_lengths
    offset = si * stretch

    def doc_of(places):
        return jnp.sum((starts[None, :] <= places[:, None]).astype(jnp.int32), axis=1)

    places = offset + jnp.arange(stretch, dtype=jnp.int32)
    docs = doc_of(places)
    away = jnp.arange(1, nseq, dtype=jnp.int32)
    before = doc_of(jnp.reshape(offset - 1, (1,)))
    final = doc_of(jnp.reshape(offset + stretch - 1, (1,)))
    causal = jnp.arange(stretch)[None, :] <= jnp.arange(stretch)[:, None]
    mask = ((docs[:, None] == docs[None, :]) & causal).astype(f32)
    from_before = jnp.broadcast_to((docs == before).astype(f32)[:, None], (stretch, 128))
    at_end = jnp.broadcast_to((docs == final).astype(f32)[:, None], (stretch, 128))
    earlier = (
        (doc_of(offset - 1 - (away - 1) * stretch) == before) & (away <= si)
    ).astype(f32)
    passes = (final == before).astype(f32)

    pick_a, pick_b, level = feature_tables()
    tables = [("state", pick_a), ("state", pick_b), ("all", level)]
    state_shape = (HEADS, STATE_ROWS, VHEAD)
    columns = ("all", (stretch, 128), f32)
    packed = (stretch, HEADS * FDIM)
    per_head = (stretch, width)

    root_one = lax.rsqrt(jnp.mean(flat * flat, axis=-1, keepdims=True) + EPS)
    low_one = (flat * root_one * gain_one).astype(bf16)
    low_one1 = over_feat(low_one)
    keys = mm(low_one, w_key).astype(bf16)
    values = mm(low_one, w_value).astype(bf16)
    (key_state,) = head_call(
        key_state_kernel,
        [*tables, ("all", keys), ("head", values), ("all", at_end)],
        [("state", state_shape, bf16)],
    )
    chain = Task(line, hops(fence(key_state)))
    queries = mm(fence(low_one), w_query).astype(bf16)
    numer, denom_here, feats = fence(
        *head_call(
            intra_kernel,
            [
                *tables,
                ("all", queries),
                ("all", keys),
                ("head", values),
                ("all", mask),
            ],
            [("head", per_head, f32), columns, ("state", (HEADS, stretch, PADF), bf16)],
        )
    )
    chain.step()

    def hidden_grad(g0, g1):
        return token_call(
            hidden_grad_kernel,
            which,
            stretch,
            [("pair", g0, g1), ("tall", w_down)],
            ["row"],
            width,
            slice_ff,
        )[0]

    def act(x0, x1, grad):
        return token_call(
            act_kernel,
            which,
            stretch,
            [("pair", x0, x1), ("row", grad), ("wide", w_gate), ("wide", w_up)],
            ["row"] * 3,
            width,
            slice_ff,
        )

    def low_grad(gg, gu, kind):
        return token_call(
            low_grad_kernel,
            which,
            stretch,
            [("row", gg), ("row", gu), ("wide", w_gate), ("wide", w_up)],
            [kind],
            width,
            slice_ff,
        )

    def layer(hid, kind):
        return token_call(
            layer_kernel,
            which,
            stretch,
            [("row", hid), ("tall", w_down)],
            [kind],
            width,
            slice_ff,
        )

    branch1, low_one1 = fence(branch1, low_one1)
    gh_near = fence(hidden_grad(branch0, branch1))
    chain.step()
    branch2 = fence(branch2)
    branch3 = over_feat(branch2)
    branch3 = fence(branch3)
    gh_far = fence(hidden_grad(branch2, branch3))
    states = chain.drain()

    mixed_low, denom, state_in = head_call(
        combine_kernel,
        [
            ("smem", earlier),
            ("state", feats),
            ("head", numer),
            ("all", denom_here),
            ("all", from_before),
            *(("state", s) for s in states),
        ],
        [("head", per_head, bf16), columns, ("state", state_shape, f32)],
    )
    mixed_low1 = over_feat(mixed_low)
    middle = flat + mm(mixed_low, w_out)
    root_two = lax.rsqrt(jnp.mean(middle * middle, axis=-1, keepdims=True) + EPS)
    low0 = fence((middle * root_two * gain_two).astype(bf16))
    low1, low2 = over_feat(low0), over_x(low0)

    mixed_low1, low1 = fence(mixed_low1, low1)
    hid_n, gg_n, gu_n = fence(*act(low0, low1, gh_near))
    glow0, glow1 = fence(*low_grad(gg_n, gu_n, "two"))
    glow1 = over_feat(glow1)
    low2 = fence(low2)
    low3 = over_feat(low2)
    low3, glow1 = fence(low3, glow1)
    hid_f, gg_f, gu_f = fence(*act(low2, low3, gh_far))

    lows = (low0, low1, low2, low3)
    branches = (branch0, branch1, branch2, branch3)
    group_rows = width // (2 * nseq)

    def wide_share(sent, kept):
        terms = [kept, (yield over_y(sent))]
        split = [t.reshape(2, nseq, 2, group_rows // 4, slice_ff) for t in terms]
        mine = yield from ring_step(lambda b: take(split, 1, b))
        mine = total_of(mine).astype(bf16)
        own = lax.dynamic_index_in_dim(mine, xb, 1, keepdims=False)
        other = yield over_x(lax.dynamic_index_in_dim(mine, 1 - xb, 1, keepdims=False))
        cols = jnp.where(
            xb == 0,
            jnp.concatenate([own, other], axis=-1),
            jnp.concatenate([other, own], axis=-1),
        )
        own = lax.dynamic_index_in_dim(cols, fi, 0, keepdims=False)
        other = yield over_feat(lax.dynamic_index_in_dim(cols, 1 - fi, 0, keepdims=False))
        return fence(
            jnp.where(
                fi == 0,
                jnp.concatenate([own, other], axis=-1),
                jnp.concatenate([other, own], axis=-1),
            ).astype(f32)
        )

    def down_share(sent, kept):
        rows = slice_ff // (2 * nseq)
        terms = [kept, (yield over_y(sent))]
        split = [t.reshape(nseq // 2, 2, rows, width) for t in terms]

        def pick(b):
            zero = jnp.int32(0)
            place = (b % (nseq // 2), b // (nseq // 2), zero, zero)
            return [
                lax.dynamic_slice(t, place, (1, 1, rows, width)).reshape(rows, width)
                for t in split
            ]

        mine = yield from ring_step(pick)
        mine = low_sum(mine)
        swaps = []
        for s in range(nseq):
            for r in range(nrows):
                x = s // (nseq // 2)
                if x != r % 2:
                    to = (r % 2) * (nseq // 2) + s % (nseq // 2)
                    swaps.append((s * nrows + r, to * nrows + (r ^ 1)))
        moved = yield lax.ppermute(mine, ("seq", "rows"), swaps)
        stays = (si // (nseq // 2)) == xb
        return fence(jnp.where(stays, mine, moved).astype(f32))

    down_parts = fence(
        *down_grad(ybit, fence(hid_n), hid_f, branches, slice_ff // (nseq // 2))
    )
    down = Task(line, down_share(*down_parts))
    glow2, *glow3 = fence(*low_grad(fence(gg_f), gu_f, "pair"))
    glow3 = [over_feat(g) for g in glow3]
    gate_parts = fence(*wide_grad(ybit, lows, fence(gg_n), gg_f, group_rows))
    glow2, *glow3 = fence(glow2, *glow3)
    far_glow = over_x(low_sum([glow2, jnp.concatenate(glow3)]))
    up_parts = fence(*wide_grad(ybit, lows, fence(gu_n), gu_f, group_rows))
    down.step()
    gate = Task(line, wide_share(*fence(*gate_parts)))
    lay0, *lay1 = fence(*layer(fence(hid_n), "pair"))
    lay1 = [over_feat(a) for a in lay1]

    grad_middle, grad_mixed_low, grad_mixed, gains_two, *copies = fence(
        *norm_back(glow0, glow1, fence(far_glow), middle, seed, gain_two, w_out)
    )
    copies = [over_feat(a) for a in copies]
    lay1 = list(fence(lay0, *lay1)[1:])

    query_state, gnum, gden = fence(
        *head_call(
            query_state_kernel,
            [
                ("state", feats),
                ("head", fence(grad_mixed)),
                ("head", mixed_low),
                ("all", denom),
                ("all", from_before),
            ],
            [("state", state_shape, bf16), ("head", per_head, bf16), columns],
        )
    )
    chain = Task(line, hops_back(query_state))
    down.step()
    lay2, *lay3 = fence(*layer(fence(hid_f), "pair"))
    lay3 = [over_feat(a) for a in lay3]

    part = width // (8 * nseq)

    def share(parts, along_x, order):
        sent, keep = parts
        terms = [keep, (yield (over_x if along_x else over_y)(sent))]
        dims = {"seq": 0, "y" if along_x else "x": 1}
        for name in order:
            dim = dims.pop(name)
            dims = {k: v - (v > dim) for k, v in dims.items()}
            if name == "seq":
                now = terms
                terms = yield from ring_step(lambda b: take(now, dim, b))
            else:
                bit, swap = {"x": (xb, over_x), "y": (yb, over_y)}[name]
                terms = yield from pair_step(terms, dim, bit, swap)
        return fence(total_of(terms))

    def back(heads, gq, gk, gv):
        return fence(
            *head_call(
                functools.partial(back_kernel, heads[0]),
                [
                    *tables,
                    ("all", queries),
                    ("all", keys),
                    ("head", values),
                    ("all", mask),
                    ("head", fence(gnum)),
                    ("all", gden),
                    ("state", state_in),
                    ("all", from_before),
                    ("all", gq),
                    ("all", gk),
                    ("any", gv),
                ],
                [("all", packed, f32), ("all", packed, f32), ("head", per_head, f32)],
                heads=heads,
                aliases={13: 2} if heads[0] else None,
            )
        )

    empty = jnp.zeros((8, 128), f32)
    chain.step()
    down.step()
    grads = back((0, HEADS // 2), empty, empty, empty)
    lay2, *lay3 = fence(lay2, *lay3)
    far_lay = over_x(low_sum([lay2, jnp.concatenate(lay3)]))
    chain.step()
    down.step()
    gate.step()
    up = Task(line, wide_share(*fence(*up_parts)))
    grad_mixed_low, *copies = fence(grad_mixed_low, *copies)
    out = []
    for place, order in enumerate((("y", "seq"), ("seq", "y"))):
        pieces = fence(
            *core_grad(
                bits,
                fence(mixed_low),
                mixed_low1,
                grad_mixed_low,
                copies,
                place,
                2,
                nseq,
                True,
            )
        )
        out.append(Task(line, share(pieces, True, order)))
    gq, gk_part, gv_part = back((HEADS // 2, HEADS), *grads)
    states = chain.drain()
    gate.step()
    down.step()
    grad_keys, grad_values_low = head_call(
        back_state_kernel,
        [
            ("smem", jnp.ones((nseq - 1,), f32)),
            *tables,
            ("all", keys),
            ("head", values),
            ("all", at_end),
            ("all", gk_part),
            ("head", gv_part),
            *(("state", s) for s in states),
        ],
        [("all", packed, bf16), ("head", per_head, bf16)],
        scratch=[pltpu.VMEM(packed, f32)],
    )
    grad_queries = gq.astype(bf16)
    half = (width + 2 * w_query.shape[1]) // 2
    grad_all = fence(
        grad_values_low[:, :half],
        jnp.concatenate([grad_values_low[:, half:], grad_queries, grad_keys], axis=-1),
    )
    grad_all1 = [over_feat(g) for g in grad_all]
    gate.step()
    layer_out = fence(middle + total_of([lay0, jnp.concatenate(lay1), fence(far_lay)]))
    inner = []
    for own, other, (along_x, order) in zip(
        grad_all, grad_all1, ((False, ("x", "seq")), (True, ("y", "seq")))
    ):
        pieces = fence(
            *core_grad(bits, low_one, low_one1, own, [fence(other)], 0, 1, nseq, along_x)
        )
        inner.append(Task(line, share(pieces, along_x, order)))
    grad_low_one = fence(
        mm(fence(grad_queries), w_query, NT)
        + mm(grad_keys, w_key, NT)
        + mm(grad_values_low, w_value, NT)
    )
    up.step()
    out[0].step()
    out[1].step()
    unit_one = flat * root_one
    grad_gain_one = jnp.sum(grad_low_one * unit_one, axis=0)
    scaled = grad_low_one * gain_one
    grad_tokens = grad_middle + root_one * (
        scaled - unit_one * jnp.mean(scaled * unit_one, axis=-1, keepdims=True)
    )
    grad_tokens, grad_gain_one = fence(grad_tokens, grad_gain_one)
    both = jnp.concatenate(
        [grad_gain_one.reshape(-1, part), gains_two[0].reshape(-1, part)], axis=-1
    )
    both = lax.all_to_all(both, ("feat", "seq", "rows"), 0, 0, tiled=True)
    tasks = [*inner, up, *out, gate, down]
    while not all(t.done for t in tasks):
        for t in tasks:
            t.step()
    gains = jnp.sum(fence(both), axis=0) + line.mark
    grad_out_w = jnp.concatenate([t.result for t in out], axis=-1)
    qk = w_query.shape[1]
    lower, upper = (t.result for t in inner)

    return (
        layer_out.reshape(rows_dev, stretch, width),
        grad_tokens.reshape(rows_dev, stretch, width),
        gains[:part],
        upper[:, width - half : width - half + qk],
        upper[:, width - half + qk :],
        jnp.concatenate([lower, upper[:, : width - half]], axis=-1),
        grad_out_w,
        gains[part:],
        gate.result,
        up.result,
        down.result,
    )


def solution(mesh):
    split = P(("feat", "rows"), "seq", None)
    vector = P(("feat", "seq", "rows"))
    matrix = P(("feat", "seq", "rows"), None)
    in_specs = (split, *(P() for _ in range(10)), split)
    out_specs = (
        split,
        split,
        vector,
        matrix,
        matrix,
        matrix,
        matrix,
        vector,
        matrix,
        matrix,
        matrix,
    )
    return jax.shard_map(shards, mesh=mesh, in_specs=in_specs, out_specs=out_specs, check_vma=False)
```

time: 842 us -> 674 us (0.80)
  waiting for transfers between devices: 351 us -> 130 us
  Pallas kernels: 271 us -> 318 us
  local copies, waits for them, and re-layouts: 21.2 us -> 52.3 us
  matrix products: 49.3 us -> 29.4 us
  starting transfers between devices: 55 us -> 46.1 us
    ppermute x10, waiting for transfers between devices: 146 us -> 43 us  [over_x(): return lax.ppermute(a, 'rows', [(r, r ^ 1) for r in range(nrows)])]
    ppermute x28, waiting for transfers between devices: 141 us -> 66.7 us  [the longest x24 66.6 us: over_seq(): lax.ppermute(a, 'seq', [(s, (s + shift) % nseq) for s in range(nseq)])]
    ppermute x7, waiting for transfers between devices: 63.8 us -> 3.65 us  [over_y(): return lax.ppermute(a, 'rows', [(r, r ^ 2) for r in range(nrows)])]
    pallas_call x13 -> x23, Pallas kernels: 271 us -> 318 us  [the longest x8 126 us: token_call(): pl.pallas_call(functools.partial(kernel, half), grid_spec=pltpu.PrefetchS...]
    unnamed x114 -> x220, local copies, waits for them, and re-layouts: 6.03 us -> 48.3 us
    dot_general x11 -> x7, matrix products: 49.3 us -> 29.4 us  [mm(): return lax.dot_general(a, b, dims, preferred_element_type=f32)]
    ppermute x14 -> x19, waiting for transfers between devices: 0.78 us -> 16.4 us  [over_feat(): return lax.ppermute(a, 'feat', [(0, 1), (1, 0)])]
    ppermute x28, starting transfers between devices: 32.5 us -> 17.7 us  [the longest x24 11.7 us: over_seq(): lax.ppermute(a, 'seq', [(s, (s + shift) % nseq) for s in range(nseq)])]
  transfers between devices with their start and end apart: 59 -> 65, of which waited for: 27 -> 26; matrix products, arithmetic and copies ran while one was open for 16% -> 16% of each run, Pallas kernels for 26% -> 41%
where the time goes in v2:
time: 674 us; the launch traced here: 664 us
  Pallas kernels  318 us (47%)
  waiting for transfers between devices  130 us (19%)
  other arithmetic  84 us (12%)
  local copies, waits for them, and re-layouts  52.3 us (8%)
  starting transfers between devices  46.1 us (7%)
  matrix products  29.4 us (4%)
    pallas_call x8, Pallas kernels, token_call(): pl.pallas_call(functools.partial(kernel, half), grid_spec=pltpu.PrefetchS...  126 us
    pallas_call x7, Pallas kernels, head_call(): pl.pallas_call(body, grid=(last - first,), in_specs=[spec(kind, a.shape)...  100 us
    ppermute x24, waiting for transfers between devices, over_seq(): lax.ppermute(a, 'seq', [(s, (s + shift) % nseq) for s in range(nseq)])  66.6 us
    convert_element_type x30, other arithmetic, low_sum(): return total_of(terms).astype(bf16)  49.7 us
    unnamed x220, local copies, waits for them, and re-layouts  48.3 us
    ppermute x10, waiting for transfers between devices, over_x(): return lax.ppermute(a, 'rows', [(r, r ^ 1) for r in range(nrows)])  43 us
    pallas_call x2, Pallas kernels, wide_grad(): pl.pallas_call(wide_grad_kernel, grid_spec=pltpu.PrefetchScalarGridSpec(n...  33.7 us
    dot_general x7, matrix products, mm(): return lax.dot_general(a, b, dims, preferred_element_type=f32)  29.4 us
  transfers between devices with their start and end apart: 65, of which 26 were waited for; matrix products, arithmetic and copies ran while one was open for 16% of the time, Pallas kernels for 41%

profile of v2, /device:TPU:0, one launch (start us, length us, event | category | flops | bytes accessed | tf_op | source)
XLA Modules:
  0.0 664.0 jit_solution(6174293371252972394)
XLA Ops:
  0.7 4.0 bitcast_convert_fusion.g0
  7.0 2.6 collective-permute-start.5
  12.8 2.3 convolution_convert_fusion.2.refs_3_.refs_4_
  17.9 8.7 %convolution_convert_fusion.refs_4_.refs_5_ = bf16[512,2048]{1,0:T(8,128)(2,1)S(1)} fusion(bf16[512,2048]{1,0:T(8,128)(2,1)} %multiply_convert_fusion.1.r0, bf16[2048,2048]{1,0:T(8,128)(2,1)} %param.20), kind=kOutput, calls=%fused_computation.14 | convolution fusion | flops 4296015872 | bytes 12582912 | tf_op jit(solution)/shard_map/dot_general | solution.py:41
  26.7 9.2 %shard_map.230 = bf16[16,160,128]{2,1,0:T(8,128)(2,1)S(1)} custom-call(bf16[16,256,256]{2,1,0:T(8,128)(2,1)S(1)} %copy-done.1, bf16[16,256,256]{2,1,0:T(8,128)(2,1)S(1)} %copy-done.2, f32[8,256]{1,0:T(8,128)S(1)} %copy-done.90, bf16[512,256]{1,0:T(8,128)(2,1)S(1)} %convolution_convert_fusion.2.refs_3_.refs_4_, ...), custom_call_target="tpu_custom_call" | custom-call | tf_op jit(solution)/shard_map/pallas_call | solution.py:291
  37.7 2.7 convolution_convert_fusion.1.refs_3_
  40.4 18.0 %shard_map.231 = (f32[512,2048]{1,0:T(8,128)S(1)}, f32[512,128]{1,0:T(8,128)S(1)}, bf16[16,512,256]{2,1,0:T(8,128)(2,1)S(1)}) custom-call(bf16[16,256,256]{2,1,0:T(8,128)(2,1)S(1)} %copy-done.1, bf16[16,256,256]{2,1,0:T(8,128)(2,1)S(1)} %copy-done.2, f32[8,256]{1,0:T(8,128)S(1)} %copy-done.90, bf16[512,256]{1,0:T(8,128)(2,1)S(1)} %convolution_convert_fusion.1.refs_3_, ...), custom_call_target="tpu_custom_call" | custom-call | tf_op jit(solution)/shard_map/pallas_call | solution.py:291
  64.8 10.8 %shard_map.232.grad_ref = bf16[1024,1408]{1,0:T(8,128)(2,1)S(1)} custom-call(s32[1]{0:T(128)} %bitcast.4.which_ref, bf16[512,2048]{1,0:T(8,128)(2,1)} %bitcast_convert_fusion.g0, bf16[512,2048]{1,0:T(8,128)(2,1)} %collective-permute-done.2.g1, bf16[5632,2048]{1,0:T(8,128)(2,1)} %wd.7), custom_call_target="tpu_custom_call" | custom-call | tf_op jit(solution)/shard_map/pallas_call | solution.py:377
  75.7 6.4 collective-permute-done.1.refs_6_
  83.2 3.3 collective-permute-done.6.g1.g3
  86.5 11.1 %shard_map.233.grad_ref = bf16[1024,1408]{1,0:T(8,128)(2,1)S(1)} custom-call(s32[1]{0:T(128)} %bitcast.4.which_ref, bf16[512,2048]{1,0:T(8,128)(2,1)} %collective-permute-done.5.g0.g2, bf16[512,2048]{1,0:T(8,128)(2,1)S(1)} %collective-permute-done.6.g1.g3, bf16[5632,2048]{1,0:T(8,128)(2,1)} %wd.7), custom_call_target="tpu_custom_call" | custom-call | tf_op jit(solution)/shard_map/pallas_call | solution.py:377
  101.6 11.8 %shard_map.234 = (bf16[512,2048]{1,0:T(8,128)(2,1)S(1)}, f32[512,128]{1,0:T(8,128)S(1)}, f32[16,160,128]{2,1,0:T(8,128)S(1)}) custom-call(f32[3]{0:T(128)S(1)} %and_convert_fusion.refs_0_, bf16[16,512,256]{2,1,0:T(8,128)(2,1)S(1)} %copy-done.19, f32[512,2048]{1,0:T(8,128)S(1)} %copy-done.56, f32[512,128]{1,0:T(8,128)S(1)} %copy-done.89, ...), custom_call_target="tpu_custom_call" | custom-call | tf_op jit(solution)/shard_map/pallas_call | solution.py:291
  114.6 4.7 multiply_reduce_fusion.2
  122.3 3.1 collective-permute-done.8.x1.l1
  125.4 3.0 collective-permute-done.7.r1
  128.4 19.5 %shard_map.235 = (bf16[1024,1408]{1,0:T(8,128)(2,1)S(1)}, bf16[1024,1408]{1,0:T(8,128)(2,1)S(1)}, bf16[1024,1408]{1,0:T(8,128)(2,1)S(1)}) custom-call(s32[1]{0:T(128)} %bitcast.4.which_ref, bf16[512,2048]{1,0:T(8,128)(2,1)S(1)} %multiply_convert_fusion.x0.l0, bf16[512,2048]{1,0:T(8,128)(2,1)S(1)} %collective-permute-done.8.x1.l1, ...), custom_call_target="tpu_custom_call" | custom-call | tf_op jit(solution)/shard_map/pallas_call | solution.py:377
  149.6 21.6 %shard_map.236 = (bf16[512,2048]{1,0:T(8,128)(2,1)S(1)}, bf16[512,2048]{1,0:T(8,128)(2,1)}) custom-call(s32[1]{0:T(128)} %bitcast.4.which_ref, bf16[1024,1408]{1,0:T(8,128)(2,1)S(1)} %get-tuple-element.391.gg.near, bf16[1024,1408]{1,0:T(8,128)(2,1)S(1)} %get-tuple-element.403.gu.near, bf16[2048,5632]{1,0:T(8,128)(2,1)} %wg.7, bf16[2048,5632]{1,0:T(8,128)(2,1)} %wu.7), custom_call_target="tpu_custom_call" | custom-call | tf_op jit(solution)/shard_map/pallas_call | solution.py:377
  173.1 4.0 collective-permute-done.10.x1.l3
  177.1 3.0 collective-permute-done.11.near
  181.9 20.0 %shard_map.237 = (bf16[1024,1408]{1,0:T(8,128)(2,1)S(1)}, bf16[1024,1408]{1,0:T(8,128)(2,1)S(1)}, bf16[1024,1408]{1,0:T(8,128)(2,1)S(1)}) custom-call(s32[1]{0:T(128)} %bitcast.4.which_ref, bf16[512,2048]{1,0:T(8,128)(2,1)} %collective-permute-done.9.x0.l2, bf16[512,2048]{1,0:T(8,128)(2,1)} %collective-permute-done.10.x1.l3, ...), custom_call_target="tpu_custom_call" | custom-call | tf_op jit(solution)/shard_map/pallas_call | solution.py:377
  203.5 16.8 %shard_map.238 = (bf16[2,352,2048]{2,1,0:T(8,128)(2,1)S(1)}, bf16[2,352,2048]{2,1,0:T(8,128)(2,1)S(1)}) custom-call(s32[1]{0:T(128)} %bitcast.5.ybit_ref, bf16[1024,1408]{1,0:T(8,128)(2,1)S(1)} %copy-done.27, bf16[1024,1408]{1,0:T(8,128)(2,1)S(1)} %get-tuple-element.447.far.hid, bf16[512,2048]{1,0:T(8,128)(2,1)} %bitcast_convert_fusion.g0, ...), custom_call_target="tpu_custom_call" | custom-call | tf_op jit(solution)/shard_map/pallas_call | solution.py:450
  223.5 2.4 copy-done.37
  225.9 18.9 %shard_map.239 = (bf16[512,2048]{1,0:T(8,128)(2,1)S(1)}, bf16[256,2048]{1,0:T(8,128)(2,1)S(1)}, bf16[256,2048]{1,0:T(8,128)(2,1)S(1)}) custom-call(s32[1]{0:T(128)} %bitcast.4.which_ref, bf16[1024,1408]{1,0:T(8,128)(2,1)S(1)} %copy-done.37, bf16[1024,1408]{1,0:T(8,128)(2,1)S(1)} %get-tuple-element.385.gu.far, bf16[2048,5632]{1,0:T(8,128)(2,1)} %wg.7, ...), custom_call_target="tpu_custom_call" | custom-call | tf_op jit(solution)/shard_map/pallas_call | solution.py:377
  247.1 16.4 %shard_map.240 = (bf16[8,128,1408]{2,1,0:T(8,128)(2,1)S(1)}, bf16[8,128,1408]{2,1,0:T(8,128)(2,1)S(1)}) custom-call(s32[1]{0:T(128)} %bitcast.5.ybit_ref, bf16[512,2048]{1,0:T(8,128)(2,1)S(1)} %copy-done.12, bf16[512,2048]{1,0:T(8,128)(2,1)S(1)} %copy-done.17, bf16[512,2048]{1,0:T(8,128)(2,1)} %collective-permute-done.9.x0.l2, ...), custom_call_target="tpu_custom_call" | custom-call | tf_op jit(solution)/shard_map/pallas_call | solution.py:419
  269.1 17.2 %shard_map.241 = (bf16[8,128,1408]{2,1,0:T(8,128)(2,1)}, bf16[8,128,1408]{2,1,0:T(8,128)(2,1)S(1)}) custom-call(s32[1]{0:T(128)} %bitcast.5.ybit_ref, bf16[512,2048]{1,0:T(8,128)(2,1)S(1)} %copy-done.12, bf16[512,2048]{1,0:T(8,128)(2,1)S(1)} %copy-done.17, bf16[512,2048]{1,0:T(8,128)(2,1)} %collective-permute-done.9.x0.l2, ...), custom_call_target="tpu_custom_call" | custom-call | tf_op jit(solution)/shard_map/pallas_call | solution.py:419
  286.6 12.3 %shard_map.242 = (bf16[512,2048]{1,0:T(8,128)(2,1)S(1)}, bf16[256,2048]{1,0:T(8,128)(2,1)}, bf16[256,2048]{1,0:T(8,128)(2,1)}) custom-call(s32[1]{0:T(128)} %bitcast.4.which_ref, bf16[1024,1408]{1,0:T(8,128)(2,1)S(1)} %copy-done.27, bf16[5632,2048]{1,0:T(8,128)(2,1)} %wd.7), custom_call_target="tpu_custom_call" | custom-call | tf_op jit(solution)/shard_map/pallas_call | solution.py:377
  300.8 2.4 fusion.14
  304.2 11.2 %collective-permute-done.17.far = bf16[512,2048]{1,0:T(8,128)(2,1)} collective-permute-done((bf16[512,2048]{1,0:T(8,128)(2,1)}, bf16[512,2048]{1,0:T(8,128)(2,1)}, u32[]{:S(2)}, u32[]{:S(2)}) %collective-permute-start.17) | collective-permute-done | bytes 2097184 | tf_op jit(solution)/shard_map/ppermute | solution.py:644
  319.2 20.8 %shard_map.243 = (f32[512,2048]{1,0:T(8,128)S(1)}, bf16[512,2048]{1,0:T(8,128)(2,1)S(1)}, f32[512,2048]{1,0:T(8,128)S(1)}, f32[8,2048]{1,0:T(8,128)S(1)}, bf16[2...) custom-call(bf16[512,2048]{1,0:T(8,128)(2,1)S(1)} %copy-done.74, bf16[512,2048]{1,0:T(8,128)(2,1)} %collective-permute-done.11.near, ...), custom_call_target="tpu_custom_call" | custom-call | tf_op jit(solution)/shard_map/pallas_call | solution.py:498
  340.2 12.4 %shard_map.244 = (bf16[16,160,128]{2,1,0:T(8,128)(2,1)}, bf16[512,2048]{1,0:T(8,128)(2,1)S(1)}, f32[512,128]{1,0:T(8,128)S(1)}) custom-call(bf16[16,512,256]{2,1,0:T(8,128)(2,1)S(1)} %copy-done.20, f32[512,2048]{1,0:T(8,128)S(1)} %get-tuple-element.439.refs_1_, bf16[512,2048]{1,0:T(8,128)(2,1)S(1)} %copy-done.14, f32[512,128]{1,0:T(8,128)S(1)} %copy-done.87, ...), custom_call_target="tpu_custom_call" | custom-call | tf_op jit(solution)/shard_map/pallas_call | solution.py:291
  356.1 2.8 fusion.9
  362.1 11.6 %shard_map.245 = (bf16[512,2048]{1,0:T(8,128)(2,1)S(1)}, bf16[256,2048]{1,0:T(8,128)(2,1)}, bf16[256,2048]{1,0:T(8,128)(2,1)}) custom-call(s32[1]{0:T(128)} %bitcast.4.which_ref, bf16[1024,1408]{1,0:T(8,128)(2,1)S(1)} %copy-done.25, bf16[5632,2048]{1,0:T(8,128)(2,1)} %wd.7), custom_call_target="tpu_custom_call" | custom-call | tf_op jit(solution)/shard_map/pallas_call | solution.py:377
  374.2 2.6 fusion.10
  378.3 8.4 %collective-permute-done.21 = bf16[176,2048]{1,0:T(8,128)(2,1)} collective-permute-done((bf16[176,2048]{1,0:T(8,128)(2,1)}, bf16[176,2048]{1,0:T(8,128)(2,1)}, u32[]{:S(2)}, u32[]{:S(2)}) %collective-permute-start.21) | collective-permute-done | bytes 720928 | tf_op jit(solution)/shard_map/ppermute | solution.py:650
  386.7 2.8 fusion.8
  399.8 15.8 %shard_map.246 = (f32[512,256]{1,0:T(8,128)S(1)}, f32[512,256]{1,0:T(8,128)S(1)}, f32[512,2048]{1,0:T(8,128)S(1)}) custom-call(bf16[16,256,256]{2,1,0:T(8,128)(2,1)S(1)} %copy-done.1, bf16[16,256,256]{2,1,0:T(8,128)(2,1)S(1)} %copy-done.3, f32[8,256]{1,0:T(8,128)S(1)} %copy-done.90, bf16[512,256]{1,0:T(8,128)(2,1)S(1)} %copy-done.65, ...), custom_call_target="tpu_custom_call" | custom-call | tf_op jit(solution)/shard_map/pallas_call | solution.py:291
  419.4 2.8 fusion.6
  425.9 2.9 collective-permute-start.27
  428.8 3.9 add_convert_fusion
  432.7 3.0 collective-permute-start.23
  435.7 4.1 shard_map.247
  439.8 4.1 shard_map.248
  444.0 15.8 %shard_map.249 = (f32[512,256]{1,0:T(8,128)S(1)}, f32[512,256]{1,0:T(8,128)S(1)}, f32[512,2048]{1,0:T(8,128)S(1)}) custom-call(bf16[16,256,256]{2,1,0:T(8,128)(2,1)S(1)} %copy-done.1, bf16[16,256,256]{2,1,0:T(8,128)(2,1)S(1)} %copy-done.4, f32[8,256]{1,0:T(8,128)S(1)} %copy-done.90, ...), custom_call_target="tpu_custom_call", output_to_operand_aliasing={{2}: (13, {})} | custom-call | tf_op jit(solution)/shard_map/pallas_call | solution.py:291
  460.3 17.1 %shard_map.250 = (bf16[512,256]{1,0:T(8,128)(2,1)S(1)}, bf16[512,2048]{1,0:T(8,128)(2,1)S(1)}) custom-call(f32[3]{0:T(128)S(1)} %broadcast_5_refs_0_.2.refs_0_, bf16[16,256,256]{2,1,0:T(8,128)(2,1)S(1)} %copy-done.1, bf16[16,256,256]{2,1,0:T(8,128)(2,1)S(1)} %copy-done.4, f32[8,256]{1,0:T(8,128)S(1)} %copy-done.90, ...), custom_call_target="tpu_custom_call" | custom-call | tf_op jit(solution)/shard_map/pallas_call | solution.py:291
  477.7 2.3 select_convert_fusion
  482.4 9.6 %fusion.50 = f32[512,2048]{1,0:T(8,128)} fusion(bf16[512,2048]{1,0:T(8,128)(2,1)S(1)} %get-tuple-element.517, bf16[2048,2048]{1,0:T(8,128)(2,1)} %param.20), kind=kOutput, calls=%fused_computation.136 | convolution fusion | flops 4294967296 | bytes 14680064 | tf_op jit(solution)/shard_map/dot_general | solution.py:41
  492.0 8.3 %collective-permute-done.31 = bf16[2,2,64,1408]{3,2,1,0:T(8,128)(2,1)S(1)} collective-permute-done((bf16[2,2,64,1408]{3,2,1,0:T(8,128)(2,1)S(1)}, bf16[2,2,64,1408]{3,2,1,0:T(8,128)(2,1)S(1)}, u32[]{:S(2)}, u32[]{:S(2)}) %collective-permute-start.31) | collective-permute-done | bytes 720928 | tf_op jit(solution)/shard_map/ppermute | solution.py:650
  502.3 5.4 add_add_fusion.1
  510.0 6.2 shard_map.251
  517.3 6.2 shard_map.252
  531.7 3.1 multiply_add_fusion
  536.7 12.2 %collective-permute-done.35 = bf16[4,2,64,1024]{3,2,1,0:T(8,128)(2,1)} collective-permute-done((bf16[4,2,64,1024]{3,2,1,0:T(8,128)(2,1)S(1)}, bf16[4,2,64,1024]{3,2,1,0:T(8,128)(2,1)}, u32[]{:S(2)}, u32[]{:S(2)}) %collective-permute-start.35) | collective-permute-done | bytes 1048608 | tf_op jit(solution)/shard_map/ppermute | solution.py:644
  548.9 2.5 fusion.16
  552.1 5.2 all-to-all-start
  558.5 3.3 collective-permute-done.40
  561.9 12.1 %collective-permute-done.39 = bf16[4,2,64,1280]{3,2,1,0:T(8,128)(2,1)} collective-permute-done((bf16[4,2,64,1280]{3,2,1,0:T(8,128)(2,1)}, bf16[4,2,64,1280]{3,2,1,0:T(8,128)(2,1)}, u32[]{:S(2)}, u32[]{:S(2)}) %collective-permute-start.39) | collective-permute-done | bytes 1310752 | tf_op jit(solution)/shard_map/ppermute | solution.py:644
  585.4 4.9 collective-permute-done.43
  593.2 10.5 %collective-permute-done.41 = bf16[2,2,64,1408]{3,2,1,0:T(8,128)(2,1)S(1)} collective-permute-done((bf16[2,2,64,1408]{3,2,1,0:T(8,128)(2,1)S(1)}, bf16[2,2,64,1408]{3,2,1,0:T(8,128)(2,1)S(1)}, u32[]{:S(2)}, u32[]{:S(2)}) %collective-permute-start.41) | collective-permute-done | bytes 720928 | tf_op jit(solution)/shard_map/ppermute | solution.py:650
  605.1 4.2 collective-permute-done.51
  609.4 2.5 collective-permute-done.49
  618.4 2.5 collective-permute-start.55
  621.9 14.0 %collective-permute-done.47 = bf16[2,2,64,1408]{3,2,1,0:T(8,128)(2,1)S(1)} collective-permute-done((bf16[2,2,64,1408]{3,2,1,0:T(8,128)(2,1)S(1)}, bf16[2,2,64,1408]{3,2,1,0:T(8,128)(2,1)S(1)}, u32[]{:S(2)}, u32[]{:S(2)}) %collective-permute-start.47) | collective-permute-done | bytes 720928 | tf_op jit(solution)/shard_map/ppermute | solution.py:650
  637.0 4.0 collective-permute-done.57
  650.8 2.6 collective-permute-done.53
  (402 shorter events, 139.7 us)
Async XLA Ops:
  6.5 58.3 %collective-permute-start.2 = (bf16[512,2048]{1,0:T(8,128)(2,1)}, bf16[512,2048]{1,0:T(8,128)(2,1)}, u32[]{:S(2)}, u32[]{:S(2)}) collective-permute-start(bf16[512,2048]{1,0:T(8,128)(2,1)} %bitcast_convert_fusion.g0), channel_id=1, source_target_pairs={{0,16},{16,0},{1,17},{17,1},{2,18},{18,2},{3,19},{19,3},{4,20},{20... | collective-permute-start | bytes 6291464 | tf_op jit(solution)/shard_map/ppermute | solution.py:641
  7.0 75.0 %collective-permute-start.5 = (bf16[512,2048]{1,0:T(8,128)(2,1)}, bf16[512,2048]{1,0:T(8,128)(2,1)}, u32[]{:S(2)}, u32[]{:S(2)}) collective-permute-start(bf16[512,2048]{1,0:T(8,128)(2,1)} %bitcast_convert_fusion.g0), channel_id=1, source_target_pairs={{0,1},{1,0},{2,3},{3,2},{4,5},{5,4},{6,7},{7,6},{8,9},{9,8},{10,11... | collective-permute-start | bytes 6291464 | tf_op jit(solution)/shard_map/ppermute | solution.py:644
  11.7 53.1 %collective-permute-start.3 = (bf16[512,2048]{1,0:T(8,128)(2,1)}, bf16[512,2048]{1,0:T(8,128)(2,1)}, u32[]{:S(2)}, u32[]{:S(2)}) collective-permute-start(bf16[512,2048]{1,0:T(8,128)(2,1)} %multiply_convert_fusion.1.r0), channel_id=1, source_target_pairs={{0,16},{16,0},{1,17},{17,1},{2,18},{18,2},{3,19},{19,3},{4,20},{20... | collective-permute-start | bytes 6291464 | tf_op jit(solution)/shard_map/ppermute | solution.py:641
  35.9 27.3 %collective-permute-start = (bf16[16,160,128]{2,1,0:T(8,128)(2,1)S(1)}, bf16[16,160,128]{2,1,0:T(8,128)(2,1)}, u32[]{:S(2)}, u32[]{:S(2)}) collective-permute-start(bf16[16,160,128]{2,1,0:T(8,128)(2,1)S(1)} %shard_map.230), channel_id=1, source_target_pairs={{0,4},{4,8},{8,12},{12,0},{1,5},{5,9},{9,13},{13,1},{2,6},{6,10},{... | collective-permute-start | bytes 1966088 | tf_op jit(solution)/shard_map/ppermute | solution.py:650
  63.3 18.8 %collective-permute-start.1 = (bf16[16,160,128]{2,1,0:T(8,128)(2,1)}, bf16[16,160,128]{2,1,0:T(8,128)(2,1)}, u32[]{:S(2)}, u32[]{:S(2)}) collective-permute-start(bf16[16,160,128]{2,1,0:T(8,128)(2,1)} %collective-permute-done.refs_5_), channel_id=1, source_target_pairs={{0,4},{4,8},{8,12},{12,0},{1,5},{5,9},{9,13},{13,1},{2,6},{6,10},{... | collective-permute-start | bytes 1966088 | tf_op jit(solution)/shard_map/ppermute | solution.py:650
  82.1 4.4 collective-permute-start.6
  82.1 19.3 %collective-permute-start.4 = (bf16[16,160,128]{2,1,0:T(8,128)(2,1)}, bf16[16,160,128]{2,1,0:T(8,128)(2,1)S(1)}, u32[]{:S(2)}, u32[]{:S(2)}) collective-permute-start(bf16[16,160,128]{2,1,0:T(8,128)(2,1)} %collective-permute-done.1.refs_6_), channel_id=1, source_target_pairs={{0,4},{4,8},{8,12},{12,0},{1,5},{5,9},{9,13},{13,1},{2,6},{6,10},{... | collective-permute-start | bytes 1966088 | tf_op jit(solution)/shard_map/ppermute | solution.py:650
  121.3 4.2 collective-permute-start.8
  121.3 7.2 %collective-permute-start.7 = (bf16[512,2048]{1,0:T(8,128)(2,1)S(1)}, bf16[512,2048]{1,0:T(8,128)(2,1)S(1)}, u32[]{:S(2)}, u32[]{:S(2)}) collective-permute-start(bf16[512,2048]{1,0:T(8,128)(2,1)S(1)} %get-tuple-element.498.refs_2_.r0), channel_id=1, source_target_pairs={{0,16},{16,0},{1,17},{17,1},{2,18},{18,2},{3,19},{19,3},{4,20},{20... | collective-permute-start | bytes 6291464 | tf_op jit(solution)/shard_map/ppermute | solution.py:641
  121.8 50.8 %collective-permute-start.9 = (bf16[512,2048]{1,0:T(8,128)(2,1)S(1)}, bf16[512,2048]{1,0:T(8,128)(2,1)}, u32[]{:S(2)}, u32[]{:S(2)}) collective-permute-start(bf16[512,2048]{1,0:T(8,128)(2,1)S(1)} %multiply_convert_fusion.x0.l0), channel_id=1, source_target_pairs={{0,1},{1,0},{2,3},{3,2},{4,5},{5,4},{6,7},{7,6},{8,9},{9,8},{10,11... | collective-permute-start | bytes 6291464 | tf_op jit(solution)/shard_map/ppermute | solution.py:644
  172.6 4.5 collective-permute-start.10
  172.8 7.4 %collective-permute-start.11 = (bf16[512,2048]{1,0:T(8,128)(2,1)}, bf16[512,2048]{1,0:T(8,128)(2,1)}, u32[]{:S(2)}, u32[]{:S(2)}) collective-permute-start(bf16[512,2048]{1,0:T(8,128)(2,1)} %get-tuple-element.368), channel_id=1, source_target_pairs={{0,16},{16,0},{1,17},{17,1},{2,18},{18,2},{3,19},{19,3},{4,20},{20... | collective-permute-start | bytes 6291464 | tf_op jit(solution)/shard_map/ppermute | solution.py:641
  222.0 64.6 %collective-permute-start.12 = (bf16[2,352,2048]{2,1,0:T(8,128)(2,1)S(1)}, bf16[2,352,2048]{2,1,0:T(8,128)(2,1)}, u32[]{:S(2)}, u32[]{:S(2)}) collective-permute-start(bf16[2,352,2048]{2,1,0:T(8,128)(2,1)S(1)} %get-tuple-element.397), channel_id=1, source_target_pairs={{0,2},{1,3},{2,0},{3,1},{4,6},{5,7},{6,4},{7,5},{8,10},{9,11},{10,... | collective-permute-start | bytes 8650760 | tf_op jit(solution)/shard_map/ppermute | solution.py:647
  244.7 18.9 %collective-permute-start.13 = (bf16[256,2048]{1,0:T(8,128)(2,1)S(1)}, bf16[256,2048]{1,0:T(8,128)(2,1)S(1)}, u32[]{:S(2)}, u32[]{:S(2)}) collective-permute-start(bf16[256,2048]{1,0:T(8,128)(2,1)S(1)} %get-tuple-element.399), channel_id=1, source_target_pairs={{0,16},{16,0},{1,17},{17,1},{2,18},{18,2},{3,19},{19,3},{4,20},{20... | collective-permute-start | bytes 3145736 | tf_op jit(solution)/shard_map/ppermute | solution.py:641
  244.8 18.8 %collective-permute-start.14 = (bf16[256,2048]{1,0:T(8,128)(2,1)S(1)}, bf16[256,2048]{1,0:T(8,128)(2,1)S(1)}, u32[]{:S(2)}, u32[]{:S(2)}) collective-permute-start(bf16[256,2048]{1,0:T(8,128)(2,1)S(1)} %get-tuple-element.400), channel_id=1, source_target_pairs={{0,16},{16,0},{1,17},{17,1},{2,18},{18,2},{3,19},{19,3},{4,20},{20... | collective-permute-start | bytes 3145736 | tf_op jit(solution)/shard_map/ppermute | solution.py:641
  267.5 47.9 %collective-permute-start.17 = (bf16[512,2048]{1,0:T(8,128)(2,1)}, bf16[512,2048]{1,0:T(8,128)(2,1)}, u32[]{:S(2)}, u32[]{:S(2)}) collective-permute-start(bf16[512,2048]{1,0:T(8,128)(2,1)} %add_convert_fusion.1), channel_id=1, source_target_pairs={{0,1},{1,0},{2,3},{3,2},{4,5},{5,4},{6,7},{7,6},{8,9},{9,8},{10,11... | collective-permute-start | bytes 6291464 | tf_op jit(solution)/shard_map/ppermute | solution.py:644
  300.3 39.8 %collective-permute-start.15 = (bf16[256,2048]{1,0:T(8,128)(2,1)}, bf16[256,2048]{1,0:T(8,128)(2,1)}, u32[]{:S(2)}, u32[]{:S(2)}) collective-permute-start(bf16[256,2048]{1,0:T(8,128)(2,1)} %get-tuple-element.416), channel_id=1, source_target_pairs={{0,16},{16,0},{1,17},{17,1},{2,18},{18,2},{3,19},{19,3},{4,20},{20... | collective-permute-start | bytes 3145736 | tf_op jit(solution)/shard_map/ppermute | solution.py:641
  300.4 39.7 %collective-permute-start.16 = (bf16[256,2048]{1,0:T(8,128)(2,1)}, bf16[256,2048]{1,0:T(8,128)(2,1)}, u32[]{:S(2)}, u32[]{:S(2)}) collective-permute-start(bf16[256,2048]{1,0:T(8,128)(2,1)} %get-tuple-element.417), channel_id=1, source_target_pairs={{0,16},{16,0},{1,17},{17,1},{2,18},{18,2},{3,19},{19,3},{4,20},{20... | collective-permute-start | bytes 3145736 | tf_op jit(solution)/shard_map/ppermute | solution.py:641
  303.3 51.4 %collective-permute-start.18 = (bf16[176,2048]{1,0:T(8,128)(2,1)}, bf16[176,2048]{1,0:T(8,128)(2,1)}, u32[]{:S(2)}, u32[]{:S(2)}) collective-permute-start(bf16[176,2048]{1,0:T(8,128)(2,1)} %fusion.14), channel_id=1, source_target_pairs={{0,4},{4,8},{8,12},{12,0},{1,5},{5,9},{9,13},{13,1},{2,6},{6,10},{... | collective-permute-start | bytes 2162696 | tf_op jit(solution)/shard_map/ppermute | solution.py:650
  303.3 120.5 %collective-permute-start.24 = (bf16[8,128,1408]{2,1,0:T(8,128)(2,1)}, bf16[8,128,1408]{2,1,0:T(8,128)(2,1)}, u32[]{:S(2)}, u32[]{:S(2)}) collective-permute-start(bf16[8,128,1408]{2,1,0:T(8,128)(2,1)} %copy-done.92), channel_id=1, source_target_pairs={{0,2},{1,3},{2,0},{3,1},{4,6},{5,7},{6,4},{7,5},{8,10},{9,11},{10,... | collective-permute-start | bytes 8650760 | tf_op jit(solution)/shard_map/ppermute | solution.py:647
  354.6 19.6 %collective-permute-start.22 = (bf16[16,160,128]{2,1,0:T(8,128)(2,1)}, bf16[16,160,128]{2,1,0:T(8,128)(2,1)}, u32[]{:S(2)}, u32[]{:S(2)}) collective-permute-start(bf16[16,160,128]{2,1,0:T(8,128)(2,1)} %get-tuple-element.457), channel_id=1, source_target_pairs={{12,8},{13,9},{14,10},{15,11},{28,24},{29,25},{30,26},{31,27}} | collective-permute-start | bytes 1966088 | tf_op jit(solution)/shard_map/ppermute | solution.py:662
  358.9 27.8 %collective-permute-start.21 = (bf16[176,2048]{1,0:T(8,128)(2,1)}, bf16[176,2048]{1,0:T(8,128)(2,1)}, u32[]{:S(2)}, u32[]{:S(2)}) collective-permute-start(bf16[176,2048]{1,0:T(8,128)(2,1)} %fusion.9), channel_id=1, source_target_pairs={{0,4},{4,8},{8,12},{12,0},{1,5},{5,9},{9,13},{13,1},{2,6},{6,10},{... | collective-permute-start | bytes 2162696 | tf_op jit(solution)/shard_map/ppermute | solution.py:650
  373.7 41.9 %collective-permute-start.19 = (bf16[256,2048]{1,0:T(8,128)(2,1)}, bf16[256,2048]{1,0:T(8,128)(2,1)}, u32[]{:S(2)}, u32[]{:S(2)}) collective-permute-start(bf16[256,2048]{1,0:T(8,128)(2,1)} %get-tuple-element.453), channel_id=1, source_target_pairs={{0,16},{16,0},{1,17},{17,1},{2,18},{18,2},{3,19},{19,3},{4,20},{20... | collective-permute-start | bytes 3145736 | tf_op jit(solution)/shard_map/ppermute | solution.py:641
  373.7 42.0 %collective-permute-start.20 = (bf16[256,2048]{1,0:T(8,128)(2,1)}, bf16[256,2048]{1,0:T(8,128)(2,1)}, u32[]{:S(2)}, u32[]{:S(2)}) collective-permute-start(bf16[256,2048]{1,0:T(8,128)(2,1)} %get-tuple-element.454), channel_id=1, source_target_pairs={{0,16},{16,0},{1,17},{17,1},{2,18},{18,2},{3,19},{19,3},{4,20},{20... | collective-permute-start | bytes 3145736 | tf_op jit(solution)/shard_map/ppermute | solution.py:641
  376.8 39.4 %collective-permute-start.26 = (bf16[16,160,128]{2,1,0:T(8,128)(2,1)}, bf16[16,160,128]{2,1,0:T(8,128)(2,1)}, u32[]{:S(2)}, u32[]{:S(2)}) collective-permute-start(bf16[16,160,128]{2,1,0:T(8,128)(2,1)} %fusion.10), channel_id=1, source_target_pairs={{8,4},{9,5},{10,6},{11,7},{24,20},{25,21},{26,22},{27,23}} | collective-permute-start | bytes 1966088 | tf_op jit(solution)/shard_map/ppermute | solution.py:662
  389.5 30.0 %collective-permute-start.25 = (bf16[176,2048]{1,0:T(8,128)(2,1)}, bf16[176,2048]{1,0:T(8,128)(2,1)}, u32[]{:S(2)}, u32[]{:S(2)}) collective-permute-start(bf16[176,2048]{1,0:T(8,128)(2,1)} %fusion.8), channel_id=1, source_target_pairs={{0,4},{4,8},{8,12},{12,0},{1,5},{5,9},{9,13},{13,1},{2,6},{6,10},{... | collective-permute-start | bytes 2162696 | tf_op jit(solution)/shard_map/ppermute | solution.py:650
  415.6 17.0 %collective-permute-start.29 = (bf16[256,2048]{1,0:T(8,128)(2,1)S(1)}, bf16[256,2048]{1,0:T(8,128)(2,1)S(1)}, u32[]{:S(2)}, u32[]{:S(2)}) collective-permute-start(bf16[256,2048]{1,0:T(8,128)(2,1)S(1)} %copy-done.96), channel_id=1, source_target_pairs={{0,16},{16,0},{1,17},{17,1},{2,18},{18,2},{3,19},{19,3},{4,20},{20... | collective-permute-start | bytes 3145736 | tf_op jit(solution)/shard_map/ppermute | solution.py:641
  415.7 19.9 %collective-permute-start.30 = (bf16[256,2048]{1,0:T(8,128)(2,1)S(1)}, bf16[256,2048]{1,0:T(8,128)(2,1)S(1)}, u32[]{:S(2)}, u32[]{:S(2)}) collective-permute-start(bf16[256,2048]{1,0:T(8,128)(2,1)S(1)} %copy-done.94), channel_id=1, source_target_pairs={{0,16},{16,0},{1,17},{17,1},{2,18},{18,2},{3,19},{19,3},{4,20},{20... | collective-permute-start | bytes 3145736 | tf_op jit(solution)/shard_map/ppermute | solution.py:641
  418.0 42.3 %collective-permute-start.28 = (bf16[16,160,128]{2,1,0:T(8,128)(2,1)S(1)}, bf16[16,160,128]{2,1,0:T(8,128)(2,1)S(1)}, u32[]{:S(2)}, u32[]{:S(2)}) collective-permute-start(bf16[16,160,128]{2,1,0:T(8,128)(2,1)S(1)} %fusion.11), channel_id=1, source_target_pairs={{4,0},{5,1},{6,2},{7,3},{20,16},{21,17},{22,18},{23,19}} | collective-permute-start | bytes 1966088 | tf_op jit(solution)/shard_map/ppermute | solution.py:662
  422.2 55.5 %collective-permute-start.32 = (bf16[176,2048]{1,0:T(8,128)(2,1)}, bf16[176,2048]{1,0:T(8,128)(2,1)}, u32[]{:S(2)}, u32[]{:S(2)}) collective-permute-start(bf16[176,2048]{1,0:T(8,128)(2,1)} %fusion.6), channel_id=1, source_target_pairs={{1,8},{3,10},{5,12},{7,14},{8,1},{10,3},{12,5},{14,7},{17,24},{19,... | collective-permute-start | bytes 2162696 | tf_op jit(solution)/shard_map/ppermute | solution.py:871
  425.9 51.8 %collective-permute-start.27 = (bf16[2,2,64,1408]{3,2,1,0:T(8,128)(2,1)}, bf16[2,2,64,1408]{3,2,1,0:T(8,128)(2,1)}, u32[]{:S(2)}, u32[]{:S(2)}) collective-permute-start(bf16[2,2,64,1408]{3,2,1,0:T(8,128)(2,1)} %fusion.15), channel_id=1, source_target_pairs={{0,4},{4,8},{8,12},{12,0},{1,5},{5,9},{9,13},{13,1},{2,6},{6,10},{... | collective-permute-start | bytes 2162696 | tf_op jit(solution)/shard_map/ppermute | solution.py:650
  432.7 67.9 %collective-permute-start.23 = (bf16[512,2048]{1,0:T(8,128)(2,1)}, bf16[512,2048]{1,0:T(8,128)(2,1)}, u32[]{:S(2)}, u32[]{:S(2)}) collective-permute-start(bf16[512,2048]{1,0:T(8,128)(2,1)} %add_convert_fusion), channel_id=1, source_target_pairs={{0,1},{1,0},{2,3},{3,2},{4,5},{5,4},{6,7},{7,6},{8,9},{9,8},{10,11... | collective-permute-start | bytes 6291464 | tf_op jit(solution)/shard_map/ppermute | solution.py:644
  459.8 75.0 %collective-permute-start.37 = (bf16[8,128,1408]{2,1,0:T(8,128)(2,1)}, bf16[8,128,1408]{2,1,0:T(8,128)(2,1)}, u32[]{:S(2)}, u32[]{:S(2)}) collective-permute-start(bf16[8,128,1408]{2,1,0:T(8,128)(2,1)} %get-tuple-element.550), channel_id=1, source_target_pairs={{0,2},{1,3},{2,0},{3,1},{4,6},{5,7},{6,4},{7,5},{8,10},{9,11},{10,... | collective-permute-start | bytes 8650760 | tf_op jit(solution)/shard_map/ppermute | solution.py:647
  481.6 18.6 %collective-permute-start.31 = (bf16[2,2,64,1408]{3,2,1,0:T(8,128)(2,1)S(1)}, bf16[2,2,64,1408]{3,2,1,0:T(8,128)(2,1)S(1)}, u32[]{:S(2)}, u32[]{:S(2)}) collective-permute-start(bf16[2,2,64,1408]{3,2,1,0:T(8,128)(2,1)S(1)} %fusion.7), channel_id=1, source_target_pairs={{0,4},{4,8},{8,12},{12,0},{1,5},{5,9},{9,13},{13,1},{2,6},{6,10},{... | collective-permute-start | bytes 2162696 | tf_op jit(solution)/shard_map/ppermute | solution.py:650
  481.9 28.1 %collective-permute-start.34 = (bf16[512,1280]{1,0:T(8,128)(2,1)S(1)}, bf16[512,1280]{1,0:T(8,128)(2,1)S(1)}, u32[]{:S(2)}, u32[]{:S(2)}) collective-permute-start(bf16[512,1280]{1,0:T(8,128)(2,1)S(1)} %slice.28.c0), channel_id=1, source_target_pairs={{0,16},{16,0},{1,17},{17,1},{2,18},{18,2},{3,19},{19,3},{4,20},{20... | collective-permute-start | bytes 3932168 | tf_op jit(solution)/shard_map/ppermute | solution.py:641
  481.9 35.4 %collective-permute-start.33 = (bf16[512,1280]{1,0:T(8,128)(2,1)S(1)}, bf16[512,1280]{1,0:T(8,128)(2,1)S(1)}, u32[]{:S(2)}, u32[]{:S(2)}) collective-permute-start(bf16[512,1280]{1,0:T(8,128)(2,1)S(1)} %pad_maximum_fusion.c0), channel_id=1, source_target_pairs={{0,16},{16,0},{1,17},{17,1},{2,18},{18,2},{3,19},{19,3},{4,20},{20... | collective-permute-start | bytes 3932168 | tf_op jit(solution)/shard_map/ppermute | solution.py:641
  500.3 34.6 %collective-permute-start.36 = (bf16[4,2,64,1024]{3,2,1,0:T(8,128)(2,1)S(1)}, bf16[4,2,64,1024]{3,2,1,0:T(8,128)(2,1)S(1)}, u32[]{:S(2)}, u32[]{:S(2)}) collective-permute-start(bf16[4,2,64,1024]{3,2,1,0:T(8,128)(2,1)S(1)} %get-tuple-element.549), channel_id=1, source_target_pairs={{0,1},{1,0},{2,3},{3,2},{4,5},{5,4},{6,7},{7,6},{8,9},{9,8},{10,11... | collective-permute-start | bytes 3145736 | tf_op jit(solution)/shard_map/ppermute | solution.py:644
  500.6 48.4 %collective-permute-start.35 = (bf16[4,2,64,1024]{3,2,1,0:T(8,128)(2,1)S(1)}, bf16[4,2,64,1024]{3,2,1,0:T(8,128)(2,1)}, u32[]{:S(2)}, u32[]{:S(2)}) collective-permute-start(bf16[4,2,64,1024]{3,2,1,0:T(8,128)(2,1)S(1)} %get-tuple-element.548), channel_id=1, source_target_pairs={{0,1},{1,0},{2,3},{3,2},{4,5},{5,4},{6,7},{7,6},{8,9},{9,8},{10,11... | collective-permute-start | bytes 3145736 | tf_op jit(solution)/shard_map/ppermute | solution.py:644
  529.8 32.1 %collective-permute-start.40 = (bf16[4,2,64,1280]{3,2,1,0:T(8,128)(2,1)}, bf16[4,2,64,1280]{3,2,1,0:T(8,128)(2,1)}, u32[]{:S(2)}, u32[]{:S(2)}) collective-permute-start(bf16[4,2,64,1280]{3,2,1,0:T(8,128)(2,1)} %get-tuple-element.561), channel_id=1, source_target_pairs={{0,2},{1,3},{2,0},{3,1},{4,6},{5,7},{6,4},{7,5},{8,10},{9,11},{10,... | collective-permute-start | bytes 3932168 | tf_op jit(solution)/shard_map/ppermute | solution.py:647
  531.4 42.5 %collective-permute-start.39 = (bf16[4,2,64,1280]{3,2,1,0:T(8,128)(2,1)}, bf16[4,2,64,1280]{3,2,1,0:T(8,128)(2,1)}, u32[]{:S(2)}, u32[]{:S(2)}) collective-permute-start(bf16[4,2,64,1280]{3,2,1,0:T(8,128)(2,1)} %get-tuple-element.560), channel_id=1, source_target_pairs={{0,1},{1,0},{2,3},{3,2},{4,5},{5,4},{6,7},{7,6},{8,9},{9,8},{10,11... | collective-permute-start | bytes 3932168 | tf_op jit(solution)/shard_map/ppermute | solution.py:644
  534.9 45.2 %collective-permute-start.44 = (bf16[2,2,64,1408]{3,2,1,0:T(8,128)(2,1)}, bf16[2,2,64,1408]{3,2,1,0:T(8,128)(2,1)}, u32[]{:S(2)}, u32[]{:S(2)}) collective-permute-start(bf16[2,2,64,1408]{3,2,1,0:T(8,128)(2,1)} %fusion.2), channel_id=1, source_target_pairs={{0,4},{4,8},{8,12},{12,0},{1,5},{5,9},{9,13},{13,1},{2,6},{6,10},{... | collective-permute-start | bytes 2162696 | tf_op jit(solution)/shard_map/ppermute | solution.py:650
  536.0 43.0 %collective-permute-start.46 = (bf16[4,64,1024]{2,1,0:T(8,128)(2,1)}, bf16[4,64,1024]{2,1,0:T(8,128)(2,1)}, u32[]{:S(2)}, u32[]{:S(2)}) collective-permute-start(bf16[4,64,1024]{2,1,0:T(8,128)(2,1)} %fusion.21), channel_id=1, source_target_pairs={{0,2},{1,3},{2,0},{3,1},{4,6},{5,7},{6,4},{7,5},{8,10},{9,11},{10,... | collective-permute-start | bytes 1572872 | tf_op jit(solution)/shard_map/ppermute | solution.py:647
  551.4 25.9 %collective-permute-start.38 = (bf16[2,2,64,1408]{3,2,1,0:T(8,128)(2,1)}, bf16[2,2,64,1408]{3,2,1,0:T(8,128)(2,1)}, u32[]{:S(2)}, u32[]{:S(2)}) collective-permute-start(bf16[2,2,64,1408]{3,2,1,0:T(8,128)(2,1)} %fusion.16), channel_id=1, source_target_pairs={{0,4},{4,8},{8,12},{12,0},{1,5},{5,9},{9,13},{13,1},{2,6},{6,10},{... | collective-permute-start | bytes 2162696 | tf_op jit(solution)/shard_map/ppermute | solution.py:650
  552.1 110.8 %all-to-all-start = ((f32[32,1,128]{2,1,0:T(1,128)}), f32[32,1,128]{2,1,0:T(1,128)S(1)}, u32[]{:S(2)}, u32[]{:S(2)}) async-start(f32[32,1,128]{2,1,0:T(1,128)} %bitcast.21), calls=%async_computation | async-start | bytes 32768 | tf_op jit(solution)/shard_map/all_to_all | solution.py:1036
  561.9 18.2 %collective-permute-start.45 = (bf16[2,64,1024]{2,1,0:T(8,128)(2,1)S(1)}, bf16[2,64,1024]{2,1,0:T(8,128)(2,1)S(1)}, u32[]{:S(2)}, u32[]{:S(2)}) collective-permute-start(bf16[2,64,1024]{2,1,0:T(8,128)(2,1)S(1)} %fusion.36), channel_id=1, source_target_pairs={{0,4},{4,8},{8,12},{12,0},{1,5},{5,9},{9,13},{13,1},{2,6},{6,10},{... | collective-permute-start | bytes 786440 | tf_op jit(solution)/shard_map/ppermute | solution.py:650
  575.4 15.0 %collective-permute-start.43 = (bf16[4,64,1280]{2,1,0:T(8,128)(2,1)S(1)}, bf16[4,64,1280]{2,1,0:T(8,128)(2,1)S(1)}, u32[]{:S(2)}, u32[]{:S(2)}) collective-permute-start(bf16[4,64,1280]{2,1,0:T(8,128)(2,1)S(1)} %fusion.20), channel_id=1, source_target_pairs={{0,1},{1,0},{2,3},{3,2},{4,5},{5,4},{6,7},{7,6},{8,9},{9,8},{10,11... | collective-permute-start | bytes 1966088 | tf_op jit(solution)/shard_map/ppermute | solution.py:644
  577.3 13.6 %collective-permute-start.42 = (bf16[4,64,1280]{2,1,0:T(8,128)(2,1)S(1)}, bf16[4,64,1280]{2,1,0:T(8,128)(2,1)S(1)}, u32[]{:S(2)}, u32[]{:S(2)}) collective-permute-start(bf16[4,64,1280]{2,1,0:T(8,128)(2,1)S(1)} %fusion.19), channel_id=1, source_target_pairs={{0,2},{1,3},{2,0},{3,1},{4,6},{5,7},{6,4},{7,5},{8,10},{9,11},{10,... | collective-permute-start | bytes 1966088 | tf_op jit(solution)/shard_map/ppermute | solution.py:647
  580.0 24.0 %collective-permute-start.52 = (bf16[64,1024]{1,0:T(8,128)(2,1)S(1)}, bf16[64,1024]{1,0:T(8,128)(2,1)S(1)}, u32[]{:S(2)}, u32[]{:S(2)}) collective-permute-start(bf16[64,1024]{1,0:T(8,128)(2,1)S(1)} %fusion.44), channel_id=1, source_target_pairs={{0,4},{4,8},{8,12},{12,0},{1,5},{5,9},{9,13},{13,1},{2,6},{6,10},{... | collective-permute-start | bytes 393224 | tf_op jit(solution)/shard_map/ppermute | solution.py:650
  581.7 22.0 %collective-permute-start.41 = (bf16[2,2,64,1408]{3,2,1,0:T(8,128)(2,1)S(1)}, bf16[2,2,64,1408]{3,2,1,0:T(8,128)(2,1)S(1)}, u32[]{:S(2)}, u32[]{:S(2)}) collective-permute-start(bf16[2,2,64,1408]{3,2,1,0:T(8,128)(2,1)S(1)} %fusion.3), channel_id=1, source_target_pairs={{0,4},{4,8},{8,12},{12,0},{1,5},{5,9},{9,13},{13,1},{2,6},{6,10},{... | collective-permute-start | bytes 2162696 | tf_op jit(solution)/shard_map/ppermute | solution.py:650
  582.9 26.5 %collective-permute-start.51 = (bf16[2,64,1024]{2,1,0:T(8,128)(2,1)S(1)}, bf16[2,64,1024]{2,1,0:T(8,128)(2,1)S(1)}, u32[]{:S(2)}, u32[]{:S(2)}) collective-permute-start(bf16[2,64,1024]{2,1,0:T(8,128)(2,1)S(1)} %fusion.23), channel_id=1, source_target_pairs={{0,4},{4,8},{8,12},{12,0},{1,5},{5,9},{9,13},{13,1},{2,6},{6,10},{... | collective-permute-start | bytes 786440 | tf_op jit(solution)/shard_map/ppermute | solution.py:650
  590.3 19.0 %collective-permute-start.50 = (bf16[2,64,1408]{2,1,0:T(8,128)(2,1)S(1)}, bf16[2,64,1408]{2,1,0:T(8,128)(2,1)S(1)}, u32[]{:S(2)}, u32[]{:S(2)}) collective-permute-start(bf16[2,64,1408]{2,1,0:T(8,128)(2,1)S(1)} %get-tuple-element.648), channel_id=1, source_target_pairs={{0,1},{1,0},{2,3},{3,2},{4,5},{5,4},{6,7},{7,6},{8,9},{9,8},{10,11... | collective-permute-start | bytes 1081352 | tf_op jit(solution)/shard_map/ppermute | solution.py:644
  591.9 19.9 %collective-permute-start.49 = (bf16[64,1280]{1,0:T(8,128)(2,1)S(1)}, bf16[64,1280]{1,0:T(8,128)(2,1)S(1)}, u32[]{:S(2)}, u32[]{:S(2)}) collective-permute-start(bf16[64,1280]{1,0:T(8,128)(2,1)S(1)} %fusion.34), channel_id=1, source_target_pairs={{0,4},{4,8},{8,12},{12,0},{1,5},{5,9},{9,13},{13,1},{2,6},{6,10},{... | collective-permute-start | bytes 491528 | tf_op jit(solution)/shard_map/ppermute | solution.py:650
  603.7 9.9 %collective-permute-start.48 = (bf16[64,1280]{1,0:T(8,128)(2,1)S(1)}, bf16[64,1280]{1,0:T(8,128)(2,1)S(1)}, u32[]{:S(2)}, u32[]{:S(2)}) collective-permute-start(bf16[64,1280]{1,0:T(8,128)(2,1)S(1)} %fusion.35), channel_id=1, source_target_pairs={{0,4},{4,8},{8,12},{12,0},{1,5},{5,9},{9,13},{13,1},{2,6},{6,10},{... | collective-permute-start | bytes 491528 | tf_op jit(solution)/shard_map/ppermute | solution.py:650
  605.0 30.9 %collective-permute-start.58 = (bf16[64,1024]{1,0:T(8,128)(2,1)S(1)}, bf16[64,1024]{1,0:T(8,128)(2,1)S(1)}, u32[]{:S(2)}, u32[]{:S(2)}) collective-permute-start(bf16[64,1024]{1,0:T(8,128)(2,1)S(1)} %fusion.43), channel_id=1, source_target_pairs={{0,4},{4,8},{8,12},{12,0},{1,5},{5,9},{9,13},{13,1},{2,6},{6,10},{... | collective-permute-start | bytes 393224 | tf_op jit(solution)/shard_map/ppermute | solution.py:650
  615.0 20.9 %collective-permute-start.47 = (bf16[2,2,64,1408]{3,2,1,0:T(8,128)(2,1)S(1)}, bf16[2,2,64,1408]{3,2,1,0:T(8,128)(2,1)S(1)}, u32[]{:S(2)}, u32[]{:S(2)}) collective-permute-start(bf16[2,2,64,1408]{3,2,1,0:T(8,128)(2,1)S(1)} %fusion.4), channel_id=1, source_target_pairs={{0,4},{4,8},{8,12},{12,0},{1,5},{5,9},{9,13},{13,1},{2,6},{6,10},{... | collective-permute-start | bytes 2162696 | tf_op jit(solution)/shard_map/ppermute | solution.py:650
  616.1 24.9 %collective-permute-start.57 = (bf16[2,64,1024]{2,1,0:T(8,128)(2,1)S(1)}, bf16[2,64,1024]{2,1,0:T(8,128)(2,1)S(1)}, u32[]{:S(2)}, u32[]{:S(2)}) collective-permute-start(bf16[2,64,1024]{2,1,0:T(8,128)(2,1)S(1)} %fusion.22), channel_id=1, source_target_pairs={{0,4},{4,8},{8,12},{12,0},{1,5},{5,9},{9,13},{13,1},{2,6},{6,10},{... | collective-permute-start | bytes 786440 | tf_op jit(solution)/shard_map/ppermute | solution.py:650
  617.3 23.7 %collective-permute-start.56 = (bf16[64,2816]{1,0:T(8,128)(2,1)S(1)}, bf16[64,2816]{1,0:T(8,128)(2,1)S(1)}, u32[]{:S(2)}, u32[]{:S(2)}) collective-permute-start(bf16[64,2816]{1,0:T(8,128)(2,1)S(1)} %get-tuple-element.646), channel_id=1, source_target_pairs={{0,16},{16,0},{1,17},{17,1},{2,18},{18,2},{3,19},{19,3},{4,20},{20... | collective-permute-start | bytes 1081352 | tf_op jit(solution)/shard_map/ppermute | solution.py:641
  618.4 24.4 %collective-permute-start.55 = (bf16[64,1280]{1,0:T(8,128)(2,1)S(1)}, bf16[64,1280]{1,0:T(8,128)(2,1)S(1)}, u32[]{:S(2)}, u32[]{:S(2)}) collective-permute-start(bf16[64,1280]{1,0:T(8,128)(2,1)S(1)} %fusion.31), channel_id=1, source_target_pairs={{0,4},{4,8},{8,12},{12,0},{1,5},{5,9},{9,13},{13,1},{2,6},{6,10},{... | collective-permute-start | bytes 491528 | tf_op jit(solution)/shard_map/ppermute | solution.py:650
  635.9 8.6 %collective-permute-start.54 = (bf16[64,1280]{1,0:T(8,128)(2,1)S(1)}, bf16[64,1280]{1,0:T(8,128)(2,1)S(1)}, u32[]{:S(2)}, u32[]{:S(2)}) collective-permute-start(bf16[64,1280]{1,0:T(8,128)(2,1)S(1)} %fusion.33), channel_id=1, source_target_pairs={{0,4},{4,8},{8,12},{12,0},{1,5},{5,9},{9,13},{13,1},{2,6},{6,10},{... | collective-permute-start | bytes 491528 | tf_op jit(solution)/shard_map/ppermute | solution.py:650
  637.0 16.5 %collective-permute-start.63 = (bf16[64,1024]{1,0:T(8,128)(2,1)S(1)}, bf16[64,1024]{1,0:T(8,128)(2,1)S(1)}, u32[]{:S(2)}, u32[]{:S(2)}) collective-permute-start(bf16[64,1024]{1,0:T(8,128)(2,1)S(1)} %fusion.38), channel_id=1, source_target_pairs={{0,4},{4,8},{8,12},{12,0},{1,5},{5,9},{9,13},{13,1},{2,6},{6,10},{... | collective-permute-start | bytes 393224 | tf_op jit(solution)/shard_map/ppermute | solution.py:650
  646.0 7.5 %collective-permute-start.53 = (bf16[2,64,1408]{2,1,0:T(8,128)(2,1)S(1)}, bf16[2,64,1408]{2,1,0:T(8,128)(2,1)S(1)}, u32[]{:S(2)}, u32[]{:S(2)}) collective-permute-start(bf16[2,64,1408]{2,1,0:T(8,128)(2,1)S(1)} %get-tuple-element.644), channel_id=1, source_target_pairs={{0,1},{1,0},{2,3},{3,2},{4,5},{5,4},{6,7},{7,6},{8,9},{9,8},{10,11... | collective-permute-start | bytes 1081352 | tf_op jit(solution)/shard_map/ppermute | solution.py:644
  648.1 6.4 collective-permute-start.62
  649.7 7.2 %collective-permute-start.61 = (bf16[64,1280]{1,0:T(8,128)(2,1)S(1)}, bf16[64,1280]{1,0:T(8,128)(2,1)S(1)}, u32[]{:S(2)}, u32[]{:S(2)}) collective-permute-start(bf16[64,1280]{1,0:T(8,128)(2,1)S(1)} %fusion.25), channel_id=1, source_target_pairs={{0,4},{4,8},{8,12},{12,0},{1,5},{5,9},{9,13},{13,1},{2,6},{6,10},{... | collective-permute-start | bytes 491528 | tf_op jit(solution)/shard_map/ppermute | solution.py:650
  650.8 7.8 %collective-permute-start.60 = (bf16[64,1280]{1,0:T(8,128)(2,1)S(1)}, bf16[64,1280]{1,0:T(8,128)(2,1)S(1)}, u32[]{:S(2)}, u32[]{:S(2)}) collective-permute-start(bf16[64,1280]{1,0:T(8,128)(2,1)S(1)} %fusion.28), channel_id=1, source_target_pairs={{0,4},{4,8},{8,12},{12,0},{1,5},{5,9},{9,13},{13,1},{2,6},{6,10},{... | collective-permute-start | bytes 491528 | tf_op jit(solution)/shard_map/ppermute | solution.py:650
  (111 other events, 1222.8 us)

commit v3 on v2

--- a/solution.py
+++ b/solution.py
@@ -479,17 +479,17 @@
     low_ref[...] = narrow
     for k, copy in enumerate(copies):
 
-        @pl.when(pl.program_id(0) // 2 == k)
+        @pl.when(pl.program_id(0) == k)
         def _(copy=copy):
             copy[...] = narrow
 
-    mixed_ref[...] = mm(narrow, w[...], NT)
+    mixed_ref[...] = mm(narrow, w[...], NT).astype(bf16)
 
 
 def norm_back(low, near, far, middle, seed, gain, w):
     count, width = middle.shape
-    tile = min(128, count // 2)
-    halves = count // (2 * tile)
+    tile = min(256, count)
+    halves = count // tile
     row = pl.BlockSpec((tile, width), lambda i: (i, 0))
 
     def held(shape):
@@ -502,17 +502,16 @@
         out_specs=[row] * 3
         + [pl.BlockSpec((8, width), lambda i: (0, 0))]
         + [
-            pl.BlockSpec((tile, width), lambda i, k=k: (jnp.clip(i - 2 * k, 0, 1), 0))
-            for k in range(halves)
+            pl.BlockSpec((tile, width), lambda i: (0, 0)) for _ in range(halves)
         ],
         out_shape=[
             sds((count, width), f32),
             sds((count, width), bf16),
-            sds((count, width), f32),
+            sds((count, width), bf16),
             sds((8, width), f32),
-            *[sds((2 * tile, width), bf16)] * halves,
+            *[sds((tile, width), bf16)] * halves,
         ],
-        compiler_params=params(VMEM_MIB),
+        compiler_params=params(50),
         cost_estimate=FREE,
     )(low, near, far, middle, seed, gain.reshape(1, width), w)
 
@@ -649,6 +648,12 @@
     def over_seq(a, shift=1):
         return lax.ppermute(a, "seq", [(s, (s + shift) % nseq) for s in range(nseq)])
 
+    depth = nseq.bit_length() - 1
+    assert nseq == 1 << depth
+
+    def over_bit(k, a):
+        return lax.ppermute(a, "seq", [(s, s ^ (1 << k)) for s in range(nseq)])
+
     def hops(state):
         states = []
         for _ in range(nseq - 1):
@@ -921,8 +926,11 @@
             dim = dims.pop(name)
             dims = {k: v - (v > dim) for k, v in dims.items()}
             if name == "seq":
-                now = terms
-                terms = yield from ring_step(lambda b: take(now, dim, b))
+                terms = [t.reshape(*t.shape[:dim], *[2] * depth, *t.shape[dim + 1 :]) for t in terms]
+                for k in range(depth):
+                    terms = yield from pair_step(
+                        terms, dim + depth - 1 - k, (si >> k) & 1, functools.partial(over_bit, k)
+                    )
             else:
                 bit, swap = {"x": (xb, over_x), "y": (yb, over_y)}[name]
                 terms = yield from pair_step(terms, dim, bit, swap)
@@ -1004,9 +1012,8 @@
         grad_values_low[:, :half],
         jnp.concatenate([grad_values_low[:, half:], grad_queries, grad_keys], axis=-1),
     )
+    up.step()
     grad_all1 = [over_feat(g) for g in grad_all]
-    gate.step()
-    layer_out = fence(middle + total_of([lay0, jnp.concatenate(lay1), fence(far_lay)]))
     inner = []
     for own, other, (along_x, order) in zip(
         grad_all, grad_all1, ((False, ("x", "seq")), (True, ("y", "seq")))
@@ -1015,6 +1022,8 @@
             *core_grad(bits, low_one, low_one1, own, [fence(other)], 0, 1, nseq, along_x)
         )
         inner.append(Task(line, share(pieces, along_x, order)))
+    gate.step()
+    layer_out = fence(middle + total_of([lay0, jnp.concatenate(lay1), fence(far_lay)]))
     grad_low_one = fence(
         mm(fence(grad_queries), w_query, NT)
         + mm(grad_keys, w_key, NT)

time: 674 us -> 666 us (0.988)
  waiting for transfers between devices: 130 us -> 98.1 us
  starting transfers between devices: 46.1 us -> 56.7 us
  local copies, waits for them, and re-layouts: 52.3 us -> 60.1 us
    ppermute x24 -> x12, waiting for transfers between devices: 66.6 us -> 27.9 us  [over_seq(): lax.ppermute(a, 'seq', [(s, (s + shift) % nseq) for s in range(nseq)])]
    ppermute x0 -> x8, waiting for transfers between devices: none -> 21.5 us  [over_bit(): return lax.ppermute(a, 'seq', [(s, s ^ 1 << k) for s in range(nseq)])]
    ppermute x10, waiting for transfers between devices: 43 us -> 26.3 us  [over_x(): return lax.ppermute(a, 'rows', [(r, r ^ 1) for r in range(nrows)])]
    ppermute x0 -> x8, starting transfers between devices: none -> 9.09 us  [over_bit(): return lax.ppermute(a, 'seq', [(s, s ^ 1 << k) for s in range(nseq)])]
    convert_element_type x30 -> x26, other arithmetic: 49.7 us -> 48.5 us  [low_sum(): return total_of(terms).astype(bf16)]
    unnamed x220 -> x254, local copies, waits for them, and re-layouts: 48.3 us -> 47.2 us
  transfers between devices with their start and end apart: 65 -> 61, of which waited for: 26 -> 21; matrix products, arithmetic and copies ran while one was open for 16% -> 18% of each run, Pallas kernels for 41% -> 41%
where the time goes in v3:
time: 666 us; the launch traced here: 657 us
  Pallas kernels  317 us (48%)
  waiting for transfers between devices  98.1 us (15%)
  other arithmetic  87.4 us (13%)
  local copies, waits for them, and re-layouts  60.1 us (9%)
  starting transfers between devices  56.7 us (9%)
  matrix products  33 us (5%)
    pallas_call x8, Pallas kernels, token_call(): pl.pallas_call(functools.partial(kernel, half), grid_spec=pltpu.PrefetchS...  125 us
    pallas_call x7, Pallas kernels, head_call(): pl.pallas_call(body, grid=(last - first,), in_specs=[spec(kind, a.shape)...  99.9 us
    convert_element_type x26, other arithmetic, low_sum(): return total_of(terms).astype(bf16)  48.5 us
    unnamed x254, local copies, waits for them, and re-layouts  47.2 us
    pallas_call x2, Pallas kernels, wide_grad(): pl.pallas_call(wide_grad_kernel, grid_spec=pltpu.PrefetchScalarGridSpec(n...  33.6 us
    dot_general x7, matrix products, mm(): return lax.dot_general(a, b, dims, preferred_element_type=f32)  33 us
    ppermute x12, waiting for transfers between devices, over_seq(): lax.ppermute(a, 'seq', [(s, (s + shift) % nseq) for s in range(nseq)])  27.9 us
    ppermute x10, waiting for transfers between devices, over_x(): return lax.ppermute(a, 'rows', [(r, r ^ 1) for r in range(nrows)])  26.3 us
  transfers between devices with their start and end apart: 61, of which 21 were waited for; matrix products, arithmetic and copies ran while one was open for 18% of the time, Pallas kernels for 41%

profile of v3, /device:TPU:0, one launch (start us, length us, event | category | flops | bytes accessed | tf_op | source)
XLA Modules:
  0.0 656.6 jit_solution(1695828623174244999)
XLA Ops:
  0.7 4.0 bitcast_convert_fusion.g0
  7.1 2.6 collective-permute-start.5
  17.9 8.7 %convolution_convert_fusion.refs_4_.refs_5_ = bf16[512,2048]{1,0:T(8,128)(2,1)S(1)} fusion(bf16[512,2048]{1,0:T(8,128)(2,1)} %multiply_convert_fusion.1.r0, bf16[2048,2048]{1,0:T(8,128)(2,1)} %param.20), kind=kOutput, calls=%fused_computation.14 | convolution fusion | flops 4296015872 | bytes 12582912 | tf_op jit(solution)/shard_map/dot_general | solution.py:41
  26.7 9.2 %shard_map.230 = bf16[16,160,128]{2,1,0:T(8,128)(2,1)S(1)} custom-call(bf16[16,256,256]{2,1,0:T(8,128)(2,1)S(1)} %copy-done.1, bf16[16,256,256]{2,1,0:T(8,128)(2,1)S(1)} %copy-done.2, f32[8,256]{1,0:T(8,128)S(1)} %copy-done.83, bf16[512,256]{1,0:T(8,128)(2,1)S(1)} %convolution_convert_fusion.2.refs_3_.refs_4_, ...), custom_call_target="tpu_custom_call" | custom-call | tf_op jit(solution)/shard_map/pallas_call | solution.py:291
  37.8 2.7 convolution_convert_fusion.1.refs_3_
  40.5 18.0 %shard_map.231 = (f32[512,2048]{1,0:T(8,128)S(1)}, f32[512,128]{1,0:T(8,128)S(1)}, bf16[16,512,256]{2,1,0:T(8,128)(2,1)S(1)}) custom-call(bf16[16,256,256]{2,1,0:T(8,128)(2,1)S(1)} %copy-done.1, bf16[16,256,256]{2,1,0:T(8,128)(2,1)S(1)} %copy-done.2, f32[8,256]{1,0:T(8,128)S(1)} %copy-done.83, bf16[512,256]{1,0:T(8,128)(2,1)S(1)} %convolution_convert_fusion.1.refs_3_, ...), custom_call_target="tpu_custom_call" | custom-call | tf_op jit(solution)/shard_map/pallas_call | solution.py:291
  64.9 10.7 %shard_map.232.grad_ref = bf16[1024,1408]{1,0:T(8,128)(2,1)S(1)} custom-call(s32[1]{0:T(128)} %bitcast.4.which_ref, bf16[512,2048]{1,0:T(8,128)(2,1)} %bitcast_convert_fusion.g0, bf16[512,2048]{1,0:T(8,128)(2,1)} %collective-permute-done.2.g1, bf16[5632,2048]{1,0:T(8,128)(2,1)} %wd.7), custom_call_target="tpu_custom_call" | custom-call | tf_op jit(solution)/shard_map/pallas_call | solution.py:377
  75.6 6.5 collective-permute-done.1.refs_6_
  83.2 3.3 collective-permute-done.6.g1.g3
  86.5 11.1 %shard_map.233.grad_ref = bf16[1024,1408]{1,0:T(8,128)(2,1)S(1)} custom-call(s32[1]{0:T(128)} %bitcast.4.which_ref, bf16[512,2048]{1,0:T(8,128)(2,1)} %collective-permute-done.5.g0.g2, bf16[512,2048]{1,0:T(8,128)(2,1)S(1)} %collective-permute-done.6.g1.g3, bf16[5632,2048]{1,0:T(8,128)(2,1)} %wd.7), custom_call_target="tpu_custom_call" | custom-call | tf_op jit(solution)/shard_map/pallas_call | solution.py:377
  97.6 3.8 collective-permute-done.4.refs_7_
  101.6 11.9 %shard_map.234 = (bf16[512,2048]{1,0:T(8,128)(2,1)S(1)}, f32[512,128]{1,0:T(8,128)S(1)}, f32[16,160,128]{2,1,0:T(8,128)S(1)}) custom-call(f32[3]{0:T(128)S(1)} %and_convert_fusion.refs_0_, bf16[16,512,256]{2,1,0:T(8,128)(2,1)S(1)} %copy-done.16, f32[512,2048]{1,0:T(8,128)S(1)} %copy-done.52, f32[512,128]{1,0:T(8,128)S(1)} %copy-done.82, ...), custom_call_target="tpu_custom_call" | custom-call | tf_op jit(solution)/shard_map/pallas_call | solution.py:291
  113.6 8.4 %multiply_reduce_fusion.2 = (f32[512]{0:T(512)S(1)}, f32[512,2048]{1,0:T(8,128)S(1)}) fusion(bf16[512,2048]{1,0:T(8,128)(2,1)S(1)} %get-tuple-element.490.refs_2_.r0, bf16[2048,2048]{1,0:T(8,128)(2,1)} %w.1, f32[1,512,2048]{2,1,0:T(8,128)S(1)} %copy-done.90), kind=kOutput, calls=%fused_computation.12 | convolution fusion | flops 4298112512 | bytes 18876416 | tf_op jit(solution)/shard_map/dot_general | solution.py:41
  125.1 3.1 collective-permute-done.8.x1.l1
  128.2 3.0 collective-permute-done.7.r1
  132.5 19.1 %shard_map.235 = (bf16[1024,1408]{1,0:T(8,128)(2,1)S(1)}, bf16[1024,1408]{1,0:T(8,128)(2,1)S(1)}, bf16[1024,1408]{1,0:T(8,128)(2,1)S(1)}) custom-call(s32[1]{0:T(128)} %bitcast.4.which_ref, bf16[512,2048]{1,0:T(8,128)(2,1)S(1)} %multiply_convert_fusion.x0.l0, bf16[512,2048]{1,0:T(8,128)(2,1)S(1)} %collective-permute-done.8.x1.l1, ...), custom_call_target="tpu_custom_call" | custom-call | tf_op jit(solution)/shard_map/pallas_call | solution.py:377
  153.1 21.6 %shard_map.236 = (bf16[512,2048]{1,0:T(8,128)(2,1)S(1)}, bf16[512,2048]{1,0:T(8,128)(2,1)}) custom-call(s32[1]{0:T(128)} %bitcast.4.which_ref, bf16[1024,1408]{1,0:T(8,128)(2,1)S(1)} %get-tuple-element.383.gg.near, bf16[1024,1408]{1,0:T(8,128)(2,1)S(1)} %get-tuple-element.395.gu.near, bf16[2048,5632]{1,0:T(8,128)(2,1)} %wg.7, bf16[2048,5632]{1,0:T(8,128)(2,1)} %wu.7), custom_call_target="tpu_custom_call" | custom-call | tf_op jit(solution)/shard_map/pallas_call | solution.py:377
  176.7 4.0 collective-permute-done.10.x1.l3
  180.7 3.0 collective-permute-done.11.near
  185.5 20.0 %shard_map.237 = (bf16[1024,1408]{1,0:T(8,128)(2,1)S(1)}, bf16[1024,1408]{1,0:T(8,128)(2,1)S(1)}, bf16[1024,1408]{1,0:T(8,128)(2,1)S(1)}) custom-call(s32[1]{0:T(128)} %bitcast.4.which_ref, bf16[512,2048]{1,0:T(8,128)(2,1)} %collective-permute-done.9.x0.l2, bf16[512,2048]{1,0:T(8,128)(2,1)} %collective-permute-done.10.x1.l3, ...), custom_call_target="tpu_custom_call" | custom-call | tf_op jit(solution)/shard_map/pallas_call | solution.py:377
  207.1 16.8 %shard_map.238 = (bf16[2,352,2048]{2,1,0:T(8,128)(2,1)S(1)}, bf16[2,352,2048]{2,1,0:T(8,128)(2,1)S(1)}) custom-call(s32[1]{0:T(128)} %bitcast.5.ybit_ref, bf16[1024,1408]{1,0:T(8,128)(2,1)S(1)} %copy-done.24, bf16[1024,1408]{1,0:T(8,128)(2,1)S(1)} %get-tuple-element.439.far.hid, bf16[512,2048]{1,0:T(8,128)(2,1)} %bitcast_convert_fusion.g0, ...), custom_call_target="tpu_custom_call" | custom-call | tf_op jit(solution)/shard_map/pallas_call | solution.py:450
  227.0 2.4 copy-done.34
  229.4 18.9 %shard_map.239 = (bf16[512,2048]{1,0:T(8,128)(2,1)S(1)}, bf16[256,2048]{1,0:T(8,128)(2,1)S(1)}, bf16[256,2048]{1,0:T(8,128)(2,1)S(1)}) custom-call(s32[1]{0:T(128)} %bitcast.4.which_ref, bf16[1024,1408]{1,0:T(8,128)(2,1)S(1)} %copy-done.34, bf16[1024,1408]{1,0:T(8,128)(2,1)S(1)} %get-tuple-element.377.gu.far, bf16[2048,5632]{1,0:T(8,128)(2,1)} %wg.7, ...), custom_call_target="tpu_custom_call" | custom-call | tf_op jit(solution)/shard_map/pallas_call | solution.py:377
  250.7 16.4 %shard_map.240 = (bf16[8,128,1408]{2,1,0:T(8,128)(2,1)S(1)}, bf16[8,128,1408]{2,1,0:T(8,128)(2,1)S(1)}) custom-call(s32[1]{0:T(128)} %bitcast.5.ybit_ref, bf16[512,2048]{1,0:T(8,128)(2,1)S(1)} %copy-done.9, bf16[512,2048]{1,0:T(8,128)(2,1)S(1)} %copy-done.14, bf16[512,2048]{1,0:T(8,128)(2,1)} %collective-permute-done.9.x0.l2, ...), custom_call_target="tpu_custom_call" | custom-call | tf_op jit(solution)/shard_map/pallas_call | solution.py:419
  272.6 17.2 %shard_map.241 = (bf16[8,128,1408]{2,1,0:T(8,128)(2,1)}, bf16[8,128,1408]{2,1,0:T(8,128)(2,1)S(1)}) custom-call(s32[1]{0:T(128)} %bitcast.5.ybit_ref, bf16[512,2048]{1,0:T(8,128)(2,1)S(1)} %copy-done.9, bf16[512,2048]{1,0:T(8,128)(2,1)S(1)} %copy-done.14, bf16[512,2048]{1,0:T(8,128)(2,1)} %collective-permute-done.9.x0.l2, ...), custom_call_target="tpu_custom_call" | custom-call | tf_op jit(solution)/shard_map/pallas_call | solution.py:419
  290.1 12.4 %shard_map.242 = (bf16[512,2048]{1,0:T(8,128)(2,1)S(1)}, bf16[256,2048]{1,0:T(8,128)(2,1)}, bf16[256,2048]{1,0:T(8,128)(2,1)}) custom-call(s32[1]{0:T(128)} %bitcast.4.which_ref, bf16[1024,1408]{1,0:T(8,128)(2,1)S(1)} %copy-done.24, bf16[5632,2048]{1,0:T(8,128)(2,1)} %wd.7), custom_call_target="tpu_custom_call" | custom-call | tf_op jit(solution)/shard_map/pallas_call | solution.py:377
  304.3 2.4 fusion.14
  307.7 11.3 %collective-permute-done.17.far = bf16[512,2048]{1,0:T(8,128)(2,1)} collective-permute-done((bf16[512,2048]{1,0:T(8,128)(2,1)}, bf16[512,2048]{1,0:T(8,128)(2,1)}, u32[]{:S(2)}, u32[]{:S(2)}) %collective-permute-start.17) | collective-permute-done | bytes 2097184 | tf_op jit(solution)/shard_map/ppermute | solution.py:643
  319.0 17.4 %shard_map.243 = (f32[512,2048]{1,0:T(8,128)}, bf16[512,2048]{1,0:T(8,128)(2,1)}, bf16[512,2048]{1,0:T(8,128)(2,1)}, f32[8,2048]{1,0:T(8,128)S(1)}, bf16[256,204...) custom-call(bf16[512,2048]{1,0:T(8,128)(2,1)} %copy-done.69, bf16[512,2048]{1,0:T(8,128)(2,1)} %collective-permute-done.11.near, ...), custom_call_target="tpu_custom_call" | custom-call | tf_op jit(solution)/shard_map/pallas_call | solution.py:498
  340.1 11.9 %shard_map.244 = (bf16[16,160,128]{2,1,0:T(8,128)(2,1)}, bf16[512,2048]{1,0:T(8,128)(2,1)S(1)}, f32[512,128]{1,0:T(8,128)S(1)}) custom-call(bf16[16,512,256]{2,1,0:T(8,128)(2,1)S(1)} %copy-done.17, bf16[512,2048]{1,0:T(8,128)(2,1)S(1)} %copy-done.68, bf16[512,2048]{1,0:T(8,128)(2,1)S(1)} %copy-done.11, f32[512,128]{1,0:T(8,128)S(1)} %copy-done.80, ...), custom_call_target="tpu_custom_call" | custom-call | tf_op jit(solution)/shard_map/pallas_call | solution.py:291
  355.6 2.7 fusion.9
  361.5 11.6 %shard_map.245 = (bf16[512,2048]{1,0:T(8,128)(2,1)S(1)}, bf16[256,2048]{1,0:T(8,128)(2,1)}, bf16[256,2048]{1,0:T(8,128)(2,1)}) custom-call(s32[1]{0:T(128)} %bitcast.4.which_ref, bf16[1024,1408]{1,0:T(8,128)(2,1)S(1)} %copy-done.22, bf16[5632,2048]{1,0:T(8,128)(2,1)} %wd.7), custom_call_target="tpu_custom_call" | custom-call | tf_op jit(solution)/shard_map/pallas_call | solution.py:377
  373.6 2.5 fusion.10
  377.7 8.4 %collective-permute-done.21 = bf16[176,2048]{1,0:T(8,128)(2,1)} collective-permute-done((bf16[176,2048]{1,0:T(8,128)(2,1)}, bf16[176,2048]{1,0:T(8,128)(2,1)}, u32[]{:S(2)}, u32[]{:S(2)}) %collective-permute-start.21) | collective-permute-done | bytes 720928 | tf_op jit(solution)/shard_map/ppermute | solution.py:649
  386.1 2.8 fusion.8
  399.9 16.0 %shard_map.246 = (f32[512,256]{1,0:T(8,128)S(1)}, f32[512,256]{1,0:T(8,128)S(1)}, f32[512,2048]{1,0:T(8,128)S(1)}) custom-call(bf16[16,256,256]{2,1,0:T(8,128)(2,1)S(1)} %copy-done.1, bf16[16,256,256]{2,1,0:T(8,128)(2,1)S(1)} %copy-done.3, f32[8,256]{1,0:T(8,128)S(1)} %copy-done.83, bf16[512,256]{1,0:T(8,128)(2,1)S(1)} %copy-done.60, ...), custom_call_target="tpu_custom_call" | custom-call | tf_op jit(solution)/shard_map/pallas_call | solution.py:291
  416.5 2.6 fusion.11
  426.1 2.7 collective-permute-start.27
  429.1 3.9 add_convert_fusion
  433.0 3.0 collective-permute-start.23
  436.0 4.9 shard_map.247
  441.0 6.1 shard_map.248
  447.1 15.8 %shard_map.249 = (f32[512,256]{1,0:T(8,128)S(1)}, f32[512,256]{1,0:T(8,128)S(1)}, f32[512,2048]{1,0:T(8,128)S(1)}) custom-call(bf16[16,256,256]{2,1,0:T(8,128)(2,1)S(1)} %copy-done.1, bf16[16,256,256]{2,1,0:T(8,128)(2,1)S(1)} %copy-done.4, f32[8,256]{1,0:T(8,128)S(1)} %copy-done.83, ...), custom_call_target="tpu_custom_call", output_to_operand_aliasing={{2}: (13, {})} | custom-call | tf_op jit(solution)/shard_map/pallas_call | solution.py:291
  463.9 17.0 %shard_map.250 = (bf16[512,256]{1,0:T(8,128)(2,1)S(1)}, bf16[512,2048]{1,0:T(8,128)(2,1)S(1)}) custom-call(f32[3]{0:T(128)S(1)} %broadcast_5_refs_0_.2.refs_0_, bf16[16,256,256]{2,1,0:T(8,128)(2,1)S(1)} %copy-done.1, bf16[16,256,256]{2,1,0:T(8,128)(2,1)S(1)} %copy-done.4, f32[8,256]{1,0:T(8,128)S(1)} %copy-done.83, ...), custom_call_target="tpu_custom_call" | custom-call | tf_op jit(solution)/shard_map/pallas_call | solution.py:291
  483.0 2.5 fusion.7
  485.8 9.4 %fusion.40 = f32[512,2048]{1,0:T(8,128)} fusion(bf16[512,2048]{1,0:T(8,128)(2,1)S(1)} %get-tuple-element.510, bf16[2048,2048]{1,0:T(8,128)(2,1)} %param.20), kind=kOutput, calls=%fused_computation.130 | convolution fusion | flops 4294967296 | bytes 14680064 | tf_op jit(solution)/shard_map/dot_general | solution.py:41
  497.3 6.2 shard_map.251
  503.5 2.6 fusion.16
  508.0 6.2 shard_map.252
  514.2 7.3 %add_add_fusion.1 = f32[512,2048]{1,0:T(8,128)} fusion(f32[512,2048]{1,0:T(8,128)} %copy-done.92, bf16[512,2048]{1,0:T(8,128)(2,1)} %collective-permute-done.23, bf16[512,2048]{1,0:T(8,128)(2,1)S(1)} %copy-done.65, bf16[256,2048]{1,0:T(8,128)(2,1)} %collective-permute-done.16, bf16[256,2048]{1,0:T(8,128)(2,1)} %collective-permute-done.15), kind=kLoop, calls=%fused_computation.8 | loop fusion | flops 9437184 | bytes 14680064 | tf_op jit(solution)/shard_map/add | solution.py:1026
  530.2 5.3 multiply_add_fusion
  539.7 4.0 collective-permute-done.36
  544.7 2.5 fusion.3
  556.0 3.4 collective-permute-done.41
  559.7 11.0 %collective-permute-done.40 = bf16[4,2,64,1280]{3,2,1,0:T(8,128)(2,1)} collective-permute-done((bf16[4,2,64,1280]{3,2,1,0:T(8,128)(2,1)}, bf16[4,2,64,1280]{3,2,1,0:T(8,128)(2,1)}, u32[]{:S(2)}, u32[]{:S(2)}) %collective-permute-start.40) | collective-permute-done | bytes 1310752 | tf_op jit(solution)/shard_map/ppermute | solution.py:643
  583.4 3.9 collective-permute-done.46
  589.2 2.3 collective-permute-done.43
  593.8 9.1 %collective-permute-done.42 = bf16[2,2,64,1408]{3,2,1,0:T(8,128)(2,1)S(1)} collective-permute-done((bf16[2,2,64,1408]{3,2,1,0:T(8,128)(2,1)S(1)}, bf16[2,2,64,1408]{3,2,1,0:T(8,128)(2,1)S(1)}, u32[]{:S(2)}, u32[]{:S(2)}) %collective-permute-start.42) | collective-permute-done | bytes 720928 | tf_op jit(solution)/shard_map/ppermute | solution.py:649
  612.6 3.8 collective-permute-start.59
  617.1 3.2 all-to-all-start
  623.0 5.4 collective-permute-done.49
  634.9 3.0 collective-permute-start.55
  640.3 8.2 %collective-permute-done.56 = bf16[64,1280]{1,0:T(8,128)(2,1)S(1)} collective-permute-done((bf16[64,1280]{1,0:T(8,128)(2,1)S(1)}, bf16[64,1280]{1,0:T(8,128)(2,1)S(1)}, u32[]{:S(2)}, u32[]{:S(2)}) %collective-permute-start.56) | collective-permute-done | bytes 163872 | tf_op jit(solution)/shard_map/ppermute | solution.py:655
  649.5 2.4 collective-permute-done.55
  (429 shorter events, 148.3 us)
Async XLA Ops:
  0.6 37.1 %copy-start = (bf16[2048,256]{1,0:T(8,128)(2,1)S(1)}, bf16[2048,256]{1,0:T(8,128)(2,1)}, u32[]{:S(2)}) copy-start(bf16[2048,256]{1,0:T(8,128)(2,1)} %param.18) | copy-start | bytes 3145732
  6.6 58.3 %collective-permute-start.2 = (bf16[512,2048]{1,0:T(8,128)(2,1)}, bf16[512,2048]{1,0:T(8,128)(2,1)}, u32[]{:S(2)}, u32[]{:S(2)}) collective-permute-start(bf16[512,2048]{1,0:T(8,128)(2,1)} %bitcast_convert_fusion.g0), channel_id=1, source_target_pairs={{0,16},{16,0},{1,17},{17,1},{2,18},{18,2},{3,19},{19,3},{4,20},{20... | collective-permute-start | bytes 6291464 | tf_op jit(solution)/shard_map/ppermute | solution.py:640
  7.1 75.0 %collective-permute-start.5 = (bf16[512,2048]{1,0:T(8,128)(2,1)}, bf16[512,2048]{1,0:T(8,128)(2,1)}, u32[]{:S(2)}, u32[]{:S(2)}) collective-permute-start(bf16[512,2048]{1,0:T(8,128)(2,1)} %bitcast_convert_fusion.g0), channel_id=1, source_target_pairs={{0,1},{1,0},{2,3},{3,2},{4,5},{5,4},{6,7},{7,6},{8,9},{9,8},{10,11... | collective-permute-start | bytes 6291464 | tf_op jit(solution)/shard_map/ppermute | solution.py:643
  11.8 53.1 %collective-permute-start.3 = (bf16[512,2048]{1,0:T(8,128)(2,1)}, bf16[512,2048]{1,0:T(8,128)(2,1)}, u32[]{:S(2)}, u32[]{:S(2)}) collective-permute-start(bf16[512,2048]{1,0:T(8,128)(2,1)} %multiply_convert_fusion.1.r0), channel_id=1, source_target_pairs={{0,16},{16,0},{1,17},{17,1},{2,18},{18,2},{3,19},{19,3},{4,20},{20... | collective-permute-start | bytes 6291464 | tf_op jit(solution)/shard_map/ppermute | solution.py:640
  35.9 27.3 %collective-permute-start = (bf16[16,160,128]{2,1,0:T(8,128)(2,1)S(1)}, bf16[16,160,128]{2,1,0:T(8,128)(2,1)}, u32[]{:S(2)}, u32[]{:S(2)}) collective-permute-start(bf16[16,160,128]{2,1,0:T(8,128)(2,1)S(1)} %shard_map.230), channel_id=1, source_target_pairs={{0,4},{4,8},{8,12},{12,0},{1,5},{5,9},{9,13},{13,1},{2,6},{6,10},{... | collective-permute-start | bytes 1966088 | tf_op jit(solution)/shard_map/ppermute | solution.py:649
  63.3 18.8 %collective-permute-start.1 = (bf16[16,160,128]{2,1,0:T(8,128)(2,1)}, bf16[16,160,128]{2,1,0:T(8,128)(2,1)}, u32[]{:S(2)}, u32[]{:S(2)}) collective-permute-start(bf16[16,160,128]{2,1,0:T(8,128)(2,1)} %collective-permute-done.refs_5_), channel_id=1, source_target_pairs={{0,4},{4,8},{8,12},{12,0},{1,5},{5,9},{9,13},{13,1},{2,6},{6,10},{... | collective-permute-start | bytes 1966088 | tf_op jit(solution)/shard_map/ppermute | solution.py:649
  82.1 4.4 collective-permute-start.6
  82.1 19.3 %collective-permute-start.4 = (bf16[16,160,128]{2,1,0:T(8,128)(2,1)}, bf16[16,160,128]{2,1,0:T(8,128)(2,1)S(1)}, u32[]{:S(2)}, u32[]{:S(2)}) collective-permute-start(bf16[16,160,128]{2,1,0:T(8,128)(2,1)} %collective-permute-done.1.refs_6_), channel_id=1, source_target_pairs={{0,4},{4,8},{8,12},{12,0},{1,5},{5,9},{9,13},{13,1},{2,6},{6,10},{... | collective-permute-start | bytes 1966088 | tf_op jit(solution)/shard_map/ppermute | solution.py:649
  124.0 4.2 collective-permute-start.8
  124.0 7.2 %collective-permute-start.7 = (bf16[512,2048]{1,0:T(8,128)(2,1)S(1)}, bf16[512,2048]{1,0:T(8,128)(2,1)S(1)}, u32[]{:S(2)}, u32[]{:S(2)}) collective-permute-start(bf16[512,2048]{1,0:T(8,128)(2,1)S(1)} %get-tuple-element.490.refs_2_.r0), channel_id=1, source_target_pairs={{0,16},{16,0},{1,17},{17,1},{2,18},{18,2},{3,19},{19,3},{4,20},{20... | collective-permute-start | bytes 6291464 | tf_op jit(solution)/shard_map/ppermute | solution.py:640
  124.5 51.6 %collective-permute-start.9 = (bf16[512,2048]{1,0:T(8,128)(2,1)S(1)}, bf16[512,2048]{1,0:T(8,128)(2,1)}, u32[]{:S(2)}, u32[]{:S(2)}) collective-permute-start(bf16[512,2048]{1,0:T(8,128)(2,1)S(1)} %multiply_convert_fusion.x0.l0), channel_id=1, source_target_pairs={{0,1},{1,0},{2,3},{3,2},{4,5},{5,4},{6,7},{7,6},{8,9},{9,8},{10,11... | collective-permute-start | bytes 6291464 | tf_op jit(solution)/shard_map/ppermute | solution.py:643
  176.1 4.5 collective-permute-start.10
  176.2 7.5 %collective-permute-start.11 = (bf16[512,2048]{1,0:T(8,128)(2,1)}, bf16[512,2048]{1,0:T(8,128)(2,1)}, u32[]{:S(2)}, u32[]{:S(2)}) collective-permute-start(bf16[512,2048]{1,0:T(8,128)(2,1)} %get-tuple-element.360), channel_id=1, source_target_pairs={{0,16},{16,0},{1,17},{17,1},{2,18},{18,2},{3,19},{19,3},{4,20},{20... | collective-permute-start | bytes 6291464 | tf_op jit(solution)/shard_map/ppermute | solution.py:640
  225.5 64.6 %collective-permute-start.12 = (bf16[2,352,2048]{2,1,0:T(8,128)(2,1)S(1)}, bf16[2,352,2048]{2,1,0:T(8,128)(2,1)}, u32[]{:S(2)}, u32[]{:S(2)}) collective-permute-start(bf16[2,352,2048]{2,1,0:T(8,128)(2,1)S(1)} %get-tuple-element.389), channel_id=1, source_target_pairs={{0,2},{1,3},{2,0},{3,1},{4,6},{5,7},{6,4},{7,5},{8,10},{9,11},{10,... | collective-permute-start | bytes 8650760 | tf_op jit(solution)/shard_map/ppermute | solution.py:646
  248.3 18.9 %collective-permute-start.13 = (bf16[256,2048]{1,0:T(8,128)(2,1)S(1)}, bf16[256,2048]{1,0:T(8,128)(2,1)S(1)}, u32[]{:S(2)}, u32[]{:S(2)}) collective-permute-start(bf16[256,2048]{1,0:T(8,128)(2,1)S(1)} %get-tuple-element.391), channel_id=1, source_target_pairs={{0,16},{16,0},{1,17},{17,1},{2,18},{18,2},{3,19},{19,3},{4,20},{20... | collective-permute-start | bytes 3145736 | tf_op jit(solution)/shard_map/ppermute | solution.py:640
  248.4 18.8 %collective-permute-start.14 = (bf16[256,2048]{1,0:T(8,128)(2,1)S(1)}, bf16[256,2048]{1,0:T(8,128)(2,1)S(1)}, u32[]{:S(2)}, u32[]{:S(2)}) collective-permute-start(bf16[256,2048]{1,0:T(8,128)(2,1)S(1)} %get-tuple-element.392), channel_id=1, source_target_pairs={{0,16},{16,0},{1,17},{17,1},{2,18},{18,2},{3,19},{19,3},{4,20},{20... | collective-permute-start | bytes 3145736 | tf_op jit(solution)/shard_map/ppermute | solution.py:640
  271.1 47.9 %collective-permute-start.17 = (bf16[512,2048]{1,0:T(8,128)(2,1)}, bf16[512,2048]{1,0:T(8,128)(2,1)}, u32[]{:S(2)}, u32[]{:S(2)}) collective-permute-start(bf16[512,2048]{1,0:T(8,128)(2,1)} %add_convert_fusion.1), channel_id=1, source_target_pairs={{0,1},{1,0},{2,3},{3,2},{4,5},{5,4},{6,7},{7,6},{8,9},{9,8},{10,11... | collective-permute-start | bytes 6291464 | tf_op jit(solution)/shard_map/ppermute | solution.py:643
  303.8 34.6 %collective-permute-start.15 = (bf16[256,2048]{1,0:T(8,128)(2,1)}, bf16[256,2048]{1,0:T(8,128)(2,1)}, u32[]{:S(2)}, u32[]{:S(2)}) collective-permute-start(bf16[256,2048]{1,0:T(8,128)(2,1)} %get-tuple-element.408), channel_id=1, source_target_pairs={{0,16},{16,0},{1,17},{17,1},{2,18},{18,2},{3,19},{19,3},{4,20},{20... | collective-permute-start | bytes 3145736 | tf_op jit(solution)/shard_map/ppermute | solution.py:640
  303.9 34.5 %collective-permute-start.16 = (bf16[256,2048]{1,0:T(8,128)(2,1)}, bf16[256,2048]{1,0:T(8,128)(2,1)}, u32[]{:S(2)}, u32[]{:S(2)}) collective-permute-start(bf16[256,2048]{1,0:T(8,128)(2,1)} %get-tuple-element.409), channel_id=1, source_target_pairs={{0,16},{16,0},{1,17},{17,1},{2,18},{18,2},{3,19},{19,3},{4,20},{20... | collective-permute-start | bytes 3145736 | tf_op jit(solution)/shard_map/ppermute | solution.py:640
  306.8 47.3 %collective-permute-start.18 = (bf16[176,2048]{1,0:T(8,128)(2,1)}, bf16[176,2048]{1,0:T(8,128)(2,1)}, u32[]{:S(2)}, u32[]{:S(2)}) collective-permute-start(bf16[176,2048]{1,0:T(8,128)(2,1)} %fusion.14), channel_id=1, source_target_pairs={{0,4},{4,8},{8,12},{12,0},{1,5},{5,9},{9,13},{13,1},{2,6},{6,10},{... | collective-permute-start | bytes 2162696 | tf_op jit(solution)/shard_map/ppermute | solution.py:649
  306.8 117.2 %collective-permute-start.24 = (bf16[8,128,1408]{2,1,0:T(8,128)(2,1)}, bf16[8,128,1408]{2,1,0:T(8,128)(2,1)}, u32[]{:S(2)}, u32[]{:S(2)}) collective-permute-start(bf16[8,128,1408]{2,1,0:T(8,128)(2,1)} %copy-done.85), channel_id=1, source_target_pairs={{0,2},{1,3},{2,0},{3,1},{4,6},{5,7},{6,4},{7,5},{8,10},{9,11},{10,... | collective-permute-start | bytes 8650760 | tf_op jit(solution)/shard_map/ppermute | solution.py:646
  354.0 19.6 %collective-permute-start.22 = (bf16[16,160,128]{2,1,0:T(8,128)(2,1)}, bf16[16,160,128]{2,1,0:T(8,128)(2,1)}, u32[]{:S(2)}, u32[]{:S(2)}) collective-permute-start(bf16[16,160,128]{2,1,0:T(8,128)(2,1)} %get-tuple-element.449), channel_id=1, source_target_pairs={{12,8},{13,9},{14,10},{15,11},{28,24},{29,25},{30,26},{31,27}} | collective-permute-start | bytes 1966088 | tf_op jit(solution)/shard_map/ppermute | solution.py:667
  358.3 27.8 %collective-permute-start.21 = (bf16[176,2048]{1,0:T(8,128)(2,1)}, bf16[176,2048]{1,0:T(8,128)(2,1)}, u32[]{:S(2)}, u32[]{:S(2)}) collective-permute-start(bf16[176,2048]{1,0:T(8,128)(2,1)} %fusion.9), channel_id=1, source_target_pairs={{0,4},{4,8},{8,12},{12,0},{1,5},{5,9},{9,13},{13,1},{2,6},{6,10},{... | collective-permute-start | bytes 2162696 | tf_op jit(solution)/shard_map/ppermute | solution.py:649
  373.1 15.8 %collective-permute-start.19 = (bf16[256,2048]{1,0:T(8,128)(2,1)}, bf16[256,2048]{1,0:T(8,128)(2,1)}, u32[]{:S(2)}, u32[]{:S(2)}) collective-permute-start(bf16[256,2048]{1,0:T(8,128)(2,1)} %get-tuple-element.445), channel_id=1, source_target_pairs={{0,16},{16,0},{1,17},{17,1},{2,18},{18,2},{3,19},{19,3},{4,20},{20... | collective-permute-start | bytes 3145736 | tf_op jit(solution)/shard_map/ppermute | solution.py:640
  373.1 42.8 %collective-permute-start.20 = (bf16[256,2048]{1,0:T(8,128)(2,1)}, bf16[256,2048]{1,0:T(8,128)(2,1)}, u32[]{:S(2)}, u32[]{:S(2)}) collective-permute-start(bf16[256,2048]{1,0:T(8,128)(2,1)} %get-tuple-element.446), channel_id=1, source_target_pairs={{0,16},{16,0},{1,17},{17,1},{2,18},{18,2},{3,19},{19,3},{4,20},{20... | collective-permute-start | bytes 3145736 | tf_op jit(solution)/shard_map/ppermute | solution.py:640
  376.2 40.3 %collective-permute-start.26 = (bf16[16,160,128]{2,1,0:T(8,128)(2,1)}, bf16[16,160,128]{2,1,0:T(8,128)(2,1)}, u32[]{:S(2)}, u32[]{:S(2)}) collective-permute-start(bf16[16,160,128]{2,1,0:T(8,128)(2,1)} %fusion.10), channel_id=1, source_target_pairs={{8,4},{9,5},{10,6},{11,7},{24,20},{25,21},{26,22},{27,23}} | collective-permute-start | bytes 1966088 | tf_op jit(solution)/shard_map/ppermute | solution.py:667
  388.9 31.6 %collective-permute-start.25 = (bf16[176,2048]{1,0:T(8,128)(2,1)}, bf16[176,2048]{1,0:T(8,128)(2,1)}, u32[]{:S(2)}, u32[]{:S(2)}) collective-permute-start(bf16[176,2048]{1,0:T(8,128)(2,1)} %fusion.8), channel_id=1, source_target_pairs={{0,4},{4,8},{8,12},{12,0},{1,5},{5,9},{9,13},{13,1},{2,6},{6,10},{... | collective-permute-start | bytes 2162696 | tf_op jit(solution)/shard_map/ppermute | solution.py:649
  389.0 39.9 %collective-permute-start.29 = (bf16[256,2048]{1,0:T(8,128)(2,1)}, bf16[256,2048]{1,0:T(8,128)(2,1)}, u32[]{:S(2)}, u32[]{:S(2)}) collective-permute-start(bf16[256,2048]{1,0:T(8,128)(2,1)} %copy-done.88), channel_id=1, source_target_pairs={{0,16},{16,0},{1,17},{17,1},{2,18},{18,2},{3,19},{19,3},{4,20},{20... | collective-permute-start | bytes 3145736 | tf_op jit(solution)/shard_map/ppermute | solution.py:640
  415.9 17.1 %collective-permute-start.30 = (bf16[256,2048]{1,0:T(8,128)(2,1)S(1)}, bf16[256,2048]{1,0:T(8,128)(2,1)S(1)}, u32[]{:S(2)}, u32[]{:S(2)}) collective-permute-start(bf16[256,2048]{1,0:T(8,128)(2,1)S(1)} %copy-done.87), channel_id=1, source_target_pairs={{0,16},{16,0},{1,17},{17,1},{2,18},{18,2},{3,19},{19,3},{4,20},{20... | collective-permute-start | bytes 3145736 | tf_op jit(solution)/shard_map/ppermute | solution.py:640
  419.1 44.8 %collective-permute-start.28 = (bf16[16,160,128]{2,1,0:T(8,128)(2,1)}, bf16[16,160,128]{2,1,0:T(8,128)(2,1)S(1)}, u32[]{:S(2)}, u32[]{:S(2)}) collective-permute-start(bf16[16,160,128]{2,1,0:T(8,128)(2,1)} %fusion.11), channel_id=1, source_target_pairs={{4,0},{5,1},{6,2},{7,3},{20,16},{21,17},{22,18},{23,19}} | collective-permute-start | bytes 1966088 | tf_op jit(solution)/shard_map/ppermute | solution.py:667
  422.4 58.8 %collective-permute-start.32 = (bf16[176,2048]{1,0:T(8,128)(2,1)S(1)}, bf16[176,2048]{1,0:T(8,128)(2,1)}, u32[]{:S(2)}, u32[]{:S(2)}) collective-permute-start(bf16[176,2048]{1,0:T(8,128)(2,1)S(1)} %fusion.6), channel_id=1, source_target_pairs={{1,8},{3,10},{5,12},{7,14},{8,1},{10,3},{12,5},{14,7},{17,24},{19,... | collective-permute-start | bytes 2162696 | tf_op jit(solution)/shard_map/ppermute | solution.py:876
  426.1 55.1 %collective-permute-start.27 = (bf16[2,2,64,1408]{3,2,1,0:T(8,128)(2,1)}, bf16[2,2,64,1408]{3,2,1,0:T(8,128)(2,1)}, u32[]{:S(2)}, u32[]{:S(2)}) collective-permute-start(bf16[2,2,64,1408]{3,2,1,0:T(8,128)(2,1)} %fusion.15), channel_id=1, source_target_pairs={{0,4},{4,8},{8,12},{12,0},{1,5},{5,9},{9,13},{13,1},{2,6},{6,10},{... | collective-permute-start | bytes 2162696 | tf_op jit(solution)/shard_map/ppermute | solution.py:649
  428.8 66.4 %collective-permute-start.35 = (bf16[8,128,1408]{2,1,0:T(8,128)(2,1)}, bf16[8,128,1408]{2,1,0:T(8,128)(2,1)}, u32[]{:S(2)}, u32[]{:S(2)}) collective-permute-start(bf16[8,128,1408]{2,1,0:T(8,128)(2,1)} %get-tuple-element.520), channel_id=1, source_target_pairs={{0,2},{1,3},{2,0},{3,1},{4,6},{5,7},{6,4},{7,5},{8,10},{9,11},{10,... | collective-permute-start | bytes 8650760 | tf_op jit(solution)/shard_map/ppermute | solution.py:646
  433.0 81.2 %collective-permute-start.23 = (bf16[512,2048]{1,0:T(8,128)(2,1)}, bf16[512,2048]{1,0:T(8,128)(2,1)}, u32[]{:S(2)}, u32[]{:S(2)}) collective-permute-start(bf16[512,2048]{1,0:T(8,128)(2,1)} %add_convert_fusion), channel_id=1, source_target_pairs={{0,1},{1,0},{2,3},{3,2},{4,5},{5,4},{6,7},{7,6},{8,9},{9,8},{10,11... | collective-permute-start | bytes 6291464 | tf_op jit(solution)/shard_map/ppermute | solution.py:643
  482.5 14.2 %collective-permute-start.34 = (bf16[512,1280]{1,0:T(8,128)(2,1)S(1)}, bf16[512,1280]{1,0:T(8,128)(2,1)S(1)}, u32[]{:S(2)}, u32[]{:S(2)}) collective-permute-start(bf16[512,1280]{1,0:T(8,128)(2,1)S(1)} %slice.28.c0), channel_id=1, source_target_pairs={{0,16},{16,0},{1,17},{17,1},{2,18},{18,2},{3,19},{19,3},{4,20},{20... | collective-permute-start | bytes 3932168 | tf_op jit(solution)/shard_map/ppermute | solution.py:640
  482.5 23.6 %collective-permute-start.33 = (bf16[512,1280]{1,0:T(8,128)(2,1)S(1)}, bf16[512,1280]{1,0:T(8,128)(2,1)S(1)}, u32[]{:S(2)}, u32[]{:S(2)}) collective-permute-start(bf16[512,1280]{1,0:T(8,128)(2,1)S(1)} %pad_maximum_fusion.c0), channel_id=1, source_target_pairs={{0,16},{16,0},{1,17},{17,1},{2,18},{18,2},{3,19},{19,3},{4,20},{20... | collective-permute-start | bytes 3932168 | tf_op jit(solution)/shard_map/ppermute | solution.py:640
  485.5 28.7 %collective-permute-start.31 = (bf16[2,2,64,1408]{3,2,1,0:T(8,128)(2,1)}, bf16[2,2,64,1408]{3,2,1,0:T(8,128)(2,1)S(1)}, u32[]{:S(2)}, u32[]{:S(2)}) collective-permute-start(bf16[2,2,64,1408]{3,2,1,0:T(8,128)(2,1)} %fusion.7), channel_id=1, source_target_pairs={{0,4},{4,8},{8,12},{12,0},{1,5},{5,9},{9,13},{13,1},{2,6},{6,10},{... | collective-permute-start | bytes 2162696 | tf_op jit(solution)/shard_map/ppermute | solution.py:649
  495.2 44.5 %collective-permute-start.37 = (bf16[4,2,64,1024]{3,2,1,0:T(8,128)(2,1)S(1)}, bf16[4,2,64,1024]{3,2,1,0:T(8,128)(2,1)}, u32[]{:S(2)}, u32[]{:S(2)}) collective-permute-start(bf16[4,2,64,1024]{3,2,1,0:T(8,128)(2,1)S(1)} %get-tuple-element.543), channel_id=1, source_target_pairs={{0,1},{1,0},{2,3},{3,2},{4,5},{5,4},{6,7},{7,6},{8,9},{9,8},{10,11... | collective-permute-start | bytes 3145736 | tf_op jit(solution)/shard_map/ppermute | solution.py:643
  496.7 47.0 %collective-permute-start.36 = (bf16[4,2,64,1024]{3,2,1,0:T(8,128)(2,1)}, bf16[4,2,64,1024]{3,2,1,0:T(8,128)(2,1)S(1)}, u32[]{:S(2)}, u32[]{:S(2)}) collective-permute-start(bf16[4,2,64,1024]{3,2,1,0:T(8,128)(2,1)} %get-tuple-element.542), channel_id=1, source_target_pairs={{0,1},{1,0},{2,3},{3,2},{4,5},{5,4},{6,7},{7,6},{8,9},{9,8},{10,11... | collective-permute-start | bytes 3145736 | tf_op jit(solution)/shard_map/ppermute | solution.py:643
  503.5 33.0 %copy-start.70 = (bf16[4,2,64,1280]{3,2,1,0:T(8,128)(2,1)}, bf16[4,2,64,1280]{3,2,1,0:T(8,128)(2,1)S(1)}, u32[]{:S(2)}) copy-start(bf16[4,2,64,1280]{3,2,1,0:T(8,128)(2,1)S(1)} %get-tuple-element.562) | copy-start | bytes 3932164
  506.1 33.6 %collective-permute-start.38 = (bf16[2,2,64,1408]{3,2,1,0:T(8,128)(2,1)}, bf16[2,2,64,1408]{3,2,1,0:T(8,128)(2,1)}, u32[]{:S(2)}, u32[]{:S(2)}) collective-permute-start(bf16[2,2,64,1408]{3,2,1,0:T(8,128)(2,1)} %fusion.16), channel_id=1, source_target_pairs={{0,4},{4,8},{8,12},{12,0},{1,5},{5,9},{9,13},{13,1},{2,6},{6,10},{... | collective-permute-start | bytes 2162696 | tf_op jit(solution)/shard_map/ppermute | solution.py:649
  527.3 32.1 %collective-permute-start.41 = (bf16[4,2,64,1280]{3,2,1,0:T(8,128)(2,1)}, bf16[4,2,64,1280]{3,2,1,0:T(8,128)(2,1)}, u32[]{:S(2)}, u32[]{:S(2)}) collective-permute-start(bf16[4,2,64,1280]{3,2,1,0:T(8,128)(2,1)} %get-tuple-element.555), channel_id=1, source_target_pairs={{0,2},{1,3},{2,0},{3,1},{4,6},{5,7},{6,4},{7,5},{8,10},{9,11},{10,... | collective-permute-start | bytes 3932168 | tf_op jit(solution)/shard_map/ppermute | solution.py:646
  529.3 41.3 %collective-permute-start.40 = (bf16[4,2,64,1280]{3,2,1,0:T(8,128)(2,1)}, bf16[4,2,64,1280]{3,2,1,0:T(8,128)(2,1)}, u32[]{:S(2)}, u32[]{:S(2)}) collective-permute-start(bf16[4,2,64,1280]{3,2,1,0:T(8,128)(2,1)} %get-tuple-element.554), channel_id=1, source_target_pairs={{0,1},{1,0},{2,3},{3,2},{4,5},{5,4},{6,7},{7,6},{8,9},{9,8},{10,11... | collective-permute-start | bytes 3932168 | tf_op jit(solution)/shard_map/ppermute | solution.py:643
  539.7 47.6 %collective-permute-start.45 = (bf16[2,2,64,1408]{3,2,1,0:T(8,128)(2,1)}, bf16[2,2,64,1408]{3,2,1,0:T(8,128)(2,1)}, u32[]{:S(2)}, u32[]{:S(2)}) collective-permute-start(bf16[2,2,64,1408]{3,2,1,0:T(8,128)(2,1)} %fusion.2), channel_id=1, source_target_pairs={{0,4},{4,8},{8,12},{12,0},{1,5},{5,9},{9,13},{13,1},{2,6},{6,10},{... | collective-permute-start | bytes 2162696 | tf_op jit(solution)/shard_map/ppermute | solution.py:649
  547.3 29.0 %collective-permute-start.39 = (bf16[2,2,64,1408]{3,2,1,0:T(8,128)(2,1)}, bf16[2,2,64,1408]{3,2,1,0:T(8,128)(2,1)}, u32[]{:S(2)}, u32[]{:S(2)}) collective-permute-start(bf16[2,2,64,1408]{3,2,1,0:T(8,128)(2,1)} %fusion.3), channel_id=1, source_target_pairs={{0,4},{4,8},{8,12},{12,0},{1,5},{5,9},{9,13},{13,1},{2,6},{6,10},{... | collective-permute-start | bytes 2162696 | tf_op jit(solution)/shard_map/ppermute | solution.py:649
  550.9 28.4 %collective-permute-start.47 = (bf16[4,64,1024]{2,1,0:T(8,128)(2,1)}, bf16[4,64,1024]{2,1,0:T(8,128)(2,1)}, u32[]{:S(2)}, u32[]{:S(2)}) collective-permute-start(bf16[4,64,1024]{2,1,0:T(8,128)(2,1)} %fusion.22), channel_id=1, source_target_pairs={{0,2},{1,3},{2,0},{3,1},{4,6},{5,7},{6,4},{7,5},{8,10},{9,11},{10,... | collective-permute-start | bytes 1572872 | tf_op jit(solution)/shard_map/ppermute | solution.py:646
  554.6 56.9 %copy-start.103 = (bf16[4,1,64,1024]{3,2,1,0:T(8,128)(2,1)}, bf16[4,1,64,1024]{3,2,1,0:T(8,128)(2,1)S(1)}, u32[]{:S(2)}) copy-start(bf16[4,1,64,1024]{3,2,1,0:T(8,128)(2,1)S(1)} %constant_dynamic-slice_fusion) | copy-start | bytes 1572868
  559.4 27.8 %collective-permute-start.46 = (bf16[2,2,64,1024]{3,2,1,0:T(8,128)(2,1)S(1)}, bf16[2,2,64,1024]{3,2,1,0:T(8,128)(2,1)S(1)}, u32[]{:S(2)}, u32[]{:S(2)}) collective-permute-start(bf16[2,2,64,1024]{3,2,1,0:T(8,128)(2,1)S(1)} %fusion.21), channel_id=1, source_target_pairs={{0,4},{4,0},{8,12},{12,8},{1,5},{5,1},{9,13},{13,9},{2,6},{6,2},{1... | collective-permute-start | bytes 1572872 | tf_op jit(solution)/shard_map/ppermute | solution.py:655
  571.9 17.2 %collective-permute-start.44 = (bf16[4,64,1280]{2,1,0:T(8,128)(2,1)S(1)}, bf16[4,64,1280]{2,1,0:T(8,128)(2,1)S(1)}, u32[]{:S(2)}, u32[]{:S(2)}) collective-permute-start(bf16[4,64,1280]{2,1,0:T(8,128)(2,1)S(1)} %fusion.20), channel_id=1, source_target_pairs={{0,1},{1,0},{2,3},{3,2},{4,5},{5,4},{6,7},{7,6},{8,9},{9,8},{10,11... | collective-permute-start | bytes 1966088 | tf_op jit(solution)/shard_map/ppermute | solution.py:643
  576.3 15.2 %collective-permute-start.43 = (bf16[4,64,1280]{2,1,0:T(8,128)(2,1)S(1)}, bf16[4,64,1280]{2,1,0:T(8,128)(2,1)S(1)}, u32[]{:S(2)}, u32[]{:S(2)}) collective-permute-start(bf16[4,64,1280]{2,1,0:T(8,128)(2,1)S(1)} %fusion.19), channel_id=1, source_target_pairs={{0,2},{1,3},{2,0},{3,1},{4,6},{5,7},{6,4},{7,5},{8,10},{9,11},{10,... | collective-permute-start | bytes 1966088 | tf_op jit(solution)/shard_map/ppermute | solution.py:646
  579.3 23.6 %collective-permute-start.42 = (bf16[2,2,64,1408]{3,2,1,0:T(8,128)(2,1)S(1)}, bf16[2,2,64,1408]{3,2,1,0:T(8,128)(2,1)S(1)}, u32[]{:S(2)}, u32[]{:S(2)}) collective-permute-start(bf16[2,2,64,1408]{3,2,1,0:T(8,128)(2,1)S(1)} %fusion.4), channel_id=1, source_target_pairs={{0,4},{4,8},{8,12},{12,0},{1,5},{5,9},{9,13},{13,1},{2,6},{6,10},{... | collective-permute-start | bytes 2162696 | tf_op jit(solution)/shard_map/ppermute | solution.py:649
  587.3 24.2 %collective-permute-start.53 = (bf16[2,64,1024]{2,1,0:T(8,128)(2,1)S(1)}, bf16[2,64,1024]{2,1,0:T(8,128)(2,1)S(1)}, u32[]{:S(2)}, u32[]{:S(2)}) collective-permute-start(bf16[2,64,1024]{2,1,0:T(8,128)(2,1)S(1)} %fusion.30), channel_id=1, source_target_pairs={{0,4},{4,0},{8,12},{12,8},{1,5},{5,1},{9,13},{13,9},{2,6},{6,2},{1... | collective-permute-start | bytes 786440 | tf_op jit(solution)/shard_map/ppermute | solution.py:655
  588.5 24.1 %collective-permute-start.52 = (bf16[2,64,1024]{2,1,0:T(8,128)(2,1)S(1)}, bf16[2,64,1024]{2,1,0:T(8,128)(2,1)}, u32[]{:S(2)}, u32[]{:S(2)}) collective-permute-start(bf16[2,64,1024]{2,1,0:T(8,128)(2,1)S(1)} %fusion.23), channel_id=1, source_target_pairs={{0,8},{4,12},{8,0},{12,4},{1,9},{5,13},{9,1},{13,5},{2,10},{6,14},... | collective-permute-start | bytes 786440 | tf_op jit(solution)/shard_map/ppermute | solution.py:655
  592.4 30.7 %collective-permute-start.50 = (bf16[2,64,1280]{2,1,0:T(8,128)(2,1)}, bf16[2,64,1280]{2,1,0:T(8,128)(2,1)}, u32[]{:S(2)}, u32[]{:S(2)}) collective-permute-start(bf16[2,64,1280]{2,1,0:T(8,128)(2,1)} %fusion.25), channel_id=1, source_target_pairs={{0,4},{4,0},{8,12},{12,8},{1,5},{5,1},{9,13},{13,9},{2,6},{6,2},{1... | collective-permute-start | bytes 983048 | tf_op jit(solution)/shard_map/ppermute | solution.py:655
  606.1 15.3 %collective-permute-start.51 = (bf16[2,64,1408]{2,1,0:T(8,128)(2,1)}, bf16[2,64,1408]{2,1,0:T(8,128)(2,1)S(1)}, u32[]{:S(2)}, u32[]{:S(2)}) collective-permute-start(bf16[2,64,1408]{2,1,0:T(8,128)(2,1)} %get-tuple-element.630), channel_id=1, source_target_pairs={{0,1},{1,0},{2,3},{3,2},{4,5},{5,4},{6,7},{7,6},{8,9},{9,8},{10,11... | collective-permute-start | bytes 1081352 | tf_op jit(solution)/shard_map/ppermute | solution.py:643
  608.3 20.1 %collective-permute-start.48 = (bf16[2,64,1408]{2,1,0:T(8,128)(2,1)}, bf16[2,64,1408]{2,1,0:T(8,128)(2,1)S(1)}, u32[]{:S(2)}, u32[]{:S(2)}) collective-permute-start(bf16[2,64,1408]{2,1,0:T(8,128)(2,1)} %get-tuple-element.632), channel_id=1, source_target_pairs={{0,1},{1,0},{2,3},{3,2},{4,5},{5,4},{6,7},{7,6},{8,9},{9,8},{10,11... | collective-permute-start | bytes 1081352 | tf_op jit(solution)/shard_map/ppermute | solution.py:643
  611.5 16.9 %collective-permute-start.49 = (bf16[2,64,1280]{2,1,0:T(8,128)(2,1)}, bf16[2,64,1280]{2,1,0:T(8,128)(2,1)S(1)}, u32[]{:S(2)}, u32[]{:S(2)}) collective-permute-start(bf16[2,64,1280]{2,1,0:T(8,128)(2,1)} %fusion.24), channel_id=1, source_target_pairs={{0,4},{4,0},{8,12},{12,8},{1,5},{5,1},{9,13},{13,9},{2,6},{6,2},{1... | collective-permute-start | bytes 983048 | tf_op jit(solution)/shard_map/ppermute | solution.py:655
  612.6 15.8 %collective-permute-start.59 = (bf16[64,1024]{1,0:T(8,128)(2,1)S(1)}, bf16[64,1024]{1,0:T(8,128)(2,1)S(1)}, u32[]{:S(2)}, u32[]{:S(2)}) collective-permute-start(bf16[64,1024]{1,0:T(8,128)(2,1)S(1)} %fusion.31), channel_id=1, source_target_pairs={{0,8},{4,12},{8,0},{12,4},{1,9},{5,13},{9,1},{13,5},{2,10},{6,14},... | collective-permute-start | bytes 393224 | tf_op jit(solution)/shard_map/ppermute | solution.py:655
  617.1 36.9 %all-to-all-start = ((f32[32,1,128]{2,1,0:T(1,128)}), f32[32,1,128]{2,1,0:T(1,128)}, u32[]{:S(2)}, u32[]{:S(2)}) async-start(f32[32,1,128]{2,1,0:T(1,128)} %bitcast.24), calls=%async_computation | async-start | bytes 32768 | tf_op jit(solution)/shard_map/all_to_all | solution.py:1045
  621.4 9.2 %collective-permute-start.58 = (bf16[64,1024]{1,0:T(8,128)(2,1)S(1)}, bf16[64,1024]{1,0:T(8,128)(2,1)S(1)}, u32[]{:S(2)}, u32[]{:S(2)}) collective-permute-start(bf16[64,1024]{1,0:T(8,128)(2,1)S(1)} %fusion.33), channel_id=1, source_target_pairs={{0,2},{1,3},{2,0},{3,1},{4,6},{5,7},{6,4},{7,5},{8,10},{9,11},{10,... | collective-permute-start | bytes 393224 | tf_op jit(solution)/shard_map/ppermute | solution.py:646
  633.5 5.5 collective-permute-start.57
  634.7 13.8 %collective-permute-start.56 = (bf16[64,1280]{1,0:T(8,128)(2,1)S(1)}, bf16[64,1280]{1,0:T(8,128)(2,1)S(1)}, u32[]{:S(2)}, u32[]{:S(2)}) collective-permute-start(bf16[64,1280]{1,0:T(8,128)(2,1)S(1)} %fusion.26), channel_id=1, source_target_pairs={{0,8},{4,12},{8,0},{12,4},{1,9},{5,13},{9,1},{13,5},{2,10},{6,14},... | collective-permute-start | bytes 491528 | tf_op jit(solution)/shard_map/ppermute | solution.py:655
  634.9 17.0 %collective-permute-start.55 = (bf16[64,1280]{1,0:T(8,128)(2,1)S(1)}, bf16[64,1280]{1,0:T(8,128)(2,1)S(1)}, u32[]{:S(2)}, u32[]{:S(2)}) collective-permute-start(bf16[64,1280]{1,0:T(8,128)(2,1)S(1)} %fusion.28), channel_id=1, source_target_pairs={{0,8},{4,12},{8,0},{12,4},{1,9},{5,13},{9,1},{13,5},{2,10},{6,14},... | collective-permute-start | bytes 491528 | tf_op jit(solution)/shard_map/ppermute | solution.py:655
  638.1 13.9 %collective-permute-start.54 = (bf16[64,2816]{1,0:T(8,128)(2,1)S(1)}, bf16[64,2816]{1,0:T(8,128)(2,1)S(1)}, u32[]{:S(2)}, u32[]{:S(2)}) collective-permute-start(bf16[64,2816]{1,0:T(8,128)(2,1)S(1)} %get-tuple-element.626), channel_id=1, source_target_pairs={{0,16},{16,0},{1,17},{17,1},{2,18},{18,2},{3,19},{19,3},{4,20},{20... | collective-permute-start | bytes 1081352 | tf_op jit(solution)/shard_map/ppermute | solution.py:640
  (124 other events, 1089.9 us)

commit v4 on v3

--- a/solution.py
+++ b/solution.py
@@ -1024,12 +1024,12 @@
         inner.append(Task(line, share(pieces, along_x, order)))
     gate.step()
     layer_out = fence(middle + total_of([lay0, jnp.concatenate(lay1), fence(far_lay)]))
+    up.step()
     grad_low_one = fence(
         mm(fence(grad_queries), w_query, NT)
         + mm(grad_keys, w_key, NT)
         + mm(grad_values_low, w_value, NT)
     )
-    up.step()
     out[0].step()
     out[1].step()
     unit_one = flat * root_one

time: 666 us -> 665 us (level)
    unnamed x254 -> x250, local copies, waits for them, and re-layouts: 47.2 us -> 47.1 us
  transfers between devices with their start and end apart: 61 -> 61, of which waited for: 21 -> 19; matrix products, arithmetic and copies ran while one was open for 18% -> 18% of each run, Pallas kernels for 41% -> 41%
where the time goes in v4:
time: 665 us; the launch traced here: 656 us
  Pallas kernels  316 us (48%)
  waiting for transfers between devices  93.9 us (14%)
  other arithmetic  88.4 us (13%)
  local copies, waits for them, and re-layouts  60.1 us (9%)
  starting transfers between devices  59.8 us (9%)
  matrix products  33 us (5%)
    pallas_call x8, Pallas kernels, token_call(): pl.pallas_call(functools.partial(kernel, half), grid_spec=pltpu.PrefetchS...  125 us
    pallas_call x7, Pallas kernels, head_call(): pl.pallas_call(body, grid=(last - first,), in_specs=[spec(kind, a.shape)...  99.9 us
    convert_element_type x26, other arithmetic, low_sum(): return total_of(terms).astype(bf16)  48.7 us
    unnamed x250, local copies, waits for them, and re-layouts  47.1 us
    pallas_call x2, Pallas kernels, wide_grad(): pl.pallas_call(wide_grad_kernel, grid_spec=pltpu.PrefetchScalarGridSpec(n...  33.6 us
    dot_general x7, matrix products, mm(): return lax.dot_general(a, b, dims, preferred_element_type=f32)  33 us
    ppermute x10, waiting for transfers between devices, over_x(): return lax.ppermute(a, 'rows', [(r, r ^ 1) for r in range(nrows)])  33 us
    ppermute x12, waiting for transfers between devices, over_seq(): lax.ppermute(a, 'seq', [(s, (s + shift) % nseq) for s in range(nseq)])  24.8 us
  transfers between devices with their start and end apart: 61, of which 19 were waited for; matrix products, arithmetic and copies ran while one was open for 18% of the time, Pallas kernels for 41%

profile of v4, /device:TPU:0, one launch (start us, length us, event | category | flops | bytes accessed | tf_op | source)
XLA Modules:
  0.0 655.5 jit_solution(1344107339409269936)
XLA Ops:
  0.7 4.0 bitcast_convert_fusion.g0
  7.1 2.6 collective-permute-start.5
  12.8 2.3 convolution_convert_fusion.2.refs_3_.refs_4_
  17.9 8.7 %convolution_convert_fusion.refs_4_.refs_5_ = bf16[512,2048]{1,0:T(8,128)(2,1)S(1)} fusion(bf16[512,2048]{1,0:T(8,128)(2,1)} %multiply_convert_fusion.1.r0, bf16[2048,2048]{1,0:T(8,128)(2,1)} %param.20), kind=kOutput, calls=%fused_computation.14 | convolution fusion | flops 4296015872 | bytes 12582912 | tf_op jit(solution)/shard_map/dot_general | solution.py:41
  26.7 9.2 %shard_map.230 = bf16[16,160,128]{2,1,0:T(8,128)(2,1)S(1)} custom-call(bf16[16,256,256]{2,1,0:T(8,128)(2,1)S(1)} %copy-done.1, bf16[16,256,256]{2,1,0:T(8,128)(2,1)S(1)} %copy-done.2, f32[8,256]{1,0:T(8,128)S(1)} %copy-done.83, bf16[512,256]{1,0:T(8,128)(2,1)S(1)} %convolution_convert_fusion.2.refs_3_.refs_4_, ...), custom_call_target="tpu_custom_call" | custom-call | tf_op jit(solution)/shard_map/pallas_call | solution.py:291
  37.8 2.7 convolution_convert_fusion.1.refs_3_
  40.5 18.1 %shard_map.231 = (f32[512,2048]{1,0:T(8,128)S(1)}, f32[512,128]{1,0:T(8,128)S(1)}, bf16[16,512,256]{2,1,0:T(8,128)(2,1)S(1)}) custom-call(bf16[16,256,256]{2,1,0:T(8,128)(2,1)S(1)} %copy-done.1, bf16[16,256,256]{2,1,0:T(8,128)(2,1)S(1)} %copy-done.2, f32[8,256]{1,0:T(8,128)S(1)} %copy-done.83, bf16[512,256]{1,0:T(8,128)(2,1)S(1)} %convolution_convert_fusion.1.refs_3_, ...), custom_call_target="tpu_custom_call" | custom-call | tf_op jit(solution)/shard_map/pallas_call | solution.py:291
  64.9 10.7 %shard_map.232.grad_ref = bf16[1024,1408]{1,0:T(8,128)(2,1)S(1)} custom-call(s32[1]{0:T(128)} %bitcast.4.which_ref, bf16[512,2048]{1,0:T(8,128)(2,1)} %bitcast_convert_fusion.g0, bf16[512,2048]{1,0:T(8,128)(2,1)} %collective-permute-done.2.g1, bf16[5632,2048]{1,0:T(8,128)(2,1)} %wd.7), custom_call_target="tpu_custom_call" | custom-call | tf_op jit(solution)/shard_map/pallas_call | solution.py:377
  75.6 6.5 collective-permute-done.1.refs_6_
  83.2 3.3 collective-permute-done.6.g1.g3
  86.5 11.1 %shard_map.233.grad_ref = bf16[1024,1408]{1,0:T(8,128)(2,1)S(1)} custom-call(s32[1]{0:T(128)} %bitcast.4.which_ref, bf16[512,2048]{1,0:T(8,128)(2,1)} %collective-permute-done.5.g0.g2, bf16[512,2048]{1,0:T(8,128)(2,1)S(1)} %collective-permute-done.6.g1.g3, bf16[5632,2048]{1,0:T(8,128)(2,1)} %wd.7), custom_call_target="tpu_custom_call" | custom-call | tf_op jit(solution)/shard_map/pallas_call | solution.py:377
  97.6 3.8 collective-permute-done.4.refs_7_
  101.6 11.9 %shard_map.234 = (bf16[512,2048]{1,0:T(8,128)(2,1)S(1)}, f32[512,128]{1,0:T(8,128)S(1)}, f32[16,160,128]{2,1,0:T(8,128)S(1)}) custom-call(f32[3]{0:T(128)S(1)} %and_convert_fusion.refs_0_, bf16[16,512,256]{2,1,0:T(8,128)(2,1)S(1)} %copy-done.16, f32[512,2048]{1,0:T(8,128)S(1)} %copy-done.52, f32[512,128]{1,0:T(8,128)S(1)} %copy-done.82, ...), custom_call_target="tpu_custom_call" | custom-call | tf_op jit(solution)/shard_map/pallas_call | solution.py:291
  113.6 8.4 %multiply_reduce_fusion.2 = (f32[512]{0:T(512)S(1)}, f32[512,2048]{1,0:T(8,128)S(1)}) fusion(bf16[512,2048]{1,0:T(8,128)(2,1)S(1)} %get-tuple-element.490.refs_2_.r0, bf16[2048,2048]{1,0:T(8,128)(2,1)} %w.1, f32[1,512,2048]{2,1,0:T(8,128)S(1)} %copy-done.90), kind=kOutput, calls=%fused_computation.12 | convolution fusion | flops 4298112512 | bytes 18876416 | tf_op jit(solution)/shard_map/dot_general | solution.py:41
  125.1 3.1 collective-permute-done.8.x1.l1
  128.2 3.0 collective-permute-done.7.r1
  132.5 19.1 %shard_map.235 = (bf16[1024,1408]{1,0:T(8,128)(2,1)S(1)}, bf16[1024,1408]{1,0:T(8,128)(2,1)S(1)}, bf16[1024,1408]{1,0:T(8,128)(2,1)S(1)}) custom-call(s32[1]{0:T(128)} %bitcast.4.which_ref, bf16[512,2048]{1,0:T(8,128)(2,1)S(1)} %multiply_convert_fusion.x0.l0, bf16[512,2048]{1,0:T(8,128)(2,1)S(1)} %collective-permute-done.8.x1.l1, ...), custom_call_target="tpu_custom_call" | custom-call | tf_op jit(solution)/shard_map/pallas_call | solution.py:377
  153.2 21.6 %shard_map.236 = (bf16[512,2048]{1,0:T(8,128)(2,1)S(1)}, bf16[512,2048]{1,0:T(8,128)(2,1)}) custom-call(s32[1]{0:T(128)} %bitcast.4.which_ref, bf16[1024,1408]{1,0:T(8,128)(2,1)S(1)} %get-tuple-element.383.gg.near, bf16[1024,1408]{1,0:T(8,128)(2,1)S(1)} %get-tuple-element.395.gu.near, bf16[2048,5632]{1,0:T(8,128)(2,1)} %wg.7, bf16[2048,5632]{1,0:T(8,128)(2,1)} %wu.7), custom_call_target="tpu_custom_call" | custom-call | tf_op jit(solution)/shard_map/pallas_call | solution.py:377
  176.7 4.0 collective-permute-done.10.x1.l3
  180.7 3.0 collective-permute-done.11.near
  185.5 20.0 %shard_map.237 = (bf16[1024,1408]{1,0:T(8,128)(2,1)S(1)}, bf16[1024,1408]{1,0:T(8,128)(2,1)S(1)}, bf16[1024,1408]{1,0:T(8,128)(2,1)S(1)}) custom-call(s32[1]{0:T(128)} %bitcast.4.which_ref, bf16[512,2048]{1,0:T(8,128)(2,1)} %collective-permute-done.9.x0.l2, bf16[512,2048]{1,0:T(8,128)(2,1)} %collective-permute-done.10.x1.l3, ...), custom_call_target="tpu_custom_call" | custom-call | tf_op jit(solution)/shard_map/pallas_call | solution.py:377
  207.1 16.8 %shard_map.238 = (bf16[2,352,2048]{2,1,0:T(8,128)(2,1)S(1)}, bf16[2,352,2048]{2,1,0:T(8,128)(2,1)S(1)}) custom-call(s32[1]{0:T(128)} %bitcast.5.ybit_ref, bf16[1024,1408]{1,0:T(8,128)(2,1)S(1)} %copy-done.24, bf16[1024,1408]{1,0:T(8,128)(2,1)S(1)} %get-tuple-element.439.far.hid, bf16[512,2048]{1,0:T(8,128)(2,1)} %bitcast_convert_fusion.g0, ...), custom_call_target="tpu_custom_call" | custom-call | tf_op jit(solution)/shard_map/pallas_call | solution.py:450
  227.0 2.4 copy-done.34
  229.4 18.9 %shard_map.239 = (bf16[512,2048]{1,0:T(8,128)(2,1)S(1)}, bf16[256,2048]{1,0:T(8,128)(2,1)S(1)}, bf16[256,2048]{1,0:T(8,128)(2,1)S(1)}) custom-call(s32[1]{0:T(128)} %bitcast.4.which_ref, bf16[1024,1408]{1,0:T(8,128)(2,1)S(1)} %copy-done.34, bf16[1024,1408]{1,0:T(8,128)(2,1)S(1)} %get-tuple-element.377.gu.far, bf16[2048,5632]{1,0:T(8,128)(2,1)} %wg.7, ...), custom_call_target="tpu_custom_call" | custom-call | tf_op jit(solution)/shard_map/pallas_call | solution.py:377
  250.7 16.4 %shard_map.240 = (bf16[8,128,1408]{2,1,0:T(8,128)(2,1)S(1)}, bf16[8,128,1408]{2,1,0:T(8,128)(2,1)S(1)}) custom-call(s32[1]{0:T(128)} %bitcast.5.ybit_ref, bf16[512,2048]{1,0:T(8,128)(2,1)S(1)} %copy-done.9, bf16[512,2048]{1,0:T(8,128)(2,1)S(1)} %copy-done.14, bf16[512,2048]{1,0:T(8,128)(2,1)} %collective-permute-done.9.x0.l2, ...), custom_call_target="tpu_custom_call" | custom-call | tf_op jit(solution)/shard_map/pallas_call | solution.py:419
  272.6 17.2 %shard_map.241 = (bf16[8,128,1408]{2,1,0:T(8,128)(2,1)}, bf16[8,128,1408]{2,1,0:T(8,128)(2,1)S(1)}) custom-call(s32[1]{0:T(128)} %bitcast.5.ybit_ref, bf16[512,2048]{1,0:T(8,128)(2,1)S(1)} %copy-done.9, bf16[512,2048]{1,0:T(8,128)(2,1)S(1)} %copy-done.14, bf16[512,2048]{1,0:T(8,128)(2,1)} %collective-permute-done.9.x0.l2, ...), custom_call_target="tpu_custom_call" | custom-call | tf_op jit(solution)/shard_map/pallas_call | solution.py:419
  290.1 12.3 %shard_map.242 = (bf16[512,2048]{1,0:T(8,128)(2,1)S(1)}, bf16[256,2048]{1,0:T(8,128)(2,1)}, bf16[256,2048]{1,0:T(8,128)(2,1)}) custom-call(s32[1]{0:T(128)} %bitcast.4.which_ref, bf16[1024,1408]{1,0:T(8,128)(2,1)S(1)} %copy-done.24, bf16[5632,2048]{1,0:T(8,128)(2,1)} %wd.7), custom_call_target="tpu_custom_call" | custom-call | tf_op jit(solution)/shard_map/pallas_call | solution.py:377
  304.3 2.4 fusion.14
  307.7 11.3 %collective-permute-done.17.far = bf16[512,2048]{1,0:T(8,128)(2,1)} collective-permute-done((bf16[512,2048]{1,0:T(8,128)(2,1)}, bf16[512,2048]{1,0:T(8,128)(2,1)}, u32[]{:S(2)}, u32[]{:S(2)}) %collective-permute-start.17) | collective-permute-done | bytes 2097184 | tf_op jit(solution)/shard_map/ppermute | solution.py:643
  319.0 17.4 %shard_map.243 = (f32[512,2048]{1,0:T(8,128)}, bf16[512,2048]{1,0:T(8,128)(2,1)}, bf16[512,2048]{1,0:T(8,128)(2,1)}, f32[8,2048]{1,0:T(8,128)S(1)}, bf16[256,204...) custom-call(bf16[512,2048]{1,0:T(8,128)(2,1)} %copy-done.69, bf16[512,2048]{1,0:T(8,128)(2,1)} %collective-permute-done.11.near, ...), custom_call_target="tpu_custom_call" | custom-call | tf_op jit(solution)/shard_map/pallas_call | solution.py:498
  340.0 11.9 %shard_map.244 = (bf16[16,160,128]{2,1,0:T(8,128)(2,1)}, bf16[512,2048]{1,0:T(8,128)(2,1)S(1)}, f32[512,128]{1,0:T(8,128)S(1)}) custom-call(bf16[16,512,256]{2,1,0:T(8,128)(2,1)S(1)} %copy-done.17, bf16[512,2048]{1,0:T(8,128)(2,1)S(1)} %copy-done.68, bf16[512,2048]{1,0:T(8,128)(2,1)S(1)} %copy-done.11, f32[512,128]{1,0:T(8,128)S(1)} %copy-done.80, ...), custom_call_target="tpu_custom_call" | custom-call | tf_op jit(solution)/shard_map/pallas_call | solution.py:291
  355.5 2.7 fusion.9
  361.5 11.6 %shard_map.245 = (bf16[512,2048]{1,0:T(8,128)(2,1)S(1)}, bf16[256,2048]{1,0:T(8,128)(2,1)}, bf16[256,2048]{1,0:T(8,128)(2,1)}) custom-call(s32[1]{0:T(128)} %bitcast.4.which_ref, bf16[1024,1408]{1,0:T(8,128)(2,1)S(1)} %copy-done.22, bf16[5632,2048]{1,0:T(8,128)(2,1)} %wd.7), custom_call_target="tpu_custom_call" | custom-call | tf_op jit(solution)/shard_map/pallas_call | solution.py:377
  373.6 2.6 fusion.10
  377.7 8.4 %collective-permute-done.21 = bf16[176,2048]{1,0:T(8,128)(2,1)} collective-permute-done((bf16[176,2048]{1,0:T(8,128)(2,1)}, bf16[176,2048]{1,0:T(8,128)(2,1)}, u32[]{:S(2)}, u32[]{:S(2)}) %collective-permute-start.21) | collective-permute-done | bytes 720928 | tf_op jit(solution)/shard_map/ppermute | solution.py:649
  386.1 2.8 fusion.8
  399.8 16.0 %shard_map.246 = (f32[512,256]{1,0:T(8,128)S(1)}, f32[512,256]{1,0:T(8,128)S(1)}, f32[512,2048]{1,0:T(8,128)S(1)}) custom-call(bf16[16,256,256]{2,1,0:T(8,128)(2,1)S(1)} %copy-done.1, bf16[16,256,256]{2,1,0:T(8,128)(2,1)S(1)} %copy-done.3, f32[8,256]{1,0:T(8,128)S(1)} %copy-done.83, bf16[512,256]{1,0:T(8,128)(2,1)S(1)} %copy-done.60, ...), custom_call_target="tpu_custom_call" | custom-call | tf_op jit(solution)/shard_map/pallas_call | solution.py:291
  416.5 2.6 fusion.11
  420.5 2.8 fusion.6
  427.0 2.7 collective-permute-start.27
  430.0 3.9 add_convert_fusion
  433.9 3.0 collective-permute-start.23
  436.9 4.9 shard_map.247
  441.9 5.3 shard_map.248
  447.4 15.8 %shard_map.249 = (f32[512,256]{1,0:T(8,128)S(1)}, f32[512,256]{1,0:T(8,128)S(1)}, f32[512,2048]{1,0:T(8,128)S(1)}) custom-call(bf16[16,256,256]{2,1,0:T(8,128)(2,1)S(1)} %copy-done.1, bf16[16,256,256]{2,1,0:T(8,128)(2,1)S(1)} %copy-done.4, f32[8,256]{1,0:T(8,128)S(1)} %copy-done.83, ...), custom_call_target="tpu_custom_call", output_to_operand_aliasing={{2}: (13, {})} | custom-call | tf_op jit(solution)/shard_map/pallas_call | solution.py:291
  464.1 17.1 %shard_map.250 = (bf16[512,256]{1,0:T(8,128)(2,1)S(1)}, bf16[512,2048]{1,0:T(8,128)(2,1)S(1)}) custom-call(f32[3]{0:T(128)S(1)} %broadcast_5_refs_0_.2.refs_0_, bf16[16,256,256]{2,1,0:T(8,128)(2,1)S(1)} %copy-done.1, bf16[16,256,256]{2,1,0:T(8,128)(2,1)S(1)} %copy-done.4, f32[8,256]{1,0:T(8,128)S(1)} %copy-done.83, ...), custom_call_target="tpu_custom_call" | custom-call | tf_op jit(solution)/shard_map/pallas_call | solution.py:291
  481.5 2.3 select_convert_fusion
  484.3 2.5 fusion.7
  487.1 9.4 %fusion.40 = f32[512,2048]{1,0:T(8,128)} fusion(bf16[512,2048]{1,0:T(8,128)(2,1)S(1)} %get-tuple-element.510, bf16[2048,2048]{1,0:T(8,128)(2,1)} %param.20), kind=kOutput, calls=%fused_computation.130 | convolution fusion | flops 4294967296 | bytes 14680064 | tf_op jit(solution)/shard_map/dot_general | solution.py:41
  498.6 6.2 shard_map.251
  507.4 6.2 shard_map.252
  513.6 7.1 %add_add_fusion.1 = f32[512,2048]{1,0:T(8,128)} fusion(f32[512,2048]{1,0:T(8,128)} %copy-done.92, bf16[512,2048]{1,0:T(8,128)(2,1)} %collective-permute-done.23, bf16[512,2048]{1,0:T(8,128)(2,1)S(1)} %copy-done.65, bf16[256,2048]{1,0:T(8,128)(2,1)} %collective-permute-done.16, bf16[256,2048]{1,0:T(8,128)(2,1)} %collective-permute-done.15), kind=kLoop, calls=%fused_computation.8 | loop fusion | flops 9437184 | bytes 14680064 | tf_op jit(solution)/shard_map/add | solution.py:1026
  526.3 2.5 fusion.2
  534.6 5.3 multiply_add_fusion
  539.9 5.1 collective-permute-done.37
  546.0 2.6 fusion.3
  556.3 15.7 %collective-permute-done.40 = bf16[4,2,64,1280]{3,2,1,0:T(8,128)(2,1)} collective-permute-done((bf16[4,2,64,1280]{3,2,1,0:T(8,128)(2,1)}, bf16[4,2,64,1280]{3,2,1,0:T(8,128)(2,1)}, u32[]{:S(2)}, u32[]{:S(2)}) %collective-permute-start.40) | collective-permute-done | bytes 1310752 | tf_op jit(solution)/shard_map/ppermute | solution.py:643
  588.8 3.1 collective-permute-done.43
  594.8 6.0 collective-permute-done.42
  610.7 6.1 collective-permute-start.59
  617.5 3.2 all-to-all-start
  623.5 3.1 collective-permute-done.49
  638.4 9.1 %collective-permute-done.56 = bf16[64,1280]{1,0:T(8,128)(2,1)S(1)} collective-permute-done((bf16[64,1280]{1,0:T(8,128)(2,1)S(1)}, bf16[64,1280]{1,0:T(8,128)(2,1)S(1)}, u32[]{:S(2)}, u32[]{:S(2)}) %collective-permute-start.56) | collective-permute-done | bytes 163872 | tf_op jit(solution)/shard_map/ppermute | solution.py:655
  648.5 2.4 collective-permute-done.55
  (425 shorter events, 146.8 us)
Async XLA Ops:
  0.6 37.1 %copy-start = (bf16[2048,256]{1,0:T(8,128)(2,1)S(1)}, bf16[2048,256]{1,0:T(8,128)(2,1)}, u32[]{:S(2)}) copy-start(bf16[2048,256]{1,0:T(8,128)(2,1)} %param.18) | copy-start | bytes 3145732
  6.6 58.3 %collective-permute-start.2 = (bf16[512,2048]{1,0:T(8,128)(2,1)}, bf16[512,2048]{1,0:T(8,128)(2,1)}, u32[]{:S(2)}, u32[]{:S(2)}) collective-permute-start(bf16[512,2048]{1,0:T(8,128)(2,1)} %bitcast_convert_fusion.g0), channel_id=1, source_target_pairs={{0,16},{16,0},{1,17},{17,1},{2,18},{18,2},{3,19},{19,3},{4,20},{20... | collective-permute-start | bytes 6291464 | tf_op jit(solution)/shard_map/ppermute | solution.py:640
  7.1 75.0 %collective-permute-start.5 = (bf16[512,2048]{1,0:T(8,128)(2,1)}, bf16[512,2048]{1,0:T(8,128)(2,1)}, u32[]{:S(2)}, u32[]{:S(2)}) collective-permute-start(bf16[512,2048]{1,0:T(8,128)(2,1)} %bitcast_convert_fusion.g0), channel_id=1, source_target_pairs={{0,1},{1,0},{2,3},{3,2},{4,5},{5,4},{6,7},{7,6},{8,9},{9,8},{10,11... | collective-permute-start | bytes 6291464 | tf_op jit(solution)/shard_map/ppermute | solution.py:643
  11.8 53.1 %collective-permute-start.3 = (bf16[512,2048]{1,0:T(8,128)(2,1)}, bf16[512,2048]{1,0:T(8,128)(2,1)}, u32[]{:S(2)}, u32[]{:S(2)}) collective-permute-start(bf16[512,2048]{1,0:T(8,128)(2,1)} %multiply_convert_fusion.1.r0), channel_id=1, source_target_pairs={{0,16},{16,0},{1,17},{17,1},{2,18},{18,2},{3,19},{19,3},{4,20},{20... | collective-permute-start | bytes 6291464 | tf_op jit(solution)/shard_map/ppermute | solution.py:640
  35.9 27.3 %collective-permute-start = (bf16[16,160,128]{2,1,0:T(8,128)(2,1)S(1)}, bf16[16,160,128]{2,1,0:T(8,128)(2,1)}, u32[]{:S(2)}, u32[]{:S(2)}) collective-permute-start(bf16[16,160,128]{2,1,0:T(8,128)(2,1)S(1)} %shard_map.230), channel_id=1, source_target_pairs={{0,4},{4,8},{8,12},{12,0},{1,5},{5,9},{9,13},{13,1},{2,6},{6,10},{... | collective-permute-start | bytes 1966088 | tf_op jit(solution)/shard_map/ppermute | solution.py:649
  63.3 18.8 %collective-permute-start.1 = (bf16[16,160,128]{2,1,0:T(8,128)(2,1)}, bf16[16,160,128]{2,1,0:T(8,128)(2,1)}, u32[]{:S(2)}, u32[]{:S(2)}) collective-permute-start(bf16[16,160,128]{2,1,0:T(8,128)(2,1)} %collective-permute-done.refs_5_), channel_id=1, source_target_pairs={{0,4},{4,8},{8,12},{12,0},{1,5},{5,9},{9,13},{13,1},{2,6},{6,10},{... | collective-permute-start | bytes 1966088 | tf_op jit(solution)/shard_map/ppermute | solution.py:649
  82.1 4.4 collective-permute-start.6
  82.1 19.3 %collective-permute-start.4 = (bf16[16,160,128]{2,1,0:T(8,128)(2,1)}, bf16[16,160,128]{2,1,0:T(8,128)(2,1)S(1)}, u32[]{:S(2)}, u32[]{:S(2)}) collective-permute-start(bf16[16,160,128]{2,1,0:T(8,128)(2,1)} %collective-permute-done.1.refs_6_), channel_id=1, source_target_pairs={{0,4},{4,8},{8,12},{12,0},{1,5},{5,9},{9,13},{13,1},{2,6},{6,10},{... | collective-permute-start | bytes 1966088 | tf_op jit(solution)/shard_map/ppermute | solution.py:649
  124.0 4.2 collective-permute-start.8
  124.0 7.2 %collective-permute-start.7 = (bf16[512,2048]{1,0:T(8,128)(2,1)S(1)}, bf16[512,2048]{1,0:T(8,128)(2,1)S(1)}, u32[]{:S(2)}, u32[]{:S(2)}) collective-permute-start(bf16[512,2048]{1,0:T(8,128)(2,1)S(1)} %get-tuple-element.490.refs_2_.r0), channel_id=1, source_target_pairs={{0,16},{16,0},{1,17},{17,1},{2,18},{18,2},{3,19},{19,3},{4,20},{20... | collective-permute-start | bytes 6291464 | tf_op jit(solution)/shard_map/ppermute | solution.py:640
  124.5 51.6 %collective-permute-start.9 = (bf16[512,2048]{1,0:T(8,128)(2,1)S(1)}, bf16[512,2048]{1,0:T(8,128)(2,1)}, u32[]{:S(2)}, u32[]{:S(2)}) collective-permute-start(bf16[512,2048]{1,0:T(8,128)(2,1)S(1)} %multiply_convert_fusion.x0.l0), channel_id=1, source_target_pairs={{0,1},{1,0},{2,3},{3,2},{4,5},{5,4},{6,7},{7,6},{8,9},{9,8},{10,11... | collective-permute-start | bytes 6291464 | tf_op jit(solution)/shard_map/ppermute | solution.py:643
  176.2 4.5 collective-permute-start.10
  176.2 7.5 %collective-permute-start.11 = (bf16[512,2048]{1,0:T(8,128)(2,1)}, bf16[512,2048]{1,0:T(8,128)(2,1)}, u32[]{:S(2)}, u32[]{:S(2)}) collective-permute-start(bf16[512,2048]{1,0:T(8,128)(2,1)} %get-tuple-element.360), channel_id=1, source_target_pairs={{0,16},{16,0},{1,17},{17,1},{2,18},{18,2},{3,19},{19,3},{4,20},{20... | collective-permute-start | bytes 6291464 | tf_op jit(solution)/shard_map/ppermute | solution.py:640
  176.7 30.4 %copy-start.24 = (bf16[1024,1408]{1,0:T(8,128)(2,1)S(1)}, bf16[1024,1408]{1,0:T(8,128)(2,1)}, u32[]{:S(2)}) copy-start(bf16[1024,1408]{1,0:T(8,128)(2,1)} %copy-done.23) | copy-start | bytes 8650756
  225.5 64.6 %collective-permute-start.12 = (bf16[2,352,2048]{2,1,0:T(8,128)(2,1)S(1)}, bf16[2,352,2048]{2,1,0:T(8,128)(2,1)}, u32[]{:S(2)}, u32[]{:S(2)}) collective-permute-start(bf16[2,352,2048]{2,1,0:T(8,128)(2,1)S(1)} %get-tuple-element.389), channel_id=1, source_target_pairs={{0,2},{1,3},{2,0},{3,1},{4,6},{5,7},{6,4},{7,5},{8,10},{9,11},{10,... | collective-permute-start | bytes 8650760 | tf_op jit(solution)/shard_map/ppermute | solution.py:646
  248.3 18.9 %collective-permute-start.13 = (bf16[256,2048]{1,0:T(8,128)(2,1)S(1)}, bf16[256,2048]{1,0:T(8,128)(2,1)S(1)}, u32[]{:S(2)}, u32[]{:S(2)}) collective-permute-start(bf16[256,2048]{1,0:T(8,128)(2,1)S(1)} %get-tuple-element.391), channel_id=1, source_target_pairs={{0,16},{16,0},{1,17},{17,1},{2,18},{18,2},{3,19},{19,3},{4,20},{20... | collective-permute-start | bytes 3145736 | tf_op jit(solution)/shard_map/ppermute | solution.py:640
  248.4 18.8 %collective-permute-start.14 = (bf16[256,2048]{1,0:T(8,128)(2,1)S(1)}, bf16[256,2048]{1,0:T(8,128)(2,1)S(1)}, u32[]{:S(2)}, u32[]{:S(2)}) collective-permute-start(bf16[256,2048]{1,0:T(8,128)(2,1)S(1)} %get-tuple-element.392), channel_id=1, source_target_pairs={{0,16},{16,0},{1,17},{17,1},{2,18},{18,2},{3,19},{19,3},{4,20},{20... | collective-permute-start | bytes 3145736 | tf_op jit(solution)/shard_map/ppermute | solution.py:640
  271.0 47.9 %collective-permute-start.17 = (bf16[512,2048]{1,0:T(8,128)(2,1)}, bf16[512,2048]{1,0:T(8,128)(2,1)}, u32[]{:S(2)}, u32[]{:S(2)}) collective-permute-start(bf16[512,2048]{1,0:T(8,128)(2,1)} %add_convert_fusion.1), channel_id=1, source_target_pairs={{0,1},{1,0},{2,3},{3,2},{4,5},{5,4},{6,7},{7,6},{8,9},{9,8},{10,11... | collective-permute-start | bytes 6291464 | tf_op jit(solution)/shard_map/ppermute | solution.py:643
  303.8 34.6 %collective-permute-start.15 = (bf16[256,2048]{1,0:T(8,128)(2,1)}, bf16[256,2048]{1,0:T(8,128)(2,1)}, u32[]{:S(2)}, u32[]{:S(2)}) collective-permute-start(bf16[256,2048]{1,0:T(8,128)(2,1)} %get-tuple-element.408), channel_id=1, source_target_pairs={{0,16},{16,0},{1,17},{17,1},{2,18},{18,2},{3,19},{19,3},{4,20},{20... | collective-permute-start | bytes 3145736 | tf_op jit(solution)/shard_map/ppermute | solution.py:640
  303.9 34.5 %collective-permute-start.16 = (bf16[256,2048]{1,0:T(8,128)(2,1)}, bf16[256,2048]{1,0:T(8,128)(2,1)}, u32[]{:S(2)}, u32[]{:S(2)}) collective-permute-start(bf16[256,2048]{1,0:T(8,128)(2,1)} %get-tuple-element.409), channel_id=1, source_target_pairs={{0,16},{16,0},{1,17},{17,1},{2,18},{18,2},{3,19},{19,3},{4,20},{20... | collective-permute-start | bytes 3145736 | tf_op jit(solution)/shard_map/ppermute | solution.py:640
  306.7 47.3 %collective-permute-start.18 = (bf16[176,2048]{1,0:T(8,128)(2,1)}, bf16[176,2048]{1,0:T(8,128)(2,1)}, u32[]{:S(2)}, u32[]{:S(2)}) collective-permute-start(bf16[176,2048]{1,0:T(8,128)(2,1)} %fusion.14), channel_id=1, source_target_pairs={{0,4},{4,8},{8,12},{12,0},{1,5},{5,9},{9,13},{13,1},{2,6},{6,10},{... | collective-permute-start | bytes 2162696 | tf_op jit(solution)/shard_map/ppermute | solution.py:649
  306.7 118.1 %collective-permute-start.24 = (bf16[8,128,1408]{2,1,0:T(8,128)(2,1)}, bf16[8,128,1408]{2,1,0:T(8,128)(2,1)}, u32[]{:S(2)}, u32[]{:S(2)}) collective-permute-start(bf16[8,128,1408]{2,1,0:T(8,128)(2,1)} %copy-done.85), channel_id=1, source_target_pairs={{0,2},{1,3},{2,0},{3,1},{4,6},{5,7},{6,4},{7,5},{8,10},{9,11},{10,... | collective-permute-start | bytes 8650760 | tf_op jit(solution)/shard_map/ppermute | solution.py:646
  354.0 19.6 %collective-permute-start.22 = (bf16[16,160,128]{2,1,0:T(8,128)(2,1)}, bf16[16,160,128]{2,1,0:T(8,128)(2,1)}, u32[]{:S(2)}, u32[]{:S(2)}) collective-permute-start(bf16[16,160,128]{2,1,0:T(8,128)(2,1)} %get-tuple-element.449), channel_id=1, source_target_pairs={{12,8},{13,9},{14,10},{15,11},{28,24},{29,25},{30,26},{31,27}} | collective-permute-start | bytes 1966088 | tf_op jit(solution)/shard_map/ppermute | solution.py:667
  358.3 27.8 %collective-permute-start.21 = (bf16[176,2048]{1,0:T(8,128)(2,1)}, bf16[176,2048]{1,0:T(8,128)(2,1)}, u32[]{:S(2)}, u32[]{:S(2)}) collective-permute-start(bf16[176,2048]{1,0:T(8,128)(2,1)} %fusion.9), channel_id=1, source_target_pairs={{0,4},{4,8},{8,12},{12,0},{1,5},{5,9},{9,13},{13,1},{2,6},{6,10},{... | collective-permute-start | bytes 2162696 | tf_op jit(solution)/shard_map/ppermute | solution.py:649
  373.1 15.8 %collective-permute-start.19 = (bf16[256,2048]{1,0:T(8,128)(2,1)}, bf16[256,2048]{1,0:T(8,128)(2,1)}, u32[]{:S(2)}, u32[]{:S(2)}) collective-permute-start(bf16[256,2048]{1,0:T(8,128)(2,1)} %get-tuple-element.445), channel_id=1, source_target_pairs={{0,16},{16,0},{1,17},{17,1},{2,18},{18,2},{3,19},{19,3},{4,20},{20... | collective-permute-start | bytes 3145736 | tf_op jit(solution)/shard_map/ppermute | solution.py:640
  373.1 42.8 %collective-permute-start.20 = (bf16[256,2048]{1,0:T(8,128)(2,1)}, bf16[256,2048]{1,0:T(8,128)(2,1)}, u32[]{:S(2)}, u32[]{:S(2)}) collective-permute-start(bf16[256,2048]{1,0:T(8,128)(2,1)} %get-tuple-element.446), channel_id=1, source_target_pairs={{0,16},{16,0},{1,17},{17,1},{2,18},{18,2},{3,19},{19,3},{4,20},{20... | collective-permute-start | bytes 3145736 | tf_op jit(solution)/shard_map/ppermute | solution.py:640
  376.2 40.3 %collective-permute-start.26 = (bf16[16,160,128]{2,1,0:T(8,128)(2,1)}, bf16[16,160,128]{2,1,0:T(8,128)(2,1)}, u32[]{:S(2)}, u32[]{:S(2)}) collective-permute-start(bf16[16,160,128]{2,1,0:T(8,128)(2,1)} %fusion.10), channel_id=1, source_target_pairs={{8,4},{9,5},{10,6},{11,7},{24,20},{25,21},{26,22},{27,23}} | collective-permute-start | bytes 1966088 | tf_op jit(solution)/shard_map/ppermute | solution.py:667
  388.9 31.7 %collective-permute-start.25 = (bf16[176,2048]{1,0:T(8,128)(2,1)}, bf16[176,2048]{1,0:T(8,128)(2,1)}, u32[]{:S(2)}, u32[]{:S(2)}) collective-permute-start(bf16[176,2048]{1,0:T(8,128)(2,1)} %fusion.8), channel_id=1, source_target_pairs={{0,4},{4,8},{8,12},{12,0},{1,5},{5,9},{9,13},{13,1},{2,6},{6,10},{... | collective-permute-start | bytes 2162696 | tf_op jit(solution)/shard_map/ppermute | solution.py:649
  388.9 40.7 %collective-permute-start.29 = (bf16[256,2048]{1,0:T(8,128)(2,1)}, bf16[256,2048]{1,0:T(8,128)(2,1)}, u32[]{:S(2)}, u32[]{:S(2)}) collective-permute-start(bf16[256,2048]{1,0:T(8,128)(2,1)} %copy-done.88), channel_id=1, source_target_pairs={{0,16},{16,0},{1,17},{17,1},{2,18},{18,2},{3,19},{19,3},{4,20},{20... | collective-permute-start | bytes 3145736 | tf_op jit(solution)/shard_map/ppermute | solution.py:640
  415.9 18.0 %collective-permute-start.30 = (bf16[256,2048]{1,0:T(8,128)(2,1)S(1)}, bf16[256,2048]{1,0:T(8,128)(2,1)S(1)}, u32[]{:S(2)}, u32[]{:S(2)}) collective-permute-start(bf16[256,2048]{1,0:T(8,128)(2,1)S(1)} %copy-done.87), channel_id=1, source_target_pairs={{0,16},{16,0},{1,17},{17,1},{2,18},{18,2},{3,19},{19,3},{4,20},{20... | collective-permute-start | bytes 3145736 | tf_op jit(solution)/shard_map/ppermute | solution.py:640
  419.1 45.0 %collective-permute-start.28 = (bf16[16,160,128]{2,1,0:T(8,128)(2,1)}, bf16[16,160,128]{2,1,0:T(8,128)(2,1)S(1)}, u32[]{:S(2)}, u32[]{:S(2)}) collective-permute-start(bf16[16,160,128]{2,1,0:T(8,128)(2,1)} %fusion.11), channel_id=1, source_target_pairs={{4,0},{5,1},{6,2},{7,3},{20,16},{21,17},{22,18},{23,19}} | collective-permute-start | bytes 1966088 | tf_op jit(solution)/shard_map/ppermute | solution.py:667
  423.3 58.2 %collective-permute-start.32 = (bf16[176,2048]{1,0:T(8,128)(2,1)}, bf16[176,2048]{1,0:T(8,128)(2,1)}, u32[]{:S(2)}, u32[]{:S(2)}) collective-permute-start(bf16[176,2048]{1,0:T(8,128)(2,1)} %fusion.6), channel_id=1, source_target_pairs={{1,8},{3,10},{5,12},{7,14},{8,1},{10,3},{12,5},{14,7},{17,24},{19,... | collective-permute-start | bytes 2162696 | tf_op jit(solution)/shard_map/ppermute | solution.py:876
  427.0 54.5 %collective-permute-start.27 = (bf16[2,2,64,1408]{3,2,1,0:T(8,128)(2,1)}, bf16[2,2,64,1408]{3,2,1,0:T(8,128)(2,1)}, u32[]{:S(2)}, u32[]{:S(2)}) collective-permute-start(bf16[2,2,64,1408]{3,2,1,0:T(8,128)(2,1)} %fusion.15), channel_id=1, source_target_pairs={{0,4},{4,8},{8,12},{12,0},{1,5},{5,9},{9,13},{13,1},{2,6},{6,10},{... | collective-permute-start | bytes 2162696 | tf_op jit(solution)/shard_map/ppermute | solution.py:649
  429.7 66.9 %collective-permute-start.35 = (bf16[8,128,1408]{2,1,0:T(8,128)(2,1)}, bf16[8,128,1408]{2,1,0:T(8,128)(2,1)}, u32[]{:S(2)}, u32[]{:S(2)}) collective-permute-start(bf16[8,128,1408]{2,1,0:T(8,128)(2,1)} %get-tuple-element.520), channel_id=1, source_target_pairs={{0,2},{1,3},{2,0},{3,1},{4,6},{5,7},{6,4},{7,5},{8,10},{9,11},{10,... | collective-permute-start | bytes 8650760 | tf_op jit(solution)/shard_map/ppermute | solution.py:646
  433.9 79.6 %collective-permute-start.23 = (bf16[512,2048]{1,0:T(8,128)(2,1)}, bf16[512,2048]{1,0:T(8,128)(2,1)}, u32[]{:S(2)}, u32[]{:S(2)}) collective-permute-start(bf16[512,2048]{1,0:T(8,128)(2,1)} %add_convert_fusion), channel_id=1, source_target_pairs={{0,1},{1,0},{2,3},{3,2},{4,5},{5,4},{6,7},{7,6},{8,9},{9,8},{10,11... | collective-permute-start | bytes 6291464 | tf_op jit(solution)/shard_map/ppermute | solution.py:643
  483.8 13.0 %collective-permute-start.34 = (bf16[512,1280]{1,0:T(8,128)(2,1)S(1)}, bf16[512,1280]{1,0:T(8,128)(2,1)S(1)}, u32[]{:S(2)}, u32[]{:S(2)}) collective-permute-start(bf16[512,1280]{1,0:T(8,128)(2,1)S(1)} %slice.28.c0), channel_id=1, source_target_pairs={{0,16},{16,0},{1,17},{17,1},{2,18},{18,2},{3,19},{19,3},{4,20},{20... | collective-permute-start | bytes 3932168 | tf_op jit(solution)/shard_map/ppermute | solution.py:640
  483.8 22.7 %collective-permute-start.33 = (bf16[512,1280]{1,0:T(8,128)(2,1)S(1)}, bf16[512,1280]{1,0:T(8,128)(2,1)S(1)}, u32[]{:S(2)}, u32[]{:S(2)}) collective-permute-start(bf16[512,1280]{1,0:T(8,128)(2,1)S(1)} %pad_maximum_fusion.c0), channel_id=1, source_target_pairs={{0,16},{16,0},{1,17},{17,1},{2,18},{18,2},{3,19},{19,3},{4,20},{20... | collective-permute-start | bytes 3932168 | tf_op jit(solution)/shard_map/ppermute | solution.py:640
  486.8 26.8 %collective-permute-start.31 = (bf16[2,2,64,1408]{3,2,1,0:T(8,128)(2,1)}, bf16[2,2,64,1408]{3,2,1,0:T(8,128)(2,1)}, u32[]{:S(2)}, u32[]{:S(2)}) collective-permute-start(bf16[2,2,64,1408]{3,2,1,0:T(8,128)(2,1)} %fusion.7), channel_id=1, source_target_pairs={{0,4},{4,8},{8,12},{12,0},{1,5},{5,9},{9,13},{13,1},{2,6},{6,10},{... | collective-permute-start | bytes 2162696 | tf_op jit(solution)/shard_map/ppermute | solution.py:649
  496.5 43.4 %collective-permute-start.38 = (bf16[4,2,64,1024]{3,2,1,0:T(8,128)(2,1)S(1)}, bf16[4,2,64,1024]{3,2,1,0:T(8,128)(2,1)}, u32[]{:S(2)}, u32[]{:S(2)}) collective-permute-start(bf16[4,2,64,1024]{3,2,1,0:T(8,128)(2,1)S(1)} %get-tuple-element.546), channel_id=1, source_target_pairs={{0,1},{1,0},{2,3},{3,2},{4,5},{5,4},{6,7},{7,6},{8,9},{9,8},{10,11... | collective-permute-start | bytes 3145736 | tf_op jit(solution)/shard_map/ppermute | solution.py:643
  496.8 48.3 %collective-permute-start.37 = (bf16[4,2,64,1024]{3,2,1,0:T(8,128)(2,1)S(1)}, bf16[4,2,64,1024]{3,2,1,0:T(8,128)(2,1)S(1)}, u32[]{:S(2)}, u32[]{:S(2)}) collective-permute-start(bf16[4,2,64,1024]{3,2,1,0:T(8,128)(2,1)S(1)} %get-tuple-element.545), channel_id=1, source_target_pairs={{0,1},{1,0},{2,3},{3,2},{4,5},{5,4},{6,7},{7,6},{8,9},{9,8},{10,11... | collective-permute-start | bytes 3145736 | tf_op jit(solution)/shard_map/ppermute | solution.py:643
  506.5 22.3 %collective-permute-start.36 = (bf16[2,2,64,1408]{3,2,1,0:T(8,128)(2,1)S(1)}, bf16[2,2,64,1408]{3,2,1,0:T(8,128)(2,1)}, u32[]{:S(2)}, u32[]{:S(2)}) collective-permute-start(bf16[2,2,64,1408]{3,2,1,0:T(8,128)(2,1)S(1)} %fusion.16), channel_id=1, source_target_pairs={{0,4},{4,8},{8,12},{12,0},{1,5},{5,9},{9,13},{13,1},{2,6},{6,10},{... | collective-permute-start | bytes 2162696 | tf_op jit(solution)/shard_map/ppermute | solution.py:649
  520.6 35.5 %collective-permute-start.41 = (bf16[4,2,64,1280]{3,2,1,0:T(8,128)(2,1)}, bf16[4,2,64,1280]{3,2,1,0:T(8,128)(2,1)}, u32[]{:S(2)}, u32[]{:S(2)}) collective-permute-start(bf16[4,2,64,1280]{3,2,1,0:T(8,128)(2,1)} %get-tuple-element.555), channel_id=1, source_target_pairs={{0,2},{1,3},{2,0},{3,1},{4,6},{5,7},{6,4},{7,5},{8,10},{9,11},{10,... | collective-permute-start | bytes 3932168 | tf_op jit(solution)/shard_map/ppermute | solution.py:646
  522.6 49.4 %collective-permute-start.40 = (bf16[4,2,64,1280]{3,2,1,0:T(8,128)(2,1)}, bf16[4,2,64,1280]{3,2,1,0:T(8,128)(2,1)}, u32[]{:S(2)}, u32[]{:S(2)}) collective-permute-start(bf16[4,2,64,1280]{3,2,1,0:T(8,128)(2,1)} %get-tuple-element.554), channel_id=1, source_target_pairs={{0,1},{1,0},{2,3},{3,2},{4,5},{5,4},{6,7},{7,6},{8,9},{9,8},{10,11... | collective-permute-start | bytes 3932168 | tf_op jit(solution)/shard_map/ppermute | solution.py:643
  528.8 56.1 %collective-permute-start.45 = (bf16[2,2,64,1408]{3,2,1,0:T(8,128)(2,1)}, bf16[2,2,64,1408]{3,2,1,0:T(8,128)(2,1)}, u32[]{:S(2)}, u32[]{:S(2)}) collective-permute-start(bf16[2,2,64,1408]{3,2,1,0:T(8,128)(2,1)} %fusion.2), channel_id=1, source_target_pairs={{0,4},{4,8},{8,12},{12,0},{1,5},{5,9},{9,13},{13,1},{2,6},{6,10},{... | collective-permute-start | bytes 2162696 | tf_op jit(solution)/shard_map/ppermute | solution.py:649
  548.6 27.9 %collective-permute-start.39 = (bf16[2,2,64,1408]{3,2,1,0:T(8,128)(2,1)}, bf16[2,2,64,1408]{3,2,1,0:T(8,128)(2,1)}, u32[]{:S(2)}, u32[]{:S(2)}) collective-permute-start(bf16[2,2,64,1408]{3,2,1,0:T(8,128)(2,1)} %fusion.3), channel_id=1, source_target_pairs={{0,4},{4,8},{8,12},{12,0},{1,5},{5,9},{9,13},{13,1},{2,6},{6,10},{... | collective-permute-start | bytes 2162696 | tf_op jit(solution)/shard_map/ppermute | solution.py:649
  551.0 28.8 %collective-permute-start.47 = (bf16[4,64,1024]{2,1,0:T(8,128)(2,1)}, bf16[4,64,1024]{2,1,0:T(8,128)(2,1)}, u32[]{:S(2)}, u32[]{:S(2)}) collective-permute-start(bf16[4,64,1024]{2,1,0:T(8,128)(2,1)} %fusion.22), channel_id=1, source_target_pairs={{0,2},{1,3},{2,0},{3,1},{4,6},{5,7},{6,4},{7,5},{8,10},{9,11},{10,... | collective-permute-start | bytes 1572872 | tf_op jit(solution)/shard_map/ppermute | solution.py:646
  554.7 55.0 %copy-start.103 = (bf16[4,1,64,1024]{3,2,1,0:T(8,128)(2,1)}, bf16[4,1,64,1024]{3,2,1,0:T(8,128)(2,1)S(1)}, u32[]{:S(2)}) copy-start(bf16[4,1,64,1024]{3,2,1,0:T(8,128)(2,1)S(1)} %constant_dynamic-slice_fusion) | copy-start | bytes 1572868
  556.1 28.4 %collective-permute-start.46 = (bf16[2,2,64,1024]{3,2,1,0:T(8,128)(2,1)S(1)}, bf16[2,2,64,1024]{3,2,1,0:T(8,128)(2,1)S(1)}, u32[]{:S(2)}, u32[]{:S(2)}) collective-permute-start(bf16[2,2,64,1024]{3,2,1,0:T(8,128)(2,1)S(1)} %fusion.21), channel_id=1, source_target_pairs={{0,4},{4,0},{8,12},{12,8},{1,5},{5,1},{9,13},{13,9},{2,6},{6,2},{1... | collective-permute-start | bytes 1572872 | tf_op jit(solution)/shard_map/ppermute | solution.py:655
  573.2 15.5 %collective-permute-start.44 = (bf16[4,64,1280]{2,1,0:T(8,128)(2,1)S(1)}, bf16[4,64,1280]{2,1,0:T(8,128)(2,1)S(1)}, u32[]{:S(2)}, u32[]{:S(2)}) collective-permute-start(bf16[4,64,1280]{2,1,0:T(8,128)(2,1)S(1)} %fusion.20), channel_id=1, source_target_pairs={{0,1},{1,0},{2,3},{3,2},{4,5},{5,4},{6,7},{7,6},{8,9},{9,8},{10,11... | collective-permute-start | bytes 1966088 | tf_op jit(solution)/shard_map/ppermute | solution.py:643
  576.5 15.4 %collective-permute-start.43 = (bf16[4,64,1280]{2,1,0:T(8,128)(2,1)S(1)}, bf16[4,64,1280]{2,1,0:T(8,128)(2,1)S(1)}, u32[]{:S(2)}, u32[]{:S(2)}) collective-permute-start(bf16[4,64,1280]{2,1,0:T(8,128)(2,1)S(1)} %fusion.19), channel_id=1, source_target_pairs={{0,2},{1,3},{2,0},{3,1},{4,6},{5,7},{6,4},{7,5},{8,10},{9,11},{10,... | collective-permute-start | bytes 1966088 | tf_op jit(solution)/shard_map/ppermute | solution.py:646
  579.8 21.1 %collective-permute-start.42 = (bf16[2,2,64,1408]{3,2,1,0:T(8,128)(2,1)S(1)}, bf16[2,2,64,1408]{3,2,1,0:T(8,128)(2,1)S(1)}, u32[]{:S(2)}, u32[]{:S(2)}) collective-permute-start(bf16[2,2,64,1408]{3,2,1,0:T(8,128)(2,1)S(1)} %fusion.4), channel_id=1, source_target_pairs={{0,4},{4,8},{8,12},{12,0},{1,5},{5,9},{9,13},{13,1},{2,6},{6,10},{... | collective-permute-start | bytes 2162696 | tf_op jit(solution)/shard_map/ppermute | solution.py:649
  584.5 25.1 %collective-permute-start.53 = (bf16[2,64,1024]{2,1,0:T(8,128)(2,1)S(1)}, bf16[2,64,1024]{2,1,0:T(8,128)(2,1)S(1)}, u32[]{:S(2)}, u32[]{:S(2)}) collective-permute-start(bf16[2,64,1024]{2,1,0:T(8,128)(2,1)S(1)} %fusion.30), channel_id=1, source_target_pairs={{0,4},{4,0},{8,12},{12,8},{1,5},{5,1},{9,13},{13,9},{2,6},{6,2},{1... | collective-permute-start | bytes 786440 | tf_op jit(solution)/shard_map/ppermute | solution.py:655
  586.0 24.8 %collective-permute-start.52 = (bf16[2,64,1024]{2,1,0:T(8,128)(2,1)S(1)}, bf16[2,64,1024]{2,1,0:T(8,128)(2,1)}, u32[]{:S(2)}, u32[]{:S(2)}) collective-permute-start(bf16[2,64,1024]{2,1,0:T(8,128)(2,1)S(1)} %fusion.23), channel_id=1, source_target_pairs={{0,8},{4,12},{8,0},{12,4},{1,9},{5,13},{9,1},{13,5},{2,10},{6,14},... | collective-permute-start | bytes 786440 | tf_op jit(solution)/shard_map/ppermute | solution.py:655
  592.9 30.6 %collective-permute-start.50 = (bf16[2,64,1280]{2,1,0:T(8,128)(2,1)}, bf16[2,64,1280]{2,1,0:T(8,128)(2,1)}, u32[]{:S(2)}, u32[]{:S(2)}) collective-permute-start(bf16[2,64,1280]{2,1,0:T(8,128)(2,1)} %fusion.25), channel_id=1, source_target_pairs={{0,4},{4,0},{8,12},{12,8},{1,5},{5,1},{9,13},{13,9},{2,6},{6,2},{1... | collective-permute-start | bytes 983048 | tf_op jit(solution)/shard_map/ppermute | solution.py:655
  604.1 17.7 %collective-permute-start.51 = (bf16[2,64,1408]{2,1,0:T(8,128)(2,1)}, bf16[2,64,1408]{2,1,0:T(8,128)(2,1)S(1)}, u32[]{:S(2)}, u32[]{:S(2)}) collective-permute-start(bf16[2,64,1408]{2,1,0:T(8,128)(2,1)} %get-tuple-element.630), channel_id=1, source_target_pairs={{0,1},{1,0},{2,3},{3,2},{4,5},{5,4},{6,7},{7,6},{8,9},{9,8},{10,11... | collective-permute-start | bytes 1081352 | tf_op jit(solution)/shard_map/ppermute | solution.py:643
  606.6 19.9 %collective-permute-start.48 = (bf16[2,64,1408]{2,1,0:T(8,128)(2,1)}, bf16[2,64,1408]{2,1,0:T(8,128)(2,1)S(1)}, u32[]{:S(2)}, u32[]{:S(2)}) collective-permute-start(bf16[2,64,1408]{2,1,0:T(8,128)(2,1)} %get-tuple-element.632), channel_id=1, source_target_pairs={{0,1},{1,0},{2,3},{3,2},{4,5},{5,4},{6,7},{7,6},{8,9},{9,8},{10,11... | collective-permute-start | bytes 1081352 | tf_op jit(solution)/shard_map/ppermute | solution.py:643
  609.6 16.9 %collective-permute-start.49 = (bf16[2,64,1280]{2,1,0:T(8,128)(2,1)}, bf16[2,64,1280]{2,1,0:T(8,128)(2,1)S(1)}, u32[]{:S(2)}, u32[]{:S(2)}) collective-permute-start(bf16[2,64,1280]{2,1,0:T(8,128)(2,1)} %fusion.24), channel_id=1, source_target_pairs={{0,4},{4,0},{8,12},{12,8},{1,5},{5,1},{9,13},{13,9},{2,6},{6,2},{1... | collective-permute-start | bytes 983048 | tf_op jit(solution)/shard_map/ppermute | solution.py:655
  610.7 15.8 %collective-permute-start.59 = (bf16[64,1024]{1,0:T(8,128)(2,1)S(1)}, bf16[64,1024]{1,0:T(8,128)(2,1)S(1)}, u32[]{:S(2)}, u32[]{:S(2)}) collective-permute-start(bf16[64,1024]{1,0:T(8,128)(2,1)S(1)} %fusion.31), channel_id=1, source_target_pairs={{0,8},{4,12},{8,0},{12,4},{1,9},{5,13},{9,1},{13,5},{2,10},{6,14},... | collective-permute-start | bytes 393224 | tf_op jit(solution)/shard_map/ppermute | solution.py:655
  617.5 35.4 %all-to-all-start = ((f32[32,1,128]{2,1,0:T(1,128)}), f32[32,1,128]{2,1,0:T(1,128)}, u32[]{:S(2)}, u32[]{:S(2)}) async-start(f32[32,1,128]{2,1,0:T(1,128)} %bitcast.24), calls=%async_computation | async-start | bytes 32768 | tf_op jit(solution)/shard_map/all_to_all | solution.py:1045
  621.8 6.9 %collective-permute-start.58 = (bf16[64,1024]{1,0:T(8,128)(2,1)S(1)}, bf16[64,1024]{1,0:T(8,128)(2,1)S(1)}, u32[]{:S(2)}, u32[]{:S(2)}) collective-permute-start(bf16[64,1024]{1,0:T(8,128)(2,1)S(1)} %fusion.33), channel_id=1, source_target_pairs={{0,2},{1,3},{2,0},{3,1},{4,6},{5,7},{6,4},{7,5},{8,10},{9,11},{10,... | collective-permute-start | bytes 393224 | tf_op jit(solution)/shard_map/ppermute | solution.py:646
  631.6 5.5 collective-permute-start.57
  632.8 14.7 %collective-permute-start.56 = (bf16[64,1280]{1,0:T(8,128)(2,1)S(1)}, bf16[64,1280]{1,0:T(8,128)(2,1)S(1)}, u32[]{:S(2)}, u32[]{:S(2)}) collective-permute-start(bf16[64,1280]{1,0:T(8,128)(2,1)S(1)} %fusion.26), channel_id=1, source_target_pairs={{0,8},{4,12},{8,0},{12,4},{1,9},{5,13},{9,1},{13,5},{2,10},{6,14},... | collective-permute-start | bytes 491528 | tf_op jit(solution)/shard_map/ppermute | solution.py:655
  634.2 16.7 %collective-permute-start.55 = (bf16[64,1280]{1,0:T(8,128)(2,1)S(1)}, bf16[64,1280]{1,0:T(8,128)(2,1)S(1)}, u32[]{:S(2)}, u32[]{:S(2)}) collective-permute-start(bf16[64,1280]{1,0:T(8,128)(2,1)S(1)} %fusion.28), channel_id=1, source_target_pairs={{0,8},{4,12},{8,0},{12,4},{1,9},{5,13},{9,1},{13,5},{2,10},{6,14},... | collective-permute-start | bytes 491528 | tf_op jit(solution)/shard_map/ppermute | solution.py:655
  636.2 14.8 %collective-permute-start.54 = (bf16[64,2816]{1,0:T(8,128)(2,1)S(1)}, bf16[64,2816]{1,0:T(8,128)(2,1)S(1)}, u32[]{:S(2)}, u32[]{:S(2)}) collective-permute-start(bf16[64,2816]{1,0:T(8,128)(2,1)S(1)} %get-tuple-element.626), channel_id=1, source_target_pairs={{0,16},{16,0},{1,17},{17,1},{2,18},{18,2},{3,19},{19,3},{4,20},{20... | collective-permute-start | bytes 1081352 | tf_op jit(solution)/shard_map/ppermute | solution.py:640
  (122 other events, 1061.6 us)
